TPU v7x, 128 devices: a whole 4x4x4 slice. The times are simulated.
128 devices in a mesh: role: 2 (over core), dev: 64 (over x, y, z).
Axes of the slice: x: 4, y: 4, z: 4, core: 2. Of those that a mesh axis runs over, the one named last changes fastest.
Arguments:
- initial_realizations: bfloat16 [64, 69, 128, 384], P('dev', None, 'role'), may hold values from -6 to 15, as said below
- diffusivity: float32 [69], replicated, may hold values from 0.05 to 0.24
- w_in: bfloat16 [512, 69], replicated, may hold values from -0.75 to 0.75
- b_in: float32 [512], replicated, may hold values from -4 to 4
- w_out: bfloat16 [69, 512], replicated, may hold values from -0.25 to 0.25
- obs_index: int32 [768, 128], P('role'), may hold values from 0 to 4415
- obs_value: float32 [768, 128], P(('role', 'dev')), may hold values from -8 to 8
- obs_weight: float32 [768, 128], P(('role', 'dev')), may hold values from 0.1 to 1
- climate: float32 [1], replicated, may hold values from -3 to 3
Outputs:
- analysis: bfloat16 [64, 69, 128, 384], P('dev', None, 'role')
Inputs may be any that keep to these rules, and one draw needn't show every extreme that they name: `initial_realizations`: field 0 carries a latitude-dependent offset. `obs_index`: entry f * 64 + a * 8 + b of a patch is field f at the cell a rows and b columns from the patch's first corner.
All inputs are finite; a program needn't handle non-finite values.
Results may differ from a plain program's by a relative error of at most 0.0071.
Values may be sent and summed in bfloat16 or wider, within the bound.
No kernel may reach another device: no remote copies, remote signals or barrier semaphores. Data moves between devices by JAX's collectives and lax.ppermute only.
A program may use at most 192 MiB of HBM per device.

v0:
```python
import jax
import jax.numpy as jnp
from jax import lax
from jax.sharding import PartitionSpec as P

TILE_EDGE_POINTS = 8
STEPS = 2
NS_ITERS = 12
CELLS = 64


HIGH = lax.Precision.HIGHEST


def extended(array, sides, width):
    for axis, dim in sides:
        peers, length = (lax.axis_size(axis), array.shape[dim])
        up = [(i, (i + 1) % peers) for i in range(peers - 1)]
        down = [(j, i) for i, j in up]
        last = lax.slice_in_dim(array, length - width, length, axis=dim)
        initial = lax.slice_in_dim(array, 0, width, axis=dim)
        before = lax.ppermute(last, axis, up)
        after = lax.ppermute(initial, axis, down)
        array = jnp.concatenate([before, array, after], axis=dim)
    return array


def advance(current, diffusivity, w_in, b_in, w_out):
    padded = extended(current, (("role", 2),), 1)
    centre = current.astype(jnp.float32)
    laplace = padded[:, :, 2:].astype(jnp.float32) + padded[:, :, :-2].astype(jnp.float32)
    laplace = laplace + jnp.roll(centre, 1, 3) + jnp.roll(centre, -1, 3) - 4.0 * centre
    smooth = (centre + diffusivity[None, :, None, None] * laplace).astype(jnp.bfloat16)
    members_here, fields, lat_rows, lon_cells = current.shape
    blocks = lat_rows // TILE_EDGE_POINTS
    stacked = jnp.moveaxis(
        smooth.reshape(members_here, fields, blocks, TILE_EDGE_POINTS * lon_cells), 2, 0
    )

    def process_block(block):
        linear = (
            jnp.einsum("hf,mfc->mhc", w_in, block, preferred_element_type=jnp.float32)
            + b_in[None, :, None]
        )
        hidden = jax.nn.gelu(linear).astype(jnp.bfloat16)
        return jnp.einsum("fh,mhc->mfc", w_out, hidden, preferred_element_type=jnp.float32)

    change = lax.map(process_block, stacked)
    change = jnp.moveaxis(change, 0, 2).reshape(members_here, fields, lat_rows, lon_cells)
    return (centre + change).astype(jnp.bfloat16)


def to_patches(grid):
    members_here, fields, lat_rows, lon_cells = grid.shape
    shaped = grid.reshape(
        members_here,
        fields,
        lat_rows // TILE_EDGE_POINTS,
        TILE_EDGE_POINTS,
        lon_cells // TILE_EDGE_POINTS,
        TILE_EDGE_POINTS,
    )
    return shaped.transpose(0, 2, 4, 1, 3, 5).reshape(
        members_here, lat_rows // TILE_EDGE_POINTS * (lon_cells // TILE_EDGE_POINTS), fields * CELLS
    )


def from_patches(tile_partition, fields, lat_rows, lon_cells):
    members_here = tile_partition.shape[0]
    shaped = tile_partition.reshape(
        members_here,
        lat_rows // TILE_EDGE_POINTS,
        lon_cells // TILE_EDGE_POINTS,
        fields,
        TILE_EDGE_POINTS,
        TILE_EDGE_POINTS,
    )
    return shaped.transpose(0, 3, 1, 4, 2, 5).reshape(members_here, fields, lat_rows, lon_cells)


def pick(tiles, index):
    members_here, patch_total, entries = tiles.shape
    fields = entries // CELLS
    shaped = tiles.reshape(members_here, patch_total, fields, CELLS)
    cell_of = index % CELLS
    field_of = index // CELLS
    cell_hot = (jnp.arange(CELLS, dtype=jnp.int32)[None, None, :] == cell_of[:, :, None]).astype(
        jnp.bfloat16
    )
    picked = jnp.einsum("mpfc,poc->mpfo", shaped, cell_hot, preferred_element_type=jnp.float32)
    field_hot = jnp.arange(fields, dtype=jnp.int32)[None, :, None] == field_of[:, None, :]
    return jnp.sum(jnp.where(field_hot[None], picked, 0.0), axis=2)


def batched(left, right):
    return jnp.einsum("pij,pjk->pik", left, right, precision=HIGH)


def build_weights(observed, obs_value, obs_weight):
    members = observed.shape[0]
    obs_mean = jnp.mean(observed, axis=0)
    obs_spread = observed - obs_mean[None]
    innovation = obs_value - obs_mean
    weighted = obs_spread * obs_weight[None]
    identity = jnp.broadcast_to(
        jnp.eye(members, dtype=jnp.float32)[None], (observed.shape[1], members, members)
    )
    precision_matrix = (members - 1.0) * identity + jnp.einsum(
        "mpo,npo->pmn", weighted, obs_spread, precision=HIGH
    )
    scale = members * jnp.trace(precision_matrix, axis1=1, axis2=2)

    def newton(counter, carry):
        iterate, root = carry
        factor = 0.5 * (3.0 * identity - batched(root, iterate))
        return (batched(iterate, factor), batched(factor, root))

    iterate, root = lax.fori_loop(
        0, NS_ITERS, newton, (precision_matrix / scale[:, None, None], identity)
    )
    transform = jnp.sqrt((members - 1.0) / scale)[:, None, None] * root
    pulled = jnp.einsum("mpo,po->pm", weighted, innovation, precision=HIGH)
    inner = jnp.einsum("pij,pj->pi", root, pulled, precision=HIGH)
    shift = jnp.einsum("pij,pj->pi", root, inner, precision=HIGH) / scale[:, None]
    return transform + shift[:, :, None]


def global_total(partial_value):
    return lax.psum(partial_value, ("role", "dev"))


def body(
    initial_realizations, diffusivity, w_in, b_in, w_out, obs_index, obs_value, obs_weight, climate
):
    current = initial_realizations
    for section in range(STEPS):
        current = advance(current, diffusivity, w_in, b_in, w_out)
    members_here, fields, lat_rows, lon_cells = current.shape
    tile_partition = to_patches(current)
    patch_count = tile_partition.shape[1] // lax.axis_size("dev")
    gathered = lax.all_to_all(tile_partition, "dev", split_axis=1, concat_axis=0, tiled=True)
    members = gathered.shape[0]
    values = gathered.astype(jnp.float32)
    mean = jnp.mean(values, axis=0)
    spread = values - mean[None]
    local_index = lax.dynamic_slice_in_dim(
        obs_index, lax.axis_index("dev") * patch_count, patch_count, 0
    )
    observed = pick(gathered, local_index)
    combined = build_weights(observed, obs_value, obs_weight)
    updated = mean[None] + jnp.einsum("pmn,mpk->npk", combined, spread, precision=HIGH)
    total = global_total(jnp.sum(updated[:, :, :CELLS]))
    tmean = total / (members * lax.axis_size("role") * lat_rows * lon_cells)
    nudged = jnp.concatenate(
        [updated[:, :, :CELLS] + (climate[0] - tmean), updated[:, :, CELLS:]], axis=2
    ).astype(jnp.bfloat16)
    returned = lax.all_to_all(nudged, "dev", split_axis=0, concat_axis=1, tiled=True)
    return from_patches(returned, fields, lat_rows, lon_cells)


def solution(mesh):
    in_specs = (
        P("dev", None, "role", None),
        P(),
        P(),
        P(),
        P(),
        P("role", None),
        P(("role", "dev"), None),
        P(("role", "dev"), None),
        P(),
    )
    out_specs = P("dev", None, "role", None)
    return jax.shard_map(body, mesh=mesh, in_specs=in_specs, out_specs=out_specs, check_vma=False)
```

profile of v0, /device:TPU:0, one launch (start us, length us, event | category | flops | bytes accessed | tf_op | source)
XLA Modules:
  0.0 701.0 jit_solution(16179795581247316664)
XLA Ops:
  7.2 9.5 %fusion.89 = (f32[1,69,64,383]{3,2,1,0:T(8,128)}, f32[1,69,64,383]{3,2,1,0:T(8,128)}) fusion(bf16[1,69,64,384]{3,2,1,0:T(8,128)(2,1)} %param.15), kind=kLoop, calls=%fused_computation.125 | loop fusion | bytes 27061248 | tf_op jit(solution)/shard_map/jit(_roll_static)/slice | solution.py:32
  19.3 11.5 %fusion.53 = bf16[1,69,64,384]{3,2,1,0:T(8,128)(2,1)} fusion(f32[1,69,64,383]{3,2,1,0:T(8,128)} %get-tuple-element.186, f32[1,69,64,1]{3,2,1,0:T(8,128)} %get-tuple-element.188, f32[1,69,64,1]{3,2,1,0:T(8,128)} %get-tuple-element.187, f32[1,69,64,383]{3,2,1,0:T(8,128)} %get-tuple-element.185, bf16[1,69,64,384]{3,2,1,0:T(8,128)(2,1)S(1)} %copy-done, ...), kind=kLoop, calls=%fused_computation.59 | loop fusion | flops 32219136 | bytes 20455188 | tf_op jit(solution)/shard_map/convert_element_type | solution.py:33
  30.9 5.0 reshape.95
  43.4 38.6 %while.33 = (s32[]{:T(128)}, f32[8,1,69,3072]{3,2,1,0:T(8,128)}, bf16[8,1,69,3072]{3,2,1,0:T(8,128)(2,1)}, bf16[512,69]{0,1:T(8,128)(2,1)S(1)}, f32[512]{0:T(512)S(1)}, /*index=5*/bf16[69,512]{1,0:T(8,128)(2,1)S(1)}, s32[]{:T(128)}) while((s32[]{:T(128)}, f32[8,1,69,3072]{3,2,1,0:T(8,128)}, bf16[8,1,69,3072]{3,2,1,0:T(8,128)(2,1)}, ...), condition=%wide.region_1.2_spmd, body=%wide.region_0.1_spmd.sunk | while | flops 449839104 | bytes 1471573 | solution.py:48
  43.4 4.8 fusion.123
  48.2 4.8 fusion.123
  57.8 4.8 fusion.123
  62.6 4.8 fusion.123
  72.3 4.9 fusion.123
  81.9 9.8 %copy.37 = f32[1,69,8,3072]{3,2,1,0:T(8,128)} copy(f32[1,69,8,3072]{3,1,0,2:T(8,128)} %bitcast.171) | data formatting | bytes 13565952 | tf_op jit(solution)/shard_map/transpose | solution.py:49
  91.7 8.3 %reshape.96 = f32[1,69,64,384]{3,2,1,0:T(8,128)} reshape(f32[1,69,8,3072]{3,2,1,0:T(8,128)} %copy.37) | data formatting | bytes 13565952 | tf_op jit(solution)/shard_map/reshape | solution.py:49
  100.0 5.1 add_convert_fusion.1
  105.3 5.1 fusion.86
  115.9 7.9 %fusion.58 = bf16[1,69,64,384]{3,2,1,0:T(8,128)(2,1)} fusion(f32[1,69,64,383]{3,2,1,0:T(8,128)S(1)} %copy-done.1, f32[1,69,64,1]{3,2,1,0:T(8,128)S(1)} %get-tuple-element.182, f32[1,69,64,1]{3,2,1,0:T(8,128)S(1)} %get-tuple-element.181, f32[1,69,64,383]{3,2,1,0:T(8,128)S(1)} %get-tuple-element.179, bf16[1,69,64,384]{3,2,1,0:T(8,128)(2,1)S(1)} %add_convert_fusion.1, ...), kind=kLoop, calls=%fused_computation.65 | loop fusion | flops 32219136 | bytes 20455188 | tf_op jit(solution)/shard_map/convert_element_type | solution.py:33
  123.9 6.3 reshape.97
  130.2 5.7 copy.38
  139.7 38.5 %while.34 = (s32[]{:T(128)}, f32[8,1,69,3072]{3,2,1,0:T(8,128)}, bf16[8,1,69,3072]{3,2,1,0:T(8,128)(2,1)}, bf16[512,69]{0,1:T(8,128)(2,1)S(1)}, f32[512]{0:T(512)S(1)}, /*index=5*/bf16[69,512]{1,0:T(8,128)(2,1)S(1)}, s32[]{:T(128)}) while((s32[]{:T(128)}, f32[8,1,69,3072]{3,2,1,0:T(8,128)}, bf16[8,1,69,3072]{3,2,1,0:T(8,128)(2,1)}, ...), condition=%wide.region_3.4_spmd, body=%wide.region_2.3_spmd.sunk | while | flops 449839104 | bytes 1471573 | solution.py:48
  144.5 4.8 fusion.127
  149.4 4.8 fusion.127
  154.2 4.8 fusion.127
  159.0 4.8 fusion.127
  168.6 4.9 fusion.127
  178.2 9.8 %copy.39 = f32[1,69,8,3072]{3,2,1,0:T(8,128)} copy(f32[1,69,8,3072]{3,1,0,2:T(8,128)} %bitcast.172) | data formatting | bytes 13565952 | tf_op jit(solution)/shard_map/transpose | solution.py:49
  188.1 8.0 %reshape.98 = f32[1,69,64,384]{3,2,1,0:T(8,128)} reshape(f32[1,69,8,3072]{3,2,1,0:T(8,128)} %copy.39) | data formatting | bytes 13565952 | tf_op jit(solution)/shard_map/reshape | solution.py:49
  196.1 5.8 add_convert_fusion
  201.9 7.9 %copy.40 = bf16[1,69,64,384]{1,3,2,0:T(8,128)(2,1)} copy(bf16[1,69,64,384]{3,2,1,0:T(8,128)(2,1)} %add_convert_fusion) | data formatting | bytes 6782976 | tf_op jit(solution)/shard_map/convert_element_type | solution.py:50
  209.9 18.2 %copy.41 = bf16[1,8,48,69,8,8]{2,1,5,4,3,0:T(8,128)(2,1)} copy(bf16[1,8,48,69,8,8]{3,5,2,4,1,0:T(8,128)(2,1)} %bitcast.174) | data formatting | bytes 6782976 | tf_op jit(solution)/shard_map/transpose | solution.py:63
  228.1 11.0 %reshape.100 = bf16[1,384,4416]{1,2,0:T(8,128)(2,1)S(1)} reshape(bf16[1,8,48,69,8,8]{2,1,5,4,3,0:T(8,128)(2,1)} %copy.41) | data formatting | bytes 6782976 | tf_op jit(solution)/shard_map/reshape | solution.py:63
  239.1 11.9 %copy.42 = bf16[1,384,4416]{2,0,1:T(2,128)(2,1)} copy(bf16[1,384,4416]{1,2,0:T(8,128)(2,1)S(1)} %reshape.100) | data formatting | bytes 6782976 | tf_op jit(solution)/shard_map/reshape | solution.py:63
  251.5 21.6 %reduce.5 = bf16[384,4416]{1,0:T(8,128)(2,1)S(1)} reduce(bf16[384,1,4416]{2,1,0:T(2,128)(2,1)} %bitcast.173, bf16[]{:T(256)} %broadcast.151), dimensions={1}, to_apply=%bitcast.107.reduce_sub_computation | reduce | bytes 6782978
  273.1 5.8 reshape.114
  278.9 11.7 %all-to-all-start = ((bf16[64,2,13248]{2,1,0:T(2,128)(2,1)}), bf16[64,2,13248]{2,1,0:T(2,128)(2,1)S(1)}, u32[]{:S(2)}, u32[]{:S(2)}) async-start(bf16[64,2,13248]{2,1,0:T(2,128)(2,1)} %reshape.114), calls=%async_computation | async-start | bytes 6815744 | tf_op jit(solution)/shard_map/all_to_all | solution.py:141
  293.4 42.4 %all-to-all-done = bf16[64,2,13248]{2,1,0:T(2,128)(2,1)S(1)} async-done(((bf16[64,2,13248]{2,1,0:T(2,128)(2,1)}), bf16[64,2,13248]{2,1,0:T(2,128)(2,1)S(1)}, u32[]{:S(2)}, u32[]{:S(2)}) %all-to-all-start) | async-done | bytes 3391520 | tf_op jit(solution)/shard_map/all_to_all | solution.py:141
  335.8 13.8 %reshape.115 = bf16[384,1,4416]{2,1,0:T(2,128)(2,1)} reshape(bf16[64,2,13248]{2,1,0:T(2,128)(2,1)S(1)} %all-to-all-done) | data formatting | bytes 6782976
  349.5 22.2 %bitcast_reduce_fusion = bf16[384,4416]{1,0:T(8,128)(2,1)S(1)} fusion(bf16[384,1,4416]{2,1,0:T(2,128)(2,1)} %reshape.115), kind=kLoop, calls=%fused_computation.127 | loop fusion | bytes 6782976 | tf_op jit(solution)/shard_map/all_to_all | solution.py:141
  371.8 24.7 %convert_reduce_fusion = f32[384,4416]{1,0:T(8,128)} fusion(bf16[384,1,4416]{2,1,0:T(2,128)(2,1)} %reshape.115), kind=kLoop, calls=%fused_computation.53 | loop fusion | flops 1695744 | bytes 10174464 | tf_op jit(solution)/shard_map/convert_element_type | solution.py:143
  396.5 8.0 %reshape.104 = f32[64,6,4416]{2,1,0:T(8,128)} reshape(f32[384,4416]{1,0:T(8,128)} %convert_reduce_fusion) | data formatting | bytes 13565952 | tf_op jit(solution)/shard_map/convert_element_type | solution.py:143
  404.5 4.9 reduce_sum.46
  411.0 7.7 %broadcast_subtract_fusion = f32[64,6,4416]{2,1,0:T(8,128)} fusion(f32[64,6,4416]{2,1,0:T(8,128)} %reshape.104, f32[6,4416]{1,0:T(8,128)S(1)} %broadcast_multiply_fusion.1), kind=kLoop, calls=%fused_computation.69 | loop fusion | flops 1695744 | bytes 13671936 | tf_op jit(solution)/shard_map/sub | solution.py:145
  418.7 7.0 reshape.101
  425.7 5.5 fusion.43
  432.6 16.3 %while.35 = (s32[]{:T(128)}, f32[6,64,64]{1,2,0:T(8,128)S(1)}, f32[6,64,64]{2,1,0:T(8,128)S(1)}, f32[64,64]{1,0:T(8,128)S(1)}, s32[]{:T(128)}) while((s32[]{:T(128)}, f32[6,64,64]{1,2,0:T(8,128)S(1)}, f32[6,64,64]{2,1,0:T(8,128)S(1)}, f32[64,64]{1,0:T(8,128)S(1)}, s32[]{:T(128)}) %tuple.71), condition=%wide.region_9.10_spmd.clone, body=%wide.region_8.9_spmd.clone.sunk | while | flops 56676352 | bytes 1327165 | solution.py:118
  449.8 12.6 %fusion.45 = f32[64,6,4416]{2,0,1:T(8,128)S(1)} fusion(f32[64,6,4416]{2,1,0:T(8,128)} %broadcast_subtract_fusion, f32[6,4416]{1,0:T(8,128)S(1)} %copy-done.4, f32[6,64,64]{2,1,0:T(8,128)S(1)} %get-tuple-element.93, f32[6,64]{1,0:T(8,128)S(1)} %bitcast_divide_fusion, f32[6]{0:T(128)S(1)} %get-tuple-element.191), kind=kOutput, calls=%fused_computation.49 | convolution fusion | flops 1304076288 | bytes 13771800 | tf_op jit(solution)/shard_map/pmn,mpk->npk/dot_general | solution.py:151
  466.2 64.7 %psum.7 = f32[]{:T(128)} all-reduce(f32[]{:T(128)} %slice_reduce_fusion), channel_id=1, replica_groups=mesh['role'=2,'dev'=64] {'role','dev'}, use_global_device_ids=true, to_apply=%region_11.12 | all-reduce | flops 1 | bytes 8 | tf_op jit(solution)/shard_map/psum | solution.py:129
  535.7 62.6 %all_to_all.8 = bf16[64,6,4416]{2,1,0:T(8,128)(2,1)} all-to-all(bf16[64,6,4416]{2,1,0:T(8,128)(2,1)S(1)} %copy.47), channel_id=1, replica_groups=mesh['role'=2,'dev'=64] {'dev'}, dimensions={0} | all-to-all | bytes 6782976 | tf_op jit(solution)/shard_map/all_to_all | solution.py:157
  598.3 41.2 %reshape.102 = bf16[1,8,48,69,8,8]{5,4,3,2,1,0:T(8,128)(2,1)} reshape(bf16[64,6,4416]{2,1,0:T(8,128)(2,1)} %all_to_all.8) | data formatting | bytes 6782976 | tf_op jit(solution)/shard_map/reshape | solution.py:70
  639.5 53.0 %copy.48 = bf16[1,69,8,8,48,8]{1,5,4,3,2,0:T(8,128)(2,1)} copy(bf16[1,69,8,8,48,8]{5,3,1,4,2,0:T(8,128)(2,1)} %bitcast.170) | data formatting | bytes 6782976 | tf_op jit(solution)/shard_map/transpose | solution.py:78
  692.5 8.1 %copy.49 = bf16[1,69,64,384]{3,2,1,0:T(8,128)(2,1)} copy(bf16[1,69,64,384]{1,3,2,0:T(8,128)(2,1)} %bitcast.175) | data formatting | bytes 6782976 | tf_op jit(solution)/shard_map/reshape | solution.py:78
  (142 shorter events, 85.5 us)
Async XLA Ops:
  2.0 17.3 %collective-permute-start = (bf16[1,69,1,384]{3,2,1,0:T(2,128)(2,1)}, bf16[1,69,1,384]{3,2,1,0:T(2,128)(2,1)S(1)}, u32[]{:S(2)}, u32[]{:S(2)}) collective-permute-start(bf16[1,69,1,384]{3,2,1,0:T(2,128)(2,1)} %get-tuple-element.183), channel_id=1, source_target_pairs={{64,0},{65,1},{66,2},{67,3},{68,4},{69,5},{70,6},{71,7},{72,8},{73... | collective-permute-start | bytes 158984 | tf_op jit(solution)/shard_map/ppermute | solution.py:23
  3.3 13.4 %copy-start = (bf16[1,69,64,384]{3,2,1,0:T(8,128)(2,1)S(1)}, bf16[1,69,64,384]{3,2,1,0:T(8,128)(2,1)}, u32[]{:S(2)}) copy-start(bf16[1,69,64,384]{3,2,1,0:T(8,128)(2,1)} %param.15) | copy-start | bytes 10174468
  3.3 16.0 %collective-permute-start.1 = (bf16[1,69,1,384]{3,2,1,0:T(2,128)(2,1)}, bf16[1,69,1,384]{3,2,1,0:T(2,128)(2,1)}, u32[]{:S(2)}, u32[]{:S(2)}) collective-permute-start(bf16[1,69,1,384]{3,2,1,0:T(2,128)(2,1)} %get-tuple-element.184), channel_id=1, source_target_pairs={{0,64},{1,65},{2,66},{3,67},{4,68},{5,69},{6,70},{7,71},{8,72},{9,... | collective-permute-start | bytes 158984 | tf_op jit(solution)/shard_map/ppermute | solution.py:22
  16.7 2.6 copy-start.7
  35.8 7.5 %copy-start.8 = (bf16[512,69]{0,1:T(8,128)(2,1)S(1)}, bf16[512,69]{0,1:T(8,128)(2,1)}, u32[]{:S(2)}) copy-start(bf16[512,69]{0,1:T(8,128)(2,1)} %param.17) | copy-start | bytes 211972
  35.8 7.5 %copy-start.11 = (f32[512]{0:T(512)S(1)}, f32[512]{0:T(512)}, u32[]{:S(2)}) copy-start(f32[512]{0:T(512)} %param.18) | copy-start | bytes 6148
  39.6 3.8 copy-start.9
  110.4 5.5 copy-start.1
  110.4 5.3 collective-permute-start.2
  112.0 4.0 collective-permute-start.3
  130.2 9.5 %copy-start.10 = (bf16[69,512]{1,0:T(8,128)(2,1)S(1)}, bf16[69,512]{1,0:T(8,128)(2,1)}, u32[]{:S(2)}) copy-start(bf16[69,512]{1,0:T(8,128)(2,1)} %param.19) | copy-start | bytes 211972
  278.9 56.9 %all-to-all-start = ((bf16[64,2,13248]{2,1,0:T(2,128)(2,1)}), bf16[64,2,13248]{2,1,0:T(2,128)(2,1)S(1)}, u32[]{:S(2)}, u32[]{:S(2)}) async-start(bf16[64,2,13248]{2,1,0:T(2,128)(2,1)} %reshape.114), calls=%async_computation | async-start | bytes 6815744 | tf_op jit(solution)/shard_map/all_to_all | solution.py:141
  410.3 0.7 copy-start.3
  425.7 5.5 copy-start.6
  425.7 5.6 copy-start.5
  432.5 17.2 %copy-start.4 = (f32[6,4416]{1,0:T(8,128)S(1)}, f32[6,4416]{1,0:T(8,128)}, u32[]{:S(2)}) copy-start(f32[6,4416]{1,0:T(8,128)} %copy-done.3) | copy-start | bytes 317956
  462.4 2.8 copy-start.2
where the time goes:
time: 708 us; the launch traced here: 701 us
  local copies, waits for them, and re-layouts  299 us (42%)
  blocking collectives  127 us (18%)
  matrix products  112 us (16%)
  other arithmetic  95.7 us (14%)
  waiting for transfers between devices  42.6 us (6%)
  starting transfers between devices  21.5 us (3%)
    dot_general x16, matrix products, process_block(): jnp.einsum('fh,mhc->mfc', w_out, hidden, preferred_element_type=jnp.float32)  77.1 us
    psum x1, blocking collectives, global_total(): return lax.psum(partial_value, ('role', 'dev'))  64.7 us
    all_to_all x1, blocking collectives, body(): lax.all_to_all(nudged, 'dev', split_axis=0, concat_axis=1, tiled=True)  62.6 us
    transpose x1, local copies, waits for them, and re-layouts, from_patches(): shaped.transpose(0, 3, 1, 4, 2, 5)  53 us
    all_to_all x1, waiting for transfers between devices, body(): lax.all_to_all(tile_partition, 'dev', split_axis=1, concat_axis=0, tiled=...  42.4 us
    reshape x1, local copies, waits for them, and re-layouts, from_patches(): tile_partition.reshape(members_here, lat_rows // TILE_EDGE_POINTS, lon_ce...  41.2 us
    convert_element_type x1, other arithmetic, body(): values = gathered.astype(jnp.float32)  24.7 us
    reshape x2, local copies, waits for them, and re-layouts, to_patches(): shaped.transpose(0, 2, 4, 1, 3, 5)  22.9 us
  transfers between devices with their start and end apart: 5, of which 2 were waited for; matrix products, arithmetic and copies ran while one was open for 2% of the time, Pallas kernels for 0%

commit v1 on v0

v1 whole, which is shorter than its diff:
```python
import jax
import jax.numpy as jnp
from jax import lax
from jax.experimental import pallas as pl
from jax.experimental.pallas import tpu as pltpu
from jax.sharding import PartitionSpec as P

EDGE = 8
NS_ITERS = 12
CELLS = 64
LANES = 128
FIELDS = 69
PADDED = 72
LATENT = 512
LON = 384
TILES = 3
ROWS = 64
MEMBERS = 64
OBS = 128
GROUP = 16
BLOCK = 256
VMEM = 56 * 1024 * 1024
GELU_A = 0.7978845608028654
GELU_B = 0.044715 * 0.7978845608028654
VALUES = MEMBERS * 128 * LON

ANY_VMEM = pl.BlockSpec(memory_space=pltpu.VMEM)
ANY_SMEM = pl.BlockSpec(memory_space=pltpu.SMEM)


def params():
    return pltpu.CompilerParams(vmem_limit_bytes=VMEM)


def mlp(smooth, w_in, w_out):
    total = None
    for part in range(LATENT // BLOCK):
        rows = slice(part * BLOCK, (part + 1) * BLOCK)
        linear = jnp.dot(w_in[rows, :], smooth, preferred_element_type=jnp.float32)
        inner = linear * (GELU_A + GELU_B * (linear * linear))
        hidden = (linear + linear * jnp.tanh(inner)).astype(jnp.bfloat16)
        change = jnp.dot(w_out[:, rows], hidden, preferred_element_type=jnp.float32)
        total = change if total is None else total + change
    return total


def first_kernel(role_ref, x_ref, halo_ref, diff_ref, w_in_ref, w_out_ref, out_ref, turn, state):
    role = role_ref[0]
    turn[...] = jnp.ones_like(turn)

    def take(block, rows, place):
        block = block.astype(jnp.float32)
        for tile in range(TILES):
            lanes = slice(tile * LANES, (tile + 1) * LANES)
            turn[tile, 0 : FIELDS * rows, :] = block[:, :, lanes].reshape(FIELDS * rows, LANES)
        for a in range(rows):
            for tile in range(TILES):
                state[place + a, :, tile * LANES : (tile + 1) * LANES] = turn[
                    tile, pl.ds(a, PADDED, stride=rows), :
                ]

    state[0:8] = jnp.zeros((8, PADDED, LON), jnp.float32)
    state[72:80] = jnp.zeros((8, PADDED, LON), jnp.float32)
    take(halo_ref[...], 8, jnp.where(role == 0, 72, 0))
    turn[...] = jnp.ones_like(turn)

    def load(step, carry):
        rows = pl.ds(pl.multiple_of(step * 16, 16), 16)
        take(x_ref[:, rows, :], 16, 8 + step * 16)
        return carry

    lax.fori_loop(0, ROWS // 16, load, 0)
    diff = diff_ref[...]
    w_in = w_in_ref[...]
    w_out = w_out_ref[...]

    def pair(step, carry):
        smooth = []
        centre = []
        for k in range(2):
            row = step * 2 + k + 7
            c = state[row]
            around = state[row - 1] + state[row + 1] + pltpu.roll(c, 1, 1) + pltpu.roll(c, LON - 1, 1)
            smooth.append((c + diff * (around - 4.0 * c)).astype(jnp.bfloat16))
            centre.append(c)
        smooth = jnp.concatenate(smooth, axis=1)
        centre = jnp.concatenate(centre, axis=1)
        new = []
        for n in range(2 * LON // BLOCK):
            cols = slice(n * BLOCK, (n + 1) * BLOCK)
            new.append(centre[:, cols] + mlp(smooth[:, cols], w_in, w_out))
        new = jnp.concatenate(new, axis=1).astype(jnp.bfloat16)
        out_ref[step * 2] = new[:, :LON]
        out_ref[step * 2 + 1] = new[:, LON:]
        return carry

    lax.fori_loop(0, (ROWS + 2) // 2, pair, 0)

    @pl.when(role == 0)
    def _():
        out_ref[0] = jnp.zeros((PADDED, LON), jnp.bfloat16)

    @pl.when(role == 1)
    def _():
        out_ref[ROWS + 1] = jnp.zeros((PADDED, LON), jnp.bfloat16)


def swap_groups(rows):
    lane = lax.broadcasted_iota(jnp.int32, rows[0].shape, 1)
    for bit in (4, 2, 1):
        shift = bit * GROUP
        high = (lane & shift) != 0
        new = list(rows)
        for a in range(8):
            if a & bit:
                continue
            first, second = rows[a], rows[a + bit]
            new[a] = jnp.where(high, pltpu.roll(second, shift, 1), first)
            new[a + bit] = jnp.where(high, second, pltpu.roll(first, LANES - shift, 1))
        rows = new
    return rows


def second_kernel(tiles, state_ref, diff_ref, w_in_ref, w_out_ref, out_ref):
    diff = diff_ref[...][:, :LANES]
    w_in = w_in_ref[...]
    w_out = w_out_ref[...]
    lane = lax.broadcasted_iota(jnp.int32, (PADDED, LANES), 1)
    first_lane = lane == 0
    last_lane = lane == LANES - 1

    def piece(row, tile):
        return state_ref[row, :, tile * LANES : (tile + 1) * LANES].astype(jnp.float32)

    def block(r, carry):
        pieces = []
        for a in range(8):
            row = r * 8 + a + 1
            for tile in tiles:
                c = piece(row, tile)
                before = piece(row, (tile - 1) % TILES)
                after = piece(row, (tile + 1) % TILES)
                left = pltpu.roll(jnp.where(last_lane, before, c), 1, 1)
                right = pltpu.roll(jnp.where(first_lane, after, c), LANES - 1, 1)
                around = piece(row - 1, tile) + piece(row + 1, tile) + left + right
                pieces.append((c, (c + diff * (around - 4.0 * c)).astype(jnp.bfloat16)))
        new = []
        for first, second in zip(pieces[0::2], pieces[1::2]):
            change = mlp(jnp.concatenate([first[1], second[1]], axis=1), w_in, w_out)
            new.append(first[0] + change[:, :LANES])
            new.append(second[0] + change[:, LANES:])
        for k in range(len(tiles)):
            for t, message in enumerate(swap_groups(new[k :: len(tiles)])):
                out_ref[r * 8 + t, k] = message.astype(jnp.bfloat16)
        return carry

    lax.fori_loop(0, ROWS // 8, block, 0)


def split(a):
    high = a.astype(jnp.bfloat16)
    return high, (a - high.astype(jnp.float32)).astype(jnp.bfloat16)


def dot3(a, b, contract=((1,), (0,))):
    (a_high, a_low), (b_high, b_low) = split(a), split(b)

    left = jnp.concatenate([a_high, a_low, a_high], axis=1)
    right = jnp.concatenate([b_high, b_high, b_low], axis=contract[1][0])
    return lax.dot_general(left, right, (contract, ((), ())), preferred_element_type=jnp.float32)


def weights_of(observed, value, weight):
    eye = jnp.where(
        lax.broadcasted_iota(jnp.int32, (MEMBERS, MEMBERS), 0)
        == lax.broadcasted_iota(jnp.int32, (MEMBERS, MEMBERS), 1),
        1.0,
        0.0,
    )
    obs_mean = jnp.sum(observed, axis=0, keepdims=True) * (1.0 / MEMBERS)
    spread = observed - obs_mean
    innovation = value - obs_mean
    weighted = spread * weight
    precision = (MEMBERS - 1.0) * eye + dot3(weighted, spread, ((1,), (1,)))
    pulled = jnp.sum(weighted * innovation, axis=1, keepdims=True)
    pulled = jnp.broadcast_to(pulled, (MEMBERS, MEMBERS))
    trace = jnp.sum(jnp.sum(precision * eye, axis=0, keepdims=True), axis=1, keepdims=True)
    scale = MEMBERS * trace
    return eye, precision / scale, pulled, scale


def mix_kernel(nt, last, *refs):
    if last:
        (idx_ref, value_ref, weight_ref, part_ref, g_ref, out_ref, picked, turn, back) = refs
    else:
        (idx_ref, value_ref, weight_ref, g_ref, out_ref, part_out, picked, turn, back) = refs
    f32, bf16 = jnp.float32, jnp.bfloat16

    gather_sum = jnp.where(
        lax.broadcasted_iota(jnp.int32, (MEMBERS, MEMBERS * 8), 1) >> 3
        == lax.broadcasted_iota(jnp.int32, (MEMBERS, MEMBERS * 8), 0),
        1.0,
        0.0,
    ).astype(bf16)
    patches = []
    for k in range(nt):
        idx = jnp.concatenate([idx_ref[2 * k : 2 * k + 1, :], idx_ref[2 * k + 1 : 2 * k + 2, :]], axis=1)
        odd = (lax.broadcasted_iota(jnp.int32, (1, 2 * OBS), 1) >= OBS).astype(jnp.int32)
        cell = idx & (CELLS - 1)
        lane = (cell >> 3) * GROUP + odd * EDGE + (cell & 7)
        field = idx >> 6
        hot = jnp.where(lax.broadcasted_iota(jnp.int32, (LANES, 2 * OBS), 0) == lane, 1.0, 0.0).astype(bf16)
        mask = lax.broadcasted_iota(jnp.int32, (PADDED, 2 * OBS), 0) == field

        def pick(step, carry):
            m = pl.multiple_of(step * 8, 8)
            block = g_ref[pl.ds(m, 8), k].astype(f32).reshape(8 * PADDED, LANES)
            turn[k, pl.ds(pl.multiple_of(step * 8 * PADDED, 8), 8 * PADDED), :] = block
            values = jnp.dot(block.astype(bf16), hot, preferred_element_type=f32)
            values = jnp.where(mask[None], values.reshape(8, PADDED, 2 * OBS), 0.0)
            values = jnp.sum(values.reshape(8, PADDED // 8, 8, 2 * OBS), axis=1)
            picked[pl.ds(pl.multiple_of(step * 64, 64), 64), :] = values.reshape(64, 2 * OBS)
            return carry

        lax.fori_loop(0, MEMBERS // 8, pick, 0)
        observed = jnp.dot(gather_sum, picked[...].astype(bf16), preferred_element_type=f32)
        for e in range(2):
            patches.append(
                weights_of(
                    observed[:, e * OBS : (e + 1) * OBS],
                    value_ref[2 * k + e : 2 * k + e + 1, :],
                    weight_ref[2 * k + e : 2 * k + e + 1, :],
                )
            )
    eye = patches[0][0]

    def newton(step, carry):
        new = []
        for iterate, root in carry:
            factor = 0.5 * (3.0 * eye - dot3(root, iterate))
            new.append((dot3(iterate, factor), dot3(factor, root)))
        return tuple(new)

    carry = tuple((iterate, eye) for _, iterate, _, _ in patches)
    carry = lax.fori_loop(0, NS_ITERS, newton, carry)
    mixes = []
    for (_, root), (_, _, pulled, scale) in zip(carry, patches):
        combined = jnp.sqrt((MEMBERS - 1.0) / scale) * root + dot3(root, dot3(root, pulled)) / scale
        rest = (1.0 - jnp.sum(combined, axis=0, keepdims=True)) * (1.0 / MEMBERS)
        mixes.append((combined + rest).T)
    even = (lax.broadcasted_iota(jnp.int32, (MEMBERS, LANES), 1) & EDGE) == 0
    partial = jnp.zeros((1, 1), f32)
    for k in range(nt):
        mix = jnp.concatenate(mixes[2 * k : 2 * k + 2], axis=0).astype(bf16)

        def apply(f):
            x = turn[k, pl.ds(f, MEMBERS, stride=PADDED), :].astype(bf16)
            both = jnp.dot(mix, x, preferred_element_type=f32)
            mixed = jnp.where(even, both[:MEMBERS], both[MEMBERS:])
            back[k, pl.ds(f, MEMBERS, stride=PADDED), :] = mixed
            return mixed

        for f in range(FIELDS):
            mixed = apply(f)
            if f == 0:
                part = jnp.sum(jnp.sum(mixed, axis=0, keepdims=True), axis=1, keepdims=True)
                partial = partial + part
    if last:
        partial = partial + part_ref[0:1, 0:1]
        high = partial.astype(bf16).astype(f32)
        middle = (partial - high).astype(bf16).astype(f32)
        low = partial - high - middle
    else:
        part_out[...] = jnp.broadcast_to(partial, (8, LANES))
    for k in range(nt):
        for row, extra in zip(range(FIELDS, PADDED), (high, middle, low) if last else (partial,) * 3):
            back[k, pl.ds(row, MEMBERS, stride=PADDED), :] = jnp.broadcast_to(extra, (MEMBERS, LANES))

        def give(step, carry):
            m = pl.multiple_of(step * 8, 8)
            block = back[k, pl.ds(pl.multiple_of(step * 8 * PADDED, 8), 8 * PADDED), :]
            out_ref[pl.ds(m, 8), k] = block.reshape(8, PADDED, LANES).astype(bf16)
            return carry

        lax.fori_loop(0, MEMBERS // 8, give, 0)


def last_kernel(offset_ref, *refs):
    sources, out_ref, turn = refs[:-2], refs[-2], refs[-1]
    offset = offset_ref[0]
    first = lax.broadcasted_iota(jnp.int32, (FIELDS, 1, LANES), 0) == 0
    add = jnp.where(first, offset, 0.0)
    places = [(ref, k) for ref in sources for k in range(ref.shape[1])]

    def block(step, carry):
        for tile, (ref, k) in enumerate(places):
            for half in range(2):
                rows = [ref[(step * 2 + half) * 8 + t, k].astype(jnp.float32) for t in range(8)]
                for a, row in enumerate(swap_groups(rows)):
                    turn[tile, pl.ds(half * 8 + a, PADDED, stride=16), :] = row
            values = turn[tile, 0 : FIELDS * 16, :].reshape(FIELDS, 16, LANES) + add
            place = pl.ds(pl.multiple_of(step * 16, 16), 16)
            out_ref[:, place, tile * LANES : (tile + 1) * LANES] = values.astype(jnp.bfloat16)
        return carry

    lax.fori_loop(0, ROWS // 16, block, 0)


def cost(flops, size, tanhs=0):
    return pl.CostEstimate(flops=flops, bytes_accessed=size, transcendentals=tanhs)


def forecast_first(role, x, halo, diff, w_in, w_out):
    cells = (ROWS + 2) * LON
    return pl.pallas_call(
        first_kernel,
        out_shape=jax.ShapeDtypeStruct((ROWS + 2, PADDED, LON), jnp.bfloat16),
        in_specs=[ANY_SMEM] + [ANY_VMEM] * 5,
        out_specs=ANY_VMEM,
        scratch_shapes=[
            pltpu.VMEM((TILES, PADDED * 16, LANES), jnp.float32),
            pltpu.VMEM((ROWS + 16, PADDED, LON), jnp.float32),
        ],
        compiler_params=params(),
        cost_estimate=cost(cells * LATENT * 256 * 4, 7 << 20, cells * LATENT),
        name="forecast_first",
    )(role, x, halo, diff, w_in, w_out)


def forecast_second(tiles, state, diff, w_in, w_out):
    cells = ROWS * LANES * len(tiles)
    return pl.pallas_call(
        lambda *refs: second_kernel(tiles, *refs),
        out_shape=jax.ShapeDtypeStruct((MEMBERS, len(tiles), PADDED, LANES), jnp.bfloat16),
        in_specs=[ANY_VMEM] * 4,
        out_specs=ANY_VMEM,
        compiler_params=params(),
        cost_estimate=cost(cells * LATENT * 256 * 4, 5 << 20, cells * LATENT),
        name="forecast_second",
    )(state, diff, w_in, w_out)


def mix(last, idx, value, weight, g, *part):
    nt = g.shape[1]
    message = jax.ShapeDtypeStruct(g.shape, jnp.bfloat16)
    sums = jax.ShapeDtypeStruct((8, LANES), jnp.float32)
    return pl.pallas_call(
        lambda *refs: mix_kernel(nt, last, *refs),
        out_shape=message if last else (message, sums),
        in_specs=[ANY_VMEM] * (4 + len(part)),
        out_specs=ANY_VMEM if last else (ANY_VMEM, ANY_VMEM),
        scratch_shapes=[
            pltpu.VMEM((MEMBERS * 8, 2 * OBS), jnp.float32),
            pltpu.VMEM((nt, MEMBERS * PADDED, LANES), jnp.float32),
            pltpu.VMEM((nt, MEMBERS * PADDED, LANES), jnp.float32),
        ],
        compiler_params=params(),
        cost_estimate=cost(8 << 30, 4 << 20),
        name="mix",
    )(idx, value, weight, *part, g)


def put_back(offset, *sources):
    return pl.pallas_call(
        last_kernel,
        out_shape=jax.ShapeDtypeStruct((FIELDS, ROWS, LON), jnp.bfloat16),
        in_specs=[ANY_SMEM] + [ANY_VMEM] * len(sources),
        out_specs=ANY_VMEM,
        scratch_shapes=[pltpu.VMEM((TILES, PADDED * 16, LANES), jnp.float32)],
        compiler_params=params(),
        cost_estimate=cost(1 << 20, 7 << 20),
        name="put_back",
    )(offset, *sources)


def exchange(messages):
    return lax.all_to_all(messages, "dev", split_axis=0, concat_axis=0, tiled=True)


def share_observations(obs_value, obs_weight):
    both = jnp.stack([obs_value.reshape(3, 2, OBS), obs_weight.reshape(3, 2, OBS)], axis=1)
    groups = [[8 * r + t for t in range(8)] for r in range(8)]
    sent = jnp.broadcast_to(both[None], (8, 3, 2, 2, OBS))
    got = lax.all_to_all(sent, "dev", 0, 0, axis_index_groups=groups, tiled=True)
    pairs = got.reshape(24, 2, 2, OBS)
    t = lax.axis_index("dev") % 8
    mine = jnp.stack([lax.dynamic_index_in_dim(pairs, 8 * j + t, 0, False) for j in range(TILES)])
    return mine[:, 0].reshape(6, OBS), mine[:, 1].reshape(6, OBS)


def body(
    initial_realizations, diffusivity, w_in, b_in, w_out, obs_index, obs_value, obs_weight, climate
):
    role = lax.axis_index("role")
    dev = lax.axis_index("dev")
    x = initial_realizations.reshape(FIELDS, ROWS, LON)
    edge = lax.dynamic_slice_in_dim(x, jnp.where(role == 0, ROWS - 8, 0), 8, 1)
    halo = lax.ppermute(edge, "role", [(0, 1), (1, 0)])
    b_high = lax.reduce_precision(b_in, 8, 7)
    b_middle = lax.reduce_precision(b_in - b_high, 8, 7)
    b_low = b_in - b_high - b_middle
    bias = jnp.stack([b_high, b_middle, b_low], axis=1).astype(jnp.bfloat16)
    w_first = jnp.concatenate([w_in, bias], axis=1)
    w_second = jnp.pad(w_out * jnp.bfloat16(0.5), ((0, PADDED - FIELDS), (0, 0)))
    diff = jnp.broadcast_to(jnp.pad(diffusivity, (0, PADDED - FIELDS))[:, None], (PADDED, LON))

    value, weight = share_observations(obs_value, obs_weight)
    rows = lax.dynamic_slice_in_dim(obs_index, (dev // 8) * 48, 48, 0).reshape(TILES, 8, 2, OBS)
    index = lax.dynamic_index_in_dim(rows, dev % 8, 1, False).reshape(6, OBS)

    state = forecast_first(role.reshape(1), x, halo, diff, w_first, w_second)
    sent_a = forecast_second((0, 1), state, diff, w_first, w_second)
    got_a = exchange(sent_a)
    sent_b = forecast_second((2,), state, diff, w_first, w_second)
    got_b = exchange(sent_b)
    mixed_a, part = mix(False, index[:4], value[:4], weight[:4], got_a)
    back_a = exchange(mixed_a)
    mixed_b = mix(True, index[4:], value[4:], weight[4:], got_b, part)
    back_b = exchange(mixed_b)
    total = jnp.sum(back_b[:, 0, FIELDS:, 0].astype(jnp.float32))
    total = lax.psum(total, "role")
    offset = climate - total / VALUES
    return put_back(offset, back_a, back_b)[None]


def solution(mesh):
    in_specs = (
        P("dev", None, "role", None),
        P(),
        P(),
        P(),
        P(),
        P("role", None),
        P(("role", "dev"), None),
        P(("role", "dev"), None),
        P(),
    )
    out_specs = P("dev", None, "role", None)
    return jax.shard_map(body, mesh=mesh, in_specs=in_specs, out_specs=out_specs, check_vma=False)
```

time: 708 us -> 255 us (0.36)
  local copies, waits for them, and re-layouts: 299 us -> 9.8 us
  Pallas kernels: 0 us -> 135 us
  matrix products: 112 us -> 0 us
  blocking collectives: 127 us -> 32.7 us
  other arithmetic: 95.7 us -> 4.61 us
  starting transfers between devices: 21.5 us -> 28.9 us
    pallas_call x0 -> x6, Pallas kernels: none -> 135 us  [the longest x2 44.5 us: forecast_second(): pl.pallas_call(lambda *refs: second_kernel(tiles, *refs), out_shape=jax.S...]
    dot_general x58 -> x0, matrix products: 112 us -> none  [the longest x16 77.1 us: process_block(): jnp.einsum('fh,mhc->mfc', w_out, hidden, preferred_element_type=jnp.float32)]
    reshape x9 -> x0, local copies, waits for them, and re-layouts: 107 us -> none  [the longest x1 41.2 us: from_patches(): tile_partition.reshape(members_here, lat_rows // TILE_EDGE_POINTS, lon_ce...]
    transpose x4 -> x0, local copies, waits for them, and re-layouts: 90.9 us -> none  [the longest x1 53 us: from_patches(): shaped.transpose(0, 3, 1, 4, 2, 5)]
    psum x1, blocking collectives: 64.7 us -> 3.11 us  [body(): total = lax.psum(total, 'role')]
    convert_element_type x6 -> x0, other arithmetic: 55.1 us -> none  [the longest x1 24.7 us: body(): values = gathered.astype(jnp.float32)]
    all_to_all x1, blocking collectives: 62.6 us -> 29.6 us  [exchange(): lax.all_to_all(messages, 'dev', split_axis=0, concat_axis=0, tiled=True)]
    all_to_all x1 -> x0, local copies, waits for them, and re-layouts: 22.2 us -> none  [body(): lax.all_to_all(tile_partition, 'dev', split_axis=1, concat_axis=0, tiled=...]
  transfers between devices with their start and end apart: 5 -> 5, of which waited for: 2 -> 2; matrix products, arithmetic and copies ran while one was open for 2% -> 4% of each run, Pallas kernels for 0% -> 43%
where the time goes in v1:
time: 255 us; the launch traced here: 254 us
  Pallas kernels  135 us (53%)
  waiting for transfers between devices  41.3 us (16%)
  blocking collectives  32.7 us (13%)
  starting transfers between devices  28.9 us (11%)
  local copies, waits for them, and re-layouts  9.8 us (4%)
  other arithmetic  4.61 us (2%)
    pallas_call x2, Pallas kernels, forecast_second(): pl.pallas_call(lambda *refs: second_kernel(tiles, *refs), out_shape=jax.S...  44.5 us
    pallas_call x1, Pallas kernels, forecast_first(): pl.pallas_call(first_kernel, out_shape=jax.ShapeDtypeStruct((ROWS + 2, PA...  44.4 us
    all_to_all x3, waiting for transfers between devices, exchange(): lax.all_to_all(messages, 'dev', split_axis=0, concat_axis=0, tiled=True)  41.3 us
    pallas_call x2, Pallas kernels, mix(): pl.pallas_call(lambda *refs: mix_kernel(nt, last, *refs), out_shape=messa...  34.4 us
    all_to_all x1, blocking collectives, exchange(): lax.all_to_all(messages, 'dev', split_axis=0, concat_axis=0, tiled=True)  29.6 us
    all_to_all x3, starting transfers between devices, exchange(): lax.all_to_all(messages, 'dev', split_axis=0, concat_axis=0, tiled=True)  22.4 us
    pallas_call x1, Pallas kernels, put_back(): pl.pallas_call(last_kernel, out_shape=jax.ShapeDtypeStruct((FIELDS, ROWS,...  11.8 us
    all_to_all x1, starting transfers between devices, share_observations(): lax.all_to_all(sent, 'dev', 0, 0, axis_index_groups=groups, tiled=True)  6.41 us
  transfers between devices with their start and end apart: 5, of which 2 were waited for; matrix products, arithmetic and copies ran while one was open for 4% of the time, Pallas kernels for 43%

profile of v1, /device:TPU:0, one launch (start us, length us, event | category | flops | bytes accessed | tf_op | source)
XLA Modules:
  0.0 254.0 jit_solution(6678697551886438929)
XLA Ops:
  0.0 0.0 copy-start
  0.0 0.7 stack_reshape.6
  0.7 0.7 stack_reshape.7
  1.4 0.6 broadcast_in_dim.6
  2.1 6.4 %all-to-all-start = ((f32[8,3,2,2,128]{4,3,2,1,0:T(2,128)}), f32[8,3,2,2,128]{4,3,2,1,0:T(2,128)S(1)}, u32[]{:S(2)}, u32[]{:S(2)}) async-start(f32[8,3,2,2,128]{4,3,2,1,0:T(2,128)} %broadcast_in_dim.6), calls=%async_computation | async-start | bytes 98304 | tf_op jit(solution)/shard_map/all_to_all | solution.py:384
  8.5 1.0 dynamic-slice_bitcast_fusion
  9.5 0.1 collective-permute-start
  9.6 0.7 reduce-precision_convert_fusion.1
  10.3 0.1 stack.28
  10.5 0.1 stack.30
  10.6 0.1 stack.29
  10.7 1.0 copy.13
  11.8 0.7 pad.8
  12.4 0.9 broadcast_multiply_fusion
  13.3 0.6 pad.9.w_out_ref.refs_3_
  13.9 0.8 pad_maximum_fusion.w_in_ref.refs_2_
  14.8 0.0 collective-permute-done.halo_ref
  14.8 0.0 copy-start.3
  14.8 0.8 broadcast_in_dim.7.diff_ref.refs_1_
  15.6 0.0 copy-done.3
  15.6 44.4 %forecast_first.1.refs_0_ = bf16[66,72,384]{2,1,0:T(8,128)(2,1)} custom-call(s32[1]{0:T(128)} %bitcast.8.role_ref, bf16[69,64,384]{2,1,0:T(8,128)(2,1)} %bitcast.19, bf16[69,8,384]{2,1,0:T(8,128)(2,1)} %copy-done.3, f32[72,384]{1,0:T(8,128)} %broadcast_in_dim.7.diff_ref.refs_1_, bf16[512,72]{1,0:T(8,128)(2,1)} %pad_maximum_fusion.w_in_ref.refs_2_, ...), custom_call_target="tpu_custom_call" | custom-call | flops 13287555072 | bytes 7340032 | tf_op jit(solution)/shard_map/forecast_first/pallas_call | solution.py:315
  60.0 28.3 %forecast_second.2 = bf16[64,2,72,128]{3,2,1,0:T(8,128)(2,1)} custom-call(bf16[66,72,384]{2,1,0:T(8,128)(2,1)} %forecast_first.1.refs_0_, f32[72,384]{1,0:T(8,128)} %broadcast_in_dim.7.diff_ref.refs_1_, bf16[512,72]{1,0:T(8,128)(2,1)} %pad_maximum_fusion.w_in_ref.refs_2_, bf16[72,512]{1,0:T(8,128)(2,1)} %pad.9.w_out_ref.refs_3_), custom_call_target="tpu_custom_call" | custom-call | flops 8589934592 | bytes 5242880 | tf_op jit(solution)/shard_map/forecast_second/pallas_call | solution.py:332
  88.3 0.0 all-to-all-done
  88.3 10.6 %all-to-all-start.1 = ((bf16[64,2,72,128]{3,2,1,0:T(8,128)(2,1)}), bf16[64,2,72,128]{3,2,1,0:T(8,128)(2,1)S(1)}, u32[]{:S(2)}, u32[]{:S(2)}) async-start(bf16[64,2,72,128]{3,2,1,0:T(8,128)(2,1)} %forecast_second.2), calls=%async_computation.1 | async-start | bytes 4718592 | tf_op jit(solution)/shard_map/all_to_all | solution.py:377
  99.0 0.0 copy-done
  99.0 0.6 constant_dynamic-slice_fusion.5
  99.6 16.2 %forecast_second.3 = bf16[64,1,72,128]{3,2,1,0:T(8,128)(2,1)} custom-call(bf16[66,72,384]{2,1,0:T(8,128)(2,1)} %forecast_first.1.refs_0_, f32[72,384]{1,0:T(8,128)} %broadcast_in_dim.7.diff_ref.refs_1_, bf16[512,72]{1,0:T(8,128)(2,1)} %pad_maximum_fusion.w_in_ref.refs_2_, bf16[72,512]{1,0:T(8,128)(2,1)} %pad.9.w_out_ref.refs_3_), custom_call_target="tpu_custom_call" | custom-call | flops 4294967296 | bytes 5242880 | tf_op jit(solution)/shard_map/forecast_second/pallas_call | solution.py:332
  115.8 15.6 %all-to-all-done.1.refs_3_ = bf16[64,2,72,128]{3,2,1,0:T(8,128)(2,1)S(1)} async-done(((bf16[64,2,72,128]{3,2,1,0:T(8,128)(2,1)}), bf16[64,2,72,128]{3,2,1,0:T(8,128)(2,1)S(1)}, u32[]{:S(2)}, u32[]{:S(2)}) %all-to-all-start.1) | async-done | bytes 2359328 | tf_op jit(solution)/shard_map/all_to_all | solution.py:377
  131.4 0.0 copy-start.2
  131.4 7.1 %all-to-all-start.2 = ((bf16[64,1,72,128]{3,2,1,0:T(8,128)(2,1)}), bf16[64,1,72,128]{3,2,1,0:T(8,128)(2,1)}, u32[]{:S(2)}, u32[]{:S(2)}) async-start(bf16[64,1,72,128]{3,2,1,0:T(8,128)(2,1)} %forecast_second.3), calls=%async_computation.2 | async-start | bytes 2359296 | tf_op jit(solution)/shard_map/all_to_all | solution.py:377
  138.5 0.6 fusion.3.refs_0_
  139.1 0.6 fusion.2
  139.7 0.6 pad_maximum_fusion.2
  140.3 0.0 copy-done.2
  140.3 21.5 %mix.2 = (bf16[64,2,72,128]{3,2,1,0:T(8,128)(2,1)}, f32[8,128]{1,0:T(8,128)}) custom-call(s32[4,128]{1,0:T(4,128)} %bitcast.22, f32[4,128]{1,0:T(4,128)} %bitcast.24, f32[4,128]{1,0:T(4,128)} %bitcast.23, bf16[64,2,72,128]{3,2,1,0:T(8,128)(2,1)} %copy-done.2), custom_call_target="tpu_custom_call" | custom-call | flops 8589934592 | bytes 4194304 | tf_op jit(solution)/shard_map/mix/pallas_call | solution.py:347
  161.8 0.0 all-to-all-done.2.refs_4_
  161.8 13.0 %mix.3 = bf16[64,1,72,128]{3,2,1,0:T(8,128)(2,1)} custom-call(s32[2,128]{1,0:T(2,128)} %fusion.3.refs_0_, f32[2,128]{1,0:T(2,128)} %get-tuple-element.12.refs_1_, f32[2,128]{1,0:T(2,128)} %get-tuple-element.11.refs_2_, f32[8,128]{1,0:T(8,128)} %get-tuple-element.7.refs_3_, bf16[64,1,72,128]{3,2,1,0:T(8,128)(2,1)} %all-to-all-done.2.refs_4_), custom_call_target="tpu_custom_call" | custom-call | flops 8589934592 | bytes 4194304 | tf_op jit(solution)/shard_map/mix/pallas_call | solution.py:347
  174.8 29.6 %all_to_all.25.refs_1_ = bf16[64,1,72,128]{3,2,1,0:T(8,128)(2,1)} all-to-all(bf16[64,1,72,128]{3,2,1,0:T(8,128)(2,1)} %mix.3), channel_id=1, replica_groups=mesh['role'=2,'dev'=64] {'dev'}, dimensions={0} | all-to-all | bytes 2359296 | tf_op jit(solution)/shard_map/all_to_all | solution.py:377
  204.4 4.7 %all-to-all-start.4 = ((bf16[64,2,72,128]{3,2,1,0:T(8,128)(2,1)}), bf16[64,2,72,128]{3,2,1,0:T(8,128)(2,1)S(1)}, u32[]{:S(2)}, u32[]{:S(2)}) async-start(bf16[64,2,72,128]{3,2,1,0:T(8,128)(2,1)} %get-tuple-element.8), calls=%async_computation.4 | async-start | bytes 4718592 | tf_op jit(solution)/shard_map/all_to_all | solution.py:377
  209.1 1.6 convert_reduce_fusion
  211.3 3.1 %psum.7 = f32[]{:T(128)} all-reduce(f32[]{:T(128)} %convert_reduce_fusion), channel_id=1, replica_groups=mesh['role'=2,'dev'=64] {'role'}, use_global_device_ids=true, to_apply=%region_1.2 | all-reduce | flops 1 | bytes 8 | tf_op jit(solution)/shard_map/psum | solution.py:421
  215.1 25.7 %all-to-all-done.4.refs_0_ = bf16[64,2,72,128]{3,2,1,0:T(8,128)(2,1)S(1)} async-done(((bf16[64,2,72,128]{3,2,1,0:T(8,128)(2,1)}), bf16[64,2,72,128]{3,2,1,0:T(8,128)(2,1)S(1)}, u32[]{:S(2)}, u32[]{:S(2)}) %all-to-all-start.4) | async-done | bytes 2359328 | tf_op jit(solution)/shard_map/all_to_all | solution.py:377
  240.8 0.0 copy-start.1
  240.8 1.4 copy-done.1
  242.2 11.8 %put_back.1 = bf16[69,64,384]{2,1,0:T(8,128)(2,1)} custom-call(f32[1]{0:T(128)S(6)} %sub.21.offset_ref, bf16[64,2,72,128]{3,2,1,0:T(8,128)(2,1)} %copy-done.1, bf16[64,1,72,128]{3,2,1,0:T(8,128)(2,1)} %all_to_all.25.refs_1_), custom_call_target="tpu_custom_call" | custom-call | flops 1048576 | bytes 7340032 | tf_op jit(solution)/shard_map/put_back/pallas_call | solution.py:364
  (4 shorter events, 0.0 us)
Async XLA Ops:
  0.0 99.0 %copy-start = (s32[384,128]{1,0:T(8,128)S(1)}, s32[384,128]{1,0:T(8,128)}, u32[]{:S(2)}) copy-start(s32[384,128]{1,0:T(8,128)} %param.14) | copy-start | bytes 589828
  2.1 86.2 %all-to-all-start = ((f32[8,3,2,2,128]{4,3,2,1,0:T(2,128)}), f32[8,3,2,2,128]{4,3,2,1,0:T(2,128)S(1)}, u32[]{:S(2)}, u32[]{:S(2)}) async-start(f32[8,3,2,2,128]{4,3,2,1,0:T(2,128)} %broadcast_in_dim.6), calls=%async_computation | async-start | bytes 98304 | tf_op jit(solution)/shard_map/all_to_all | solution.py:384
  9.5 5.2 %collective-permute-start = (bf16[69,8,384]{2,1,0:T(8,128)(2,1)S(1)}, bf16[69,8,384]{2,1,0:T(8,128)(2,1)S(1)}, u32[]{:S(2)}, u32[]{:S(2)}) collective-permute-start(bf16[69,8,384]{2,1,0:T(8,128)(2,1)S(1)} %dynamic-slice_bitcast_fusion), channel_id=1, source_target_pairs={{0,64},{64,0},{1,65},{65,1},{2,66},{66,2},{3,67},{67,3},{4,68},{68... | collective-permute-start | bytes 1271816 | tf_op jit(solution)/shard_map/ppermute | solution.py:398
  14.8 0.8 copy-start.3
  88.3 43.1 %all-to-all-start.1 = ((bf16[64,2,72,128]{3,2,1,0:T(8,128)(2,1)}), bf16[64,2,72,128]{3,2,1,0:T(8,128)(2,1)S(1)}, u32[]{:S(2)}, u32[]{:S(2)}) async-start(bf16[64,2,72,128]{3,2,1,0:T(8,128)(2,1)} %forecast_second.2), calls=%async_computation.1 | async-start | bytes 4718592 | tf_op jit(solution)/shard_map/all_to_all | solution.py:377
  131.4 8.9 %copy-start.2 = (bf16[64,2,72,128]{3,2,1,0:T(8,128)(2,1)}, bf16[64,2,72,128]{3,2,1,0:T(8,128)(2,1)S(1)}, u32[]{:S(2)}) copy-start(bf16[64,2,72,128]{3,2,1,0:T(8,128)(2,1)S(1)} %all-to-all-done.1.refs_3_) | copy-start | bytes 7077892
  131.4 30.4 %all-to-all-start.2 = ((bf16[64,1,72,128]{3,2,1,0:T(8,128)(2,1)}), bf16[64,1,72,128]{3,2,1,0:T(8,128)(2,1)}, u32[]{:S(2)}, u32[]{:S(2)}) async-start(bf16[64,1,72,128]{3,2,1,0:T(8,128)(2,1)} %forecast_second.3), calls=%async_computation.2 | async-start | bytes 2359296 | tf_op jit(solution)/shard_map/all_to_all | solution.py:377
  204.4 36.4 %all-to-all-start.4 = ((bf16[64,2,72,128]{3,2,1,0:T(8,128)(2,1)}), bf16[64,2,72,128]{3,2,1,0:T(8,128)(2,1)S(1)}, u32[]{:S(2)}, u32[]{:S(2)}) async-start(bf16[64,2,72,128]{3,2,1,0:T(8,128)(2,1)} %get-tuple-element.8), calls=%async_computation.4 | async-start | bytes 4718592 | tf_op jit(solution)/shard_map/all_to_all | solution.py:377
  240.8 1.4 copy-start.1

commit v2 on v0

v2 whole, which is shorter than its diff:
```python
import jax
import jax.numpy as jnp
from jax import lax
from jax.experimental import pallas as pl
from jax.experimental.pallas import tpu as pltpu
from jax.sharding import PartitionSpec as P

EDGE = 8
NS_ITERS = 12
CELLS = 64
LANES = 128
FIELDS = 69
PADDED = 72
LATENT = 512
LON = 384
TILES = 3
ROWS = 64
MEMBERS = 64
OBS = 128
PATCHES = 6
GROUP = 16
BLOCK = 256
DEPTH = 2
VMEM = 56 * 1024 * 1024
GELU_A = 0.7978845608028654
GELU_B = 0.044715 * 0.7978845608028654
VALUES = MEMBERS * 128 * LON

IN_VMEM = pl.BlockSpec(memory_space=pltpu.VMEM)
IN_SMEM = pl.BlockSpec(memory_space=pltpu.SMEM)


def params():
    return pltpu.CompilerParams(vmem_limit_bytes=VMEM)


def cost(flops, size, tanhs=0):
    return pl.CostEstimate(flops=flops, bytes_accessed=size, transcendentals=tanhs)


def gelu_twice(linear):
    inner = linear * (GELU_A + GELU_B * (linear * linear))
    return (linear + linear * jnp.tanh(inner)).astype(jnp.bfloat16)


def mlp(smooth, w_in, w_out):
    count = smooth.shape[1] // BLOCK
    linear, changes = {}, []
    for n in range(count + DEPTH):
        if n < count:
            cols = slice(n * BLOCK, (n + 1) * BLOCK)
            linear[n] = jnp.dot(w_in, smooth[:, cols], preferred_element_type=jnp.float32)
        if n >= DEPTH:
            hidden = gelu_twice(linear.pop(n - DEPTH))
            changes.append(jnp.dot(w_out, hidden, preferred_element_type=jnp.float32))
    return jnp.concatenate(changes, axis=1)


def swap_groups(rows):
    lane = lax.broadcasted_iota(jnp.int32, rows[0].shape, 1)
    for bit in (4, 2, 1):
        shift = bit * GROUP
        high = (lane & shift) != 0
        new = list(rows)
        for a in range(8):
            if a & bit:
                continue
            first, second = rows[a], rows[a + bit]
            new[a] = jnp.where(high, pltpu.roll(second, shift, 1), first)
            new[a + bit] = jnp.where(high, second, pltpu.roll(first, LANES - shift, 1))
        rows = new
    return rows


def owner_of(r, tile, group):
    number = tile * 8 + group
    return r * 8 + number // 3, number % 3


def forecast_kernel(
    role_ref, x_ref, halo_ref, diff_ref, w_in_ref, b_in_ref, w_out_ref, out_ref, before, after
):
    f32, bf16 = jnp.float32, jnp.bfloat16
    role = role_ref[0]

    def turned(block):
        ones = jnp.ones((PADDED - FIELDS,) + block.shape[1:], bf16)
        return jnp.swapaxes(jnp.concatenate([block, ones], axis=0), 0, 1)

    zeros = jnp.zeros((8, PADDED, LON), bf16)
    before[0:8] = zeros
    before[72:80] = zeros
    before[pl.ds(jnp.where(role == 0, 72, 0), 8)] = turned(halo_ref[...])

    def load(step, carry):
        place = pl.multiple_of(step * 16, 16)
        before[pl.ds(8 + place, 16)] = turned(x_ref[:, pl.ds(place, 16), :])
        return carry

    lax.fori_loop(0, ROWS // 16, load, 0)

    diff = jnp.concatenate([diff_ref[...], jnp.zeros((1, LANES - FIELDS), f32)], axis=1)
    diff = jnp.broadcast_to(diff, (LANES, LANES)).T[:PADDED]
    diff = jnp.concatenate([diff] * TILES, axis=1)
    bias = b_in_ref[...]
    high = bias.astype(bf16)
    middle = (bias - high.astype(f32)).astype(bf16)
    low = (bias - high.astype(f32) - middle.astype(f32)).astype(bf16)
    w_in = jnp.concatenate([w_in_ref[...], high, middle, low], axis=0).astype(f32)
    w_in = jnp.concatenate([w_in, jnp.zeros((LANES - PADDED, LATENT), f32)], axis=0).T[:, :PADDED].astype(bf16)
    w_out = jnp.concatenate(
        [w_out_ref[...] * bf16(0.5), jnp.zeros((PADDED - FIELDS, LATENT), bf16)], axis=0
    )

    def advance(ref, place, count):
        centre, smooth = [], []
        rows = [ref[place + k - 1].astype(f32) for k in range(count + 2)]
        for k in range(count):
            c = rows[k + 1]
            around = rows[k] + rows[k + 2] + pltpu.roll(c, 1, 1) + pltpu.roll(c, LON - 1, 1)
            smooth.append((c + diff * (around - 4.0 * c)).astype(bf16))
            centre.append(c)
        change = mlp(jnp.concatenate(smooth, axis=1), w_in, w_out)
        return [centre[k] + change[:, k * LON : (k + 1) * LON] for k in range(count)]

    def first(step, carry):
        for k, row in enumerate(advance(before, step * 6 + 7, 6)):
            after[step * 6 + k] = row.astype(bf16)
        return carry

    lax.fori_loop(0, (ROWS + 2) // 6, first, 0)

    @pl.when(role == 0)
    def _():
        after[0] = jnp.zeros((PADDED, LON), bf16)

    @pl.when(role == 1)
    def _():
        after[ROWS + 1] = jnp.zeros((PADDED, LON), bf16)

    def second(r, carry):
        rows = advance(after, r * 8 + 1, 8)
        for tile in range(TILES):
            pieces = [row[:, tile * LANES : (tile + 1) * LANES] for row in rows]
            for group, message in enumerate(swap_groups(pieces)):
                owner, slot = owner_of(r, tile, group)
                out_ref[owner, slot] = message.astype(bf16)
        return carry

    lax.fori_loop(0, ROWS // 8, second, 0)


def split(a):
    high = a.astype(jnp.bfloat16)
    return high, (a - high.astype(jnp.float32)).astype(jnp.bfloat16)


def dot3(a, b, contract=((1,), (0,))):
    (a_high, a_low), (b_high, b_low) = split(a), split(b)
    left = jnp.concatenate([a_high, a_low, a_high], axis=1)
    right = jnp.concatenate([b_high, b_high, b_low], axis=contract[1][0])
    return lax.dot_general(left, right, (contract, ((), ())), preferred_element_type=jnp.float32)


def mix_kernel(dev_ref, idx_ref, value_ref, weight_ref, g_ref, out_ref, turn, back):
    f32, bf16 = jnp.float32, jnp.bfloat16
    dev = dev_ref[0]
    eye = jnp.where(
        lax.broadcasted_iota(jnp.int32, (MEMBERS, MEMBERS), 0)
        == lax.broadcasted_iota(jnp.int32, (MEMBERS, MEMBERS), 1),
        1.0,
        0.0,
    )
    odd = jnp.where(lax.broadcasted_iota(jnp.int32, (1, 2 * OBS), 1) >= OBS, EDGE, 0)
    spreads, weights, innovations = [], [], []
    for k in range(TILES):

        def load(step, carry):
            m = pl.multiple_of(step * 16, 16)
            turn[k, :, pl.ds(m, 16), :] = jnp.swapaxes(g_ref[pl.ds(m, 16), k], 0, 1)
            return carry

        lax.fori_loop(0, MEMBERS // 16, load, 0)
        idx = jnp.concatenate(
            [idx_ref[pl.ds(dev * PATCHES + 2 * k + e, 1), :] for e in range(2)], axis=1
        )
        cell = idx & (CELLS - 1)
        lane = (cell >> 3) * GROUP + odd + (cell & 7)
        field = idx >> 6
        hot = jnp.where(lax.broadcasted_iota(jnp.int32, (LANES, 2 * OBS), 0) == lane, 1.0, 0.0)
        hot = hot.astype(bf16)

        def pick(step, total):
            block = turn[k, pl.ds(step * 8, 8)].reshape(8 * MEMBERS, LANES)
            values = jnp.dot(block, hot, preferred_element_type=f32)
            for f in range(8):
                here = field == step * 8 + f
                total = total + jnp.where(here, values[f * MEMBERS : (f + 1) * MEMBERS], 0.0)
            return total

        observed = lax.fori_loop(0, PADDED // 8, pick, jnp.zeros((MEMBERS, 2 * OBS), f32))
        for e in range(2):
            mine = observed[:, e * OBS : (e + 1) * OBS]
            obs_mean = jnp.sum(mine, axis=0, keepdims=True) * (1.0 / MEMBERS)
            row = slice(2 * k + e, 2 * k + e + 1)
            spreads.append(mine - obs_mean)
            innovations.append(value_ref[row, :] - obs_mean)
            weights.append(weight_ref[row, :])

    weighted = [s * w for s, w in zip(spreads, weights)]
    precisions = [dot3(w, s, ((1,), (1,))) + (MEMBERS - 1.0) * eye for w, s in zip(weighted, spreads)]
    pulled = [
        jnp.broadcast_to(jnp.sum(w * i, axis=1, keepdims=True), (MEMBERS, MEMBERS))
        for w, i in zip(weighted, innovations)
    ]
    scales = [
        MEMBERS * jnp.sum(jnp.sum(p * eye, axis=0, keepdims=True), axis=1, keepdims=True)
        for p in precisions
    ]
    iterates = [p / s for p, s in zip(precisions, scales)]

    def newton(step, carry):
        iterates, roots = carry
        factors = [0.5 * (3.0 * eye - dot3(r, i)) for r, i in zip(roots, iterates)]
        new_iterates = [dot3(i, f) for i, f in zip(iterates, factors)]
        return new_iterates, [dot3(f, r) for f, r in zip(factors, roots)]

    _, roots = lax.fori_loop(0, NS_ITERS, newton, (iterates, [eye] * PATCHES))
    shifts = [dot3(r, p) for r, p in zip(roots, pulled)]
    shifts = [dot3(r, p) for r, p in zip(roots, shifts)]
    mixes = []
    for root, shift, scale in zip(roots, shifts, scales):
        combined = jnp.sqrt((MEMBERS - 1.0) / scale) * root + shift / scale
        rest = (1.0 - jnp.sum(combined, axis=0, keepdims=True)) * (1.0 / MEMBERS)
        mixes.append((combined + rest).T)

    even = (lax.broadcasted_iota(jnp.int32, (MEMBERS, BLOCK), 1) & EDGE) == 0
    total = jnp.zeros((1, 1), f32)
    for k in range(TILES):
        mix = jnp.concatenate(mixes[2 * k : 2 * k + 2], axis=0).astype(bf16)

        def mixed(x):
            both = jnp.dot(mix, x, preferred_element_type=f32)
            return jnp.where(even[:, : x.shape[1]], both[:MEMBERS], both[MEMBERS:])

        def apply(step, carry):
            for pair in range(4):
                f = step * 8 + 2 * pair
                new = mixed(jnp.concatenate([turn[k, f], turn[k, f + 1]], axis=1)).astype(bf16)
                back[k, f] = new[:, :LANES]
                back[k, f + 1] = new[:, LANES:]
            return carry

        lax.fori_loop(0, PADDED // 8, apply, 0)
        first = mixed(turn[k, 0])
        total = total + jnp.sum(jnp.sum(first, axis=0, keepdims=True), axis=1, keepdims=True)

    high = total.astype(bf16)
    middle = (total - high.astype(f32)).astype(bf16)
    low = (total - high.astype(f32) - middle.astype(f32)).astype(bf16)
    for row, part in enumerate((high, middle, low)):
        back[TILES - 1, FIELDS + row] = jnp.broadcast_to(part, (MEMBERS, LANES))
    for k in range(TILES):

        def give(step, carry):
            m = pl.multiple_of(step * 16, 16)
            out_ref[pl.ds(m, 16), k] = jnp.swapaxes(back[k, :, pl.ds(m, 16), :], 0, 1)
            return carry

        lax.fori_loop(0, MEMBERS // 16, give, 0)


def last_kernel(offset_ref, back_ref, out_ref):
    offset = offset_ref[0]
    first = lax.broadcasted_iota(jnp.int32, (FIELDS, 1, LANES), 0) == 0
    add = jnp.where(first, offset, 0.0)

    def block(step, carry):
        for tile in range(TILES):
            rows = []
            for half in range(2):
                pieces = []
                for group in range(8):
                    owner, slot = owner_of(step * 2 + half, tile, group)
                    pieces.append(back_ref[owner, slot].astype(jnp.float32))
                rows += [row.astype(jnp.bfloat16) for row in swap_groups(pieces)]
            values = jnp.swapaxes(jnp.stack(rows), 0, 1)[:FIELDS].astype(jnp.float32) + add
            place = pl.ds(pl.multiple_of(step * 16, 16), 16)
            out_ref[:, place, tile * LANES : (tile + 1) * LANES] = values.astype(jnp.bfloat16)
        return carry

    lax.fori_loop(0, ROWS // 16, block, 0)


MESSAGES = jax.ShapeDtypeStruct((MEMBERS, TILES, PADDED, LANES), jnp.bfloat16)


def forecast(role, x, halo, diff, w_in, b_in, w_out):
    cells = 2 * ROWS * LON
    return pl.pallas_call(
        forecast_kernel,
        out_shape=MESSAGES,
        in_specs=[IN_SMEM] + [IN_VMEM] * 6,
        out_specs=IN_VMEM,
        scratch_shapes=[
            pltpu.VMEM((ROWS + 16, PADDED, LON), jnp.bfloat16),
            pltpu.VMEM((ROWS + 2, PADDED, LON), jnp.bfloat16),
        ],
        compiler_params=params(),
        cost_estimate=cost(cells * LATENT * 256 * 4, 7 << 20, cells * LATENT),
        name="forecast",
    )(role, x, halo, diff, w_in, b_in, w_out)


def mix(dev, idx, value, weight, g):
    return pl.pallas_call(
        mix_kernel,
        out_shape=MESSAGES,
        in_specs=[IN_SMEM] + [IN_VMEM] * 4,
        out_specs=IN_VMEM,
        scratch_shapes=[
            pltpu.VMEM((TILES, PADDED, MEMBERS, LANES), jnp.bfloat16),
            pltpu.VMEM((TILES, PADDED, MEMBERS, LANES), jnp.bfloat16),
        ],
        compiler_params=params(),
        cost_estimate=cost(8 << 30, 7 << 20),
        name="mix",
    )(dev, idx, value, weight, g)


def put_back(offset, back):
    return pl.pallas_call(
        last_kernel,
        out_shape=jax.ShapeDtypeStruct((FIELDS, ROWS, LON), jnp.bfloat16),
        in_specs=[IN_SMEM, IN_VMEM],
        out_specs=IN_VMEM,
        compiler_params=params(),
        cost_estimate=cost(1 << 20, 7 << 20),
        name="put_back",
    )(offset, back)


def exchange(messages):
    return lax.all_to_all(messages, "dev", split_axis=0, concat_axis=0, tiled=True)


def body(
    initial_realizations, diffusivity, w_in, b_in, w_out, obs_index, obs_value, obs_weight, climate
):
    role = lax.axis_index("role")
    dev = lax.axis_index("dev")
    x = initial_realizations.reshape(FIELDS, ROWS, LON)
    edge = lax.dynamic_slice_in_dim(x, jnp.where(role == 0, ROWS - 8, 0), 8, 1)
    halo = lax.ppermute(edge, "role", [(0, 1), (1, 0)])
    sent = forecast(
        role.reshape(1), x, halo, diffusivity.reshape(1, FIELDS), w_in.T, b_in.reshape(1, LATENT), w_out
    )
    got = exchange(sent)
    mixed = mix(dev.reshape(1), obs_index, obs_value, obs_weight, got)
    back = exchange(mixed)
    total = jnp.sum(back[:, TILES - 1, FIELDS:, 0].astype(jnp.float32))
    total = lax.psum(total, "role")
    offset = climate - total / VALUES
    return put_back(offset, back)[None]


def solution(mesh):
    in_specs = (
        P("dev", None, "role", None),
        P(),
        P(),
        P(),
        P(),
        P("role", None),
        P(("role", "dev"), None),
        P(("role", "dev"), None),
        P(),
    )
    out_specs = P("dev", None, "role", None)
    return jax.shard_map(body, mesh=mesh, in_specs=in_specs, out_specs=out_specs, check_vma=False)
```

time: 708 us -> 211 us (0.30)
  local copies, waits for them, and re-layouts: 299 us -> 3.56 us
  matrix products: 112 us -> 0 us
  other arithmetic: 95.7 us -> 0.79 us
  Pallas kernels: 0 us -> 87.1 us
  blocking collectives: 127 us -> 58 us
  starting transfers between devices: 21.5 us -> 11.6 us
    dot_general x58 -> x0, matrix products: 112 us -> none  [the longest x16 77.1 us: process_block(): jnp.einsum('fh,mhc->mfc', w_out, hidden, preferred_element_type=jnp.float32)]
    reshape x9 -> x0, local copies, waits for them, and re-layouts: 107 us -> none  [the longest x1 41.2 us: from_patches(): tile_partition.reshape(members_here, lat_rows // TILE_EDGE_POINTS, lon_ce...]
    transpose x4 -> x0, local copies, waits for them, and re-layouts: 90.9 us -> none  [the longest x1 53 us: from_patches(): shaped.transpose(0, 3, 1, 4, 2, 5)]
    pallas_call x0 -> x3, Pallas kernels: none -> 87.1 us  [the longest x1 51.3 us: forecast(): pl.pallas_call(forecast_kernel, out_shape=MESSAGES, in_specs=[IN_SMEM] +...]
    psum x1, blocking collectives: 64.7 us -> 3.11 us  [body(): total = lax.psum(total, 'role')]
    convert_element_type x6 -> x0, other arithmetic: 55.1 us -> none  [the longest x1 24.7 us: body(): values = gathered.astype(jnp.float32)]
    all_to_all x1 -> x0, local copies, waits for them, and re-layouts: 22.2 us -> none  [body(): lax.all_to_all(tile_partition, 'dev', split_axis=1, concat_axis=0, tiled=...]
    unnamed x1 -> x0, other arithmetic: 21.6 us -> none
  transfers between devices with their start and end apart: 5 -> 2, of which waited for: 2 -> 2; matrix products, arithmetic and copies ran while one was open for 2% -> 0% of each run, Pallas kernels for 0% -> 0%
where the time goes in v2:
time: 211 us; the launch traced here: 210 us
  Pallas kernels  87.1 us (41%)
  blocking collectives  58 us (27%)
  waiting for transfers between devices  47.3 us (22%)
  starting transfers between devices  11.6 us (5%)
  local copies, waits for them, and re-layouts  3.56 us (2%)
    all_to_all x1, blocking collectives, exchange(): lax.all_to_all(messages, 'dev', split_axis=0, concat_axis=0, tiled=True)  54.9 us
    pallas_call x1, Pallas kernels, forecast(): pl.pallas_call(forecast_kernel, out_shape=MESSAGES, in_specs=[IN_SMEM] +...  51.3 us
    all_to_all x1, waiting for transfers between devices, exchange(): lax.all_to_all(messages, 'dev', split_axis=0, concat_axis=0, tiled=True)  45.6 us
    pallas_call x1, Pallas kernels, mix(): pl.pallas_call(mix_kernel, out_shape=MESSAGES, in_specs=[IN_SMEM] + [IN_V...  26.2 us
    all_to_all x1, starting transfers between devices, exchange(): lax.all_to_all(messages, 'dev', split_axis=0, concat_axis=0, tiled=True)  11.5 us
    pallas_call x1, Pallas kernels, put_back(): pl.pallas_call(last_kernel, out_shape=jax.ShapeDtypeStruct((FIELDS, ROWS,...  9.59 us
  transfers between devices with their start and end apart: 2, of which 2 were waited for; matrix products, arithmetic and copies ran while one was open for 0% of the time, Pallas kernels for 0%

profile of v2, /device:TPU:0, one launch (start us, length us, event | category | flops | bytes accessed | tf_op | source)
XLA Modules:
  0.0 209.7 jit_solution(17670284476269093851)
XLA Ops:
  0.0 1.0 dynamic-slice_bitcast_fusion
  1.1 0.1 collective-permute-start
  1.1 1.8 collective-permute-done.halo_ref
  2.9 0.0 copy-start.2
  2.9 0.8 copy-done.2
  3.7 51.3 %forecast.1 = bf16[64,3,72,128]{3,2,1,0:T(8,128)(2,1)} custom-call(s32[1]{0:T(128)} %bitcast.1.role_ref, bf16[69,64,384]{2,1,0:T(8,128)(2,1)} %bitcast.10, bf16[69,8,384]{2,1,0:T(8,128)(2,1)} %copy-done.2, f32[1,69]{1,0:T(1,128)} %bitcast.13, bf16[69,512]{1,0:T(8,128)(2,1)} %bitcast.11, f32[1,512]{1,0:T(1,128)} %bitcast.12, bf16[69,512]{1,0:T(8,128)(2,1)} %w_out_ref.1), custom_call_target="tpu_custom_call" | custom-call | flops 25769803776 | bytes 7340032 | tf_op jit(solution)/shard_map/forecast/pallas_call | solution.py:300
  54.9 11.5 %all-to-all-start = ((bf16[64,3,72,128]{3,2,1,0:T(8,128)(2,1)}), bf16[64,3,72,128]{3,2,1,0:T(8,128)(2,1)S(1)}, u32[]{:S(2)}, u32[]{:S(2)}) async-start(bf16[64,3,72,128]{3,2,1,0:T(8,128)(2,1)} %forecast.1), calls=%async_computation | async-start | bytes 7077888 | tf_op jit(solution)/shard_map/all_to_all | solution.py:344
  66.4 45.6 %all-to-all-done.g_ref = bf16[64,3,72,128]{3,2,1,0:T(8,128)(2,1)S(1)} async-done(((bf16[64,3,72,128]{3,2,1,0:T(8,128)(2,1)}), bf16[64,3,72,128]{3,2,1,0:T(8,128)(2,1)S(1)}, u32[]{:S(2)}, u32[]{:S(2)}) %all-to-all-start) | async-done | bytes 3538976 | tf_op jit(solution)/shard_map/all_to_all | solution.py:344
  112.0 0.0 copy-start.1
  112.0 1.8 copy-done.1
  113.7 26.2 %mix.1 = bf16[64,3,72,128]{3,2,1,0:T(8,128)(2,1)} custom-call(s32[1]{0:T(128)} %bitcast.dev_ref, s32[384,128]{1,0:T(8,128)} %idx_ref.1, f32[6,128]{1,0:T(8,128)} %value_ref.1, f32[6,128]{1,0:T(8,128)} %weight_ref.1, bf16[64,3,72,128]{3,2,1,0:T(8,128)(2,1)} %copy-done.1), custom_call_target="tpu_custom_call" | custom-call | flops 8589934592 | bytes 7340032 | tf_op jit(solution)/shard_map/mix/pallas_call | solution.py:316
  140.0 54.9 %all_to_all.10.back_ref = bf16[64,3,72,128]{3,2,1,0:T(8,128)(2,1)S(1)} all-to-all(bf16[64,3,72,128]{3,2,1,0:T(8,128)(2,1)} %mix.1), channel_id=1, replica_groups=mesh['role'=2,'dev'=64] {'dev'}, dimensions={0} | all-to-all | bytes 7077888 | tf_op jit(solution)/shard_map/all_to_all | solution.py:344
  194.9 0.0 copy-start
  194.9 0.8 convert_reduce_fusion
  196.3 3.1 %psum.7 = f32[]{:T(128)} all-reduce(f32[]{:T(128)} %convert_reduce_fusion), channel_id=1, replica_groups=mesh['role'=2,'dev'=64] {'role'}, use_global_device_ids=true, to_apply=%region_1.2 | all-reduce | flops 1 | bytes 8 | tf_op jit(solution)/shard_map/psum | solution.py:362
  200.1 0.0 copy-done
  200.1 9.6 %put_back.1 = bf16[69,64,384]{2,1,0:T(8,128)(2,1)} custom-call(f32[1]{0:T(128)S(6)} %sub.7.offset_ref, bf16[64,3,72,128]{3,2,1,0:T(8,128)(2,1)} %copy-done), custom_call_target="tpu_custom_call" | custom-call | flops 1048576 | bytes 7340032 | tf_op jit(solution)/shard_map/put_back/pallas_call | solution.py:332
Async XLA Ops:
  1.1 1.8 collective-permute-start
  2.9 0.8 copy-start.2
  54.9 57.1 %all-to-all-start = ((bf16[64,3,72,128]{3,2,1,0:T(8,128)(2,1)}), bf16[64,3,72,128]{3,2,1,0:T(8,128)(2,1)S(1)}, u32[]{:S(2)}, u32[]{:S(2)}) async-start(bf16[64,3,72,128]{3,2,1,0:T(8,128)(2,1)} %forecast.1), calls=%async_computation | async-start | bytes 7077888 | tf_op jit(solution)/shard_map/all_to_all | solution.py:344
  112.0 1.8 copy-start.1
  194.9 5.2 %copy-start = (bf16[64,3,72,128]{3,2,1,0:T(8,128)(2,1)}, bf16[64,3,72,128]{3,2,1,0:T(8,128)(2,1)S(1)}, u32[]{:S(2)}) copy-start(bf16[64,3,72,128]{3,2,1,0:T(8,128)(2,1)S(1)} %all_to_all.10.back_ref) | copy-start | bytes 10616836

commit v3 on v2

v3 whole, which is shorter than its diff:
```python
import jax
import jax.numpy as jnp
from jax import lax
from jax.experimental import pallas as pl
from jax.experimental.pallas import tpu as pltpu
from jax.sharding import PartitionSpec as P

EDGE = 8
NS_ITERS = 12
CELLS = 64
LANES = 128
FIELDS = 69
PADDED = 72
LATENT = 512
LON = 384
TILES = 3
ROWS = 64
MEMBERS = 64
OBS = 128
PATCHES = 6
GROUP = 16
BLOCK = 256
DEPTH = 3
GELU_A = 0.7978845608028654
GELU_B = 0.044715 * 0.7978845608028654
VALUES = MEMBERS * 128 * LON

IN_VMEM = pl.BlockSpec(memory_space=pltpu.VMEM)
IN_HBM = pl.BlockSpec(memory_space=pltpu.HBM)
IN_SMEM = pl.BlockSpec(memory_space=pltpu.SMEM)


def params(mib):
    return pltpu.CompilerParams(vmem_limit_bytes=mib * 1024 * 1024)


def cost(flops, size, tanhs=0):
    return pl.CostEstimate(flops=flops, bytes_accessed=size, transcendentals=tanhs)


def gelu_twice(linear):
    linear = linear.astype(jnp.bfloat16)
    inner = linear * (jnp.bfloat16(GELU_A) + jnp.bfloat16(GELU_B) * (linear * linear))
    return linear + linear * jnp.tanh(inner)


def mlp(smooth, w_in, w_out):
    count = smooth.shape[1] // BLOCK
    linear, changes = {}, []
    for n in range(count + DEPTH):
        if n < count:
            cols = slice(n * BLOCK, (n + 1) * BLOCK)
            linear[n] = jnp.dot(w_in, smooth[:, cols], preferred_element_type=jnp.float32)
        if n >= DEPTH:
            hidden = gelu_twice(linear.pop(n - DEPTH))
            changes.append(jnp.dot(w_out, hidden, preferred_element_type=jnp.float32))
    return jnp.concatenate(changes, axis=1)


def swap_groups(rows):
    lane = lax.broadcasted_iota(jnp.int32, rows[0].shape, 1)
    rows = [pltpu.roll(row, a * GROUP, 1) if a else row for a, row in enumerate(rows)]
    rows = [rows[-p % 8] for p in range(8)]
    for bit in (1, 2, 4):
        move = (lane & (bit * GROUP)) != 0
        rows = [jnp.where(move, rows[(p - bit) % 8], rows[p]) for p in range(8)]
    return [pltpu.roll(row, LANES - p * GROUP, 1) if p else row for p, row in enumerate(rows)]


def owner_of(r, tile, group):
    number = tile * 8 + group
    return r * 8 + number // 3, number % 3


def forecast_kernel(
    role_ref, x_ref, halo_ref, diff_ref, w_in_ref, b_in_ref, w_out_ref, out_ref, own, before, after, messages,
    in_sems, out_sems,
):
    f32, bf16 = jnp.float32, jnp.bfloat16
    role = role_ref[0]

    def fetch(step):
        rows = pl.ds(step * 16, 16)
        return pltpu.make_async_copy(x_ref.at[:, rows, :], own.at[:, rows, :], in_sems.at[step])

    def send(r):
        owners = pl.ds(r * 8, 8)
        return pltpu.make_async_copy(messages.at[owners], out_ref.at[owners], out_sems.at[r])

    for step in range(ROWS // 16):
        fetch(step).start()

    def turned(block):
        ones = jnp.ones((PADDED - FIELDS,) + block.shape[1:], bf16)
        return jnp.swapaxes(jnp.concatenate([block, ones], axis=0), 0, 1)

    zeros = jnp.zeros((8, PADDED, LON), bf16)
    before[0:8] = zeros
    before[72:80] = zeros
    before[pl.ds(jnp.where(role == 0, 72, 0), 8)] = turned(halo_ref[...])

    for step in range(ROWS // 16):
        fetch(step).wait()
        before[8 + step * 16 : 24 + step * 16] = turned(own[:, step * 16 : (step + 1) * 16, :])

    diff = jnp.concatenate([diff_ref[...], jnp.zeros((1, LANES - FIELDS), f32)], axis=1)
    diff = jnp.broadcast_to(diff, (LANES, LANES)).T[:PADDED]
    diff = jnp.concatenate([diff] * TILES, axis=1)
    bias = b_in_ref[...]
    high = bias.astype(bf16)
    middle = (bias - high.astype(f32)).astype(bf16)
    low = (bias - high.astype(f32) - middle.astype(f32)).astype(bf16)
    w_in = jnp.concatenate([w_in_ref[...], high, middle, low], axis=0).astype(f32)
    w_in = jnp.concatenate([w_in, jnp.zeros((LANES - PADDED, LATENT), f32)], axis=0).T[:, :PADDED].astype(bf16)
    w_out = jnp.concatenate(
        [w_out_ref[...] * bf16(0.5), jnp.zeros((PADDED - FIELDS, LATENT), bf16)], axis=0
    )

    def advance(ref, place, count):
        centre, smooth = [], []
        packed = [ref[place + k - 1] for k in range(count + 2)]
        rows = [row.astype(f32) for row in packed]
        for k in range(count):
            c = rows[k + 1]
            around = rows[k] + rows[k + 2] + pltpu.roll(packed[k + 1], 1, 1).astype(f32) + pltpu.roll(packed[k + 1], LON - 1, 1).astype(f32)
            smooth.append((c + diff * (around - 4.0 * c)).astype(bf16))
            centre.append(c)
        change = mlp(jnp.concatenate(smooth, axis=1), w_in, w_out)
        return [centre[k] + change[:, k * LON : (k + 1) * LON] for k in range(count)]

    def first(step, carry):
        for k, row in enumerate(advance(before, step * 6 + 7, 6)):
            after[step * 6 + k] = row.astype(bf16)
        return carry

    lax.fori_loop(0, (ROWS + 2) // 6, first, 0)

    @pl.when(role == 0)
    def _():
        after[0] = jnp.zeros((PADDED, LON), bf16)

    @pl.when(role == 1)
    def _():
        after[ROWS + 1] = jnp.zeros((PADDED, LON), bf16)

    def second(r, carry):
        rows = advance(after, r * 8 + 1, 8)
        for tile in range(TILES):
            pieces = [row[:, tile * LANES : (tile + 1) * LANES].astype(bf16) for row in rows]
            for group, message in enumerate(swap_groups(pieces)):
                owner, slot = owner_of(r, tile, group)
                messages[owner, slot] = message
        send(r).start()
        return carry

    lax.fori_loop(0, ROWS // 8, second, 0)
    for r in range(ROWS // 8):
        send(r).wait()


def split(a):
    high = a.astype(jnp.bfloat16)
    return high, (a - high.astype(jnp.float32)).astype(jnp.bfloat16)


def stacked(a):
    low = lax.broadcasted_iota(jnp.int32, (MEMBERS, LANES), 1) < MEMBERS
    high, rest = split(a)
    high_turned, rest_turned = pltpu.roll(high, MEMBERS, 1), pltpu.roll(rest, MEMBERS, 1)
    first = jnp.concatenate([jnp.where(low, high, rest_turned), high[:, :MEMBERS]], axis=1)
    second = jnp.concatenate([jnp.where(low, high_turned, rest), high_turned[:, :MEMBERS]], axis=1)
    return jnp.concatenate([first, second], axis=0)


def pair_dot(lefts, right):
    low = lax.broadcasted_iota(jnp.int32, (MEMBERS, LANES), 1) < MEMBERS
    high, rest = split(right)
    right = jnp.concatenate([high, high, rest], axis=0)
    left = jnp.concatenate([stacked(a) for a in lefts], axis=0)
    both = jnp.dot(left, right, preferred_element_type=jnp.float32)
    return [
        jnp.where(low, both[n * LANES : n * LANES + MEMBERS], both[n * LANES + MEMBERS : (n + 1) * LANES])
        for n in range(len(lefts))
    ]


def wide_dot(a, b):
    (a_high, a_low), (b_high, b_low) = split(a), split(b)
    left = jnp.concatenate([a_high, a_low, a_high], axis=1)
    right = jnp.concatenate([b_high, b_high, b_low], axis=1)
    return lax.dot_general(left, right, (((1,), (1,)), ((), ())), preferred_element_type=jnp.float32)


def mix_kernel(idx_ref, value_ref, weight_ref, g_ref, out_ref, turn, back, messages, sems):
    f32, bf16 = jnp.float32, jnp.bfloat16
    lane = lax.broadcasted_iota(jnp.int32, (MEMBERS, LANES), 1)
    low = lane < MEMBERS
    eye = jnp.where(
        (lane & (MEMBERS - 1)) == lax.broadcasted_iota(jnp.int32, (MEMBERS, LANES), 0), 1.0, 0.0
    )
    odd = jnp.where(lax.broadcasted_iota(jnp.int32, (1, 2 * OBS), 1) >= OBS, EDGE, 0)

    def halves(a):
        first = jnp.sum(jnp.where(low[: a.shape[0]], a, 0.0), axis=1, keepdims=True)
        second = jnp.sum(jnp.where(low[: a.shape[0]], 0.0, a), axis=1, keepdims=True)
        return jnp.where(low[: a.shape[0]], first, second)

    def send(k):
        return pltpu.make_async_copy(messages.at[:, k], out_ref.at[:, k], sems.at[k])

    precisions, pulled = [], []
    for k in range(TILES):

        def load(step, carry):
            m = pl.multiple_of(step * 16, 16)
            turn[k, :, pl.ds(m, 16), :] = jnp.swapaxes(g_ref[pl.ds(m, 16), k], 0, 1)
            return carry

        lax.fori_loop(0, MEMBERS // 16, load, 0, unroll=2)
    for k in range(TILES):
        idx = jnp.concatenate(
            [idx_ref[2 * k + e : 2 * k + e + 1, :] for e in range(2)], axis=1
        )
        cell = idx & (CELLS - 1)
        place = (cell >> 3) * GROUP + odd + (cell & 7)
        field = jnp.broadcast_to(idx >> 6, (MEMBERS, 2 * OBS))
        hot = jnp.where(lax.broadcasted_iota(jnp.int32, (LANES, 2 * OBS), 0) == place, 1.0, 0.0)
        hot = hot.astype(bf16)

        def pick(step, total):
            for part in range(3):
                start = step * 24 + part * 8
                block = turn[k, pl.ds(start, 8)].reshape(8 * MEMBERS, LANES)
                values = jnp.dot(block, hot, preferred_element_type=f32)
                for f in range(8):
                    here = field == start + f
                    total = jnp.where(here, values[f * MEMBERS : (f + 1) * MEMBERS], total)
            return total

        observed = lax.fori_loop(0, PADDED // 24, pick, jnp.zeros((MEMBERS, 2 * OBS), f32))
        sides, pulls = [], []
        for e in range(2):
            mine = observed[:, e * OBS : (e + 1) * OBS]
            row = slice(2 * k + e, 2 * k + e + 1)
            obs_mean = jnp.sum(mine, axis=0, keepdims=True) * (1.0 / MEMBERS)
            spread = mine - obs_mean
            weighted = spread * weight_ref[row, :]
            sides.append(wide_dot(weighted, spread))
            pulls.append(jnp.sum(weighted * (value_ref[row, :] - obs_mean), axis=1, keepdims=True))
        precisions.append(jnp.concatenate(sides, axis=1) + (MEMBERS - 1.0) * eye)
        pulled.append(jnp.where(low, pulls[0], pulls[1]))

    scales = [MEMBERS * halves(jnp.sum(p * eye, axis=0, keepdims=True)) for p in precisions]
    iterates = [p / s for p, s in zip(precisions, scales)]

    def newton(step, carry):
        iterates, roots = carry
        products = [pair_dot([r], i)[0] for r, i in zip(roots, iterates)]
        factors = [0.5 * (3.0 * eye - p) for p in products]
        new = [pair_dot([i, r], f) for i, r, f in zip(iterates, roots, factors)]
        return [n[0] for n in new], [n[1] for n in new]

    _, roots = lax.fori_loop(0, NS_ITERS, newton, (iterates, [eye] * TILES))
    shifts = [pair_dot([r], p)[0] for r, p in zip(roots, pulled)]
    shifts = [pair_dot([r], p)[0] for r, p in zip(roots, shifts)]
    even = jnp.where((lax.broadcasted_iota(jnp.int32, (MEMBERS, BLOCK), 1) & EDGE) == 0, 1.0, 0.0)
    even = even.astype(bf16)
    uneven = bf16(1.0) - even
    mixes = []
    for root, shift, scale in zip(roots, shifts, scales):
        combined = jnp.sqrt((MEMBERS - 1.0) / scale) * root + shift / scale
        rest = (1.0 - jnp.sum(combined, axis=0, keepdims=True)) * (1.0 / MEMBERS)
        across = (combined + rest).T
        mixes.append(jnp.concatenate([across[:MEMBERS], across[MEMBERS:]], axis=1).astype(bf16))

    def mixed(k, f):
        x = jnp.concatenate([turn[k, f], turn[k, f + 1]], axis=1)
        x = jnp.concatenate([x * even, x * uneven], axis=0)
        return jnp.dot(mixes[k], x, preferred_element_type=f32)

    total = jnp.zeros((1, 1), f32)
    for k in range(TILES):

        def apply(step, carry):
            for pair in range(12):
                f = step * 24 + 2 * pair
                new = mixed(k, f).astype(bf16)
                back[k, f] = new[:, :LANES]
                back[k, f + 1] = new[:, LANES:]
            return carry

        lax.fori_loop(0, PADDED // 24, apply, 0)
        first = mixed(k, 0)[:, :LANES]
        total = total + jnp.sum(jnp.sum(first, axis=0, keepdims=True), axis=1, keepdims=True)

    high = total.astype(bf16)
    middle = (total - high.astype(f32)).astype(bf16)
    low_part = (total - high.astype(f32) - middle.astype(f32)).astype(bf16)
    for row, part in enumerate((high, middle, low_part)):
        back[TILES - 1, FIELDS + row] = jnp.broadcast_to(part, (MEMBERS, LANES))
    for k in range(TILES):

        def give(step, carry):
            m = pl.multiple_of(step * 16, 16)
            messages[pl.ds(m, 16), k] = jnp.swapaxes(back[k, :, pl.ds(m, 16), :], 0, 1)
            return carry

        lax.fori_loop(0, MEMBERS // 16, give, 0, unroll=2)
        send(k).start()
    for k in range(TILES):
        send(k).wait()


def last_kernel(back_ref, out_ref, grid, sems):
    def send(step):
        rows = pl.ds(pl.multiple_of(step * 16, 16), 16)
        return pltpu.make_async_copy(grid.at[:, rows, :], out_ref.at[:, rows, :], sems.at[step])

    def block(step, carry):
        for tile in range(TILES):
            rows = []
            for half in range(2):
                pieces = []
                for group in range(8):
                    owner, slot = owner_of(step * 2 + half, tile, group)
                    pieces.append(back_ref[owner, slot])
                rows += swap_groups(pieces)
            values = jnp.swapaxes(jnp.stack(rows), 0, 1)[:FIELDS]
            place = pl.ds(pl.multiple_of(step * 16, 16), 16)
            grid[:, place, tile * LANES : (tile + 1) * LANES] = values
        send(step).start()
        return carry

    lax.fori_loop(0, ROWS // 16, block, 0)
    for step in range(ROWS // 16):
        send(step).wait()


MESSAGES = jax.ShapeDtypeStruct((MEMBERS, TILES, PADDED, LANES), jnp.bfloat16)


def forecast(role, x, halo, diff, w_in, b_in, w_out):
    cells = 2 * ROWS * LON
    return pl.pallas_call(
        forecast_kernel,
        out_shape=MESSAGES,
        in_specs=[IN_SMEM, IN_HBM] + [IN_VMEM] * 5,
        out_specs=IN_HBM,
        scratch_shapes=[
            pltpu.VMEM((FIELDS, ROWS, LON), jnp.bfloat16),
            pltpu.VMEM((ROWS + 16, PADDED, LON), jnp.bfloat16),
            pltpu.VMEM((ROWS + 2, PADDED, LON), jnp.bfloat16),
            pltpu.VMEM(MESSAGES.shape, jnp.bfloat16),
            pltpu.SemaphoreType.DMA((ROWS // 16,)),
            pltpu.SemaphoreType.DMA((ROWS // 8,)),
        ],
        compiler_params=params(56),
        cost_estimate=cost(cells * LATENT * 256 * 4, 7 << 20, cells * LATENT),
        name="forecast",
    )(role, x, halo, diff, w_in, b_in, w_out)


def mix(idx, value, weight, g):
    return pl.pallas_call(
        mix_kernel,
        out_shape=MESSAGES,
        in_specs=[IN_VMEM] * 4,
        out_specs=IN_HBM,
        scratch_shapes=[
            pltpu.VMEM((TILES, PADDED, MEMBERS, LANES), jnp.bfloat16),
            pltpu.VMEM((TILES, PADDED, MEMBERS, LANES), jnp.bfloat16),
            pltpu.VMEM(MESSAGES.shape, jnp.bfloat16),
            pltpu.SemaphoreType.DMA((TILES,)),
        ],
        compiler_params=params(53),
        cost_estimate=cost(8 << 30, 7 << 20),
        name="mix",
    )(idx, value, weight, g)


def put_back(back):
    return pl.pallas_call(
        last_kernel,
        out_shape=jax.ShapeDtypeStruct((FIELDS, ROWS, LON), jnp.bfloat16),
        in_specs=[IN_VMEM],
        out_specs=IN_HBM,
        scratch_shapes=[
            pltpu.VMEM((FIELDS, ROWS, LON), jnp.bfloat16),
            pltpu.SemaphoreType.DMA((ROWS // 16,)),
        ],
        compiler_params=params(50),
        cost_estimate=cost(1 << 20, 7 << 20),
        name="put_back",
    )(back)


def nudge_kernel(total_ref, other_ref, climate_ref, field_ref, out_ref):
    offset = climate_ref[0] - (total_ref[0] + other_ref[0]) / VALUES
    out_ref[...] = (field_ref[...].astype(jnp.float32) + offset).astype(jnp.bfloat16)


def nudge(total, other, climate, placed):
    field = pl.BlockSpec((1, ROWS, LON), lambda i: (0, 0, 0))
    return pl.pallas_call(
        nudge_kernel,
        out_shape=jax.ShapeDtypeStruct(placed.shape, placed.dtype),
        grid=(1,),
        in_specs=[IN_SMEM, IN_SMEM, IN_SMEM, field],
        out_specs=field,
        input_output_aliases={3: 0},
        cost_estimate=cost(1 << 16, 1 << 17),
        name="nudge",
    )(total, other, climate, placed)


def exchange(messages):
    return lax.all_to_all(messages, "dev", split_axis=0, concat_axis=0, tiled=True)


def body(
    initial_realizations, diffusivity, w_in, b_in, w_out, obs_index, obs_value, obs_weight, climate
):
    role = lax.axis_index("role")
    dev = lax.axis_index("dev")
    x = initial_realizations.reshape(FIELDS, ROWS, LON)
    edge = lax.dynamic_slice_in_dim(x, jnp.where(role == 0, ROWS - 8, 0), 8, 1)
    halo = lax.ppermute(edge, "role", [(0, 1), (1, 0)])
    sent = forecast(
        role.reshape(1), x, halo, diffusivity.reshape(1, FIELDS), w_in.T, b_in.reshape(1, LATENT), w_out
    )
    got = exchange(sent)
    index = lax.dynamic_slice_in_dim(obs_index, dev * PATCHES, PATCHES, 0)
    mixed = mix(index, obs_value, obs_weight, got)
    back = exchange(mixed)
    total = jnp.sum(back[:, TILES - 1, FIELDS:, 0].astype(jnp.float32)).reshape(1)
    other = lax.ppermute(total, "role", [(0, 1), (1, 0)])
    return nudge(total, other, climate, put_back(back))[None]


def solution(mesh):
    in_specs = (
        P("dev", None, "role", None),
        P(),
        P(),
        P(),
        P(),
        P("role", None),
        P(("role", "dev"), None),
        P(("role", "dev"), None),
        P(),
    )
    out_specs = P("dev", None, "role", None)
    return jax.shard_map(body, mesh=mesh, in_specs=in_specs, out_specs=out_specs, check_vma=False)
```

time: 211 us -> 181 us (0.86)
  blocking collectives: 58 us -> 0 us
  waiting for transfers between devices: 47.3 us -> 89.1 us
  Pallas kernels: 87.1 us -> 62.7 us
  starting transfers between devices: 11.6 us -> 22.6 us
    all_to_all x1 -> x0, blocking collectives: 54.9 us -> none  [exchange(): lax.all_to_all(messages, 'dev', split_axis=0, concat_axis=0, tiled=True)]
    all_to_all x1 -> x2, waiting for transfers between devices: 45.6 us -> 87.4 us  [exchange(): lax.all_to_all(messages, 'dev', split_axis=0, concat_axis=0, tiled=True)]
    pallas_call x2 -> x3, Pallas kernels: 77.5 us -> 55.7 us  [the longest x1 33.6 us: forecast(): pl.pallas_call(forecast_kernel, out_shape=MESSAGES, in_specs=[IN_SMEM, IN...]
    all_to_all x1 -> x2, starting transfers between devices: 11.5 us -> 22.5 us  [exchange(): lax.all_to_all(messages, 'dev', split_axis=0, concat_axis=0, tiled=True)]
    psum x1 -> x0, blocking collectives: 3.11 us -> none  [body(): total = lax.psum(total, 'role')]
    pallas_call x1, Pallas kernels: 9.59 us -> 7.05 us  [put_back(): pl.pallas_call(last_kernel, out_shape=jax.ShapeDtypeStruct((FIELDS, ROWS,...]
  transfers between devices with their start and end apart: 2 -> 4, of which waited for: 2 -> 3; matrix products, arithmetic and copies ran while one was open for 0% -> 0% of each run, Pallas kernels for 0% -> 4%
where the time goes in v3:
time: 181 us; the launch traced here: 179 us
  waiting for transfers between devices  89.1 us (49%)
  Pallas kernels  62.7 us (35%)
  starting transfers between devices  22.6 us (12%)
  local copies, waits for them, and re-layouts  1.87 us (1%)
    all_to_all x2, waiting for transfers between devices, exchange(): lax.all_to_all(messages, 'dev', split_axis=0, concat_axis=0, tiled=True)  87.4 us
    pallas_call x1, Pallas kernels, forecast(): pl.pallas_call(forecast_kernel, out_shape=MESSAGES, in_specs=[IN_SMEM, IN...  33.6 us
    all_to_all x2, starting transfers between devices, exchange(): lax.all_to_all(messages, 'dev', split_axis=0, concat_axis=0, tiled=True)  22.5 us
    pallas_call x1, Pallas kernels, mix(): pl.pallas_call(mix_kernel, out_shape=MESSAGES, in_specs=[IN_VMEM] * 4, ou...  19.4 us
    pallas_call x1, Pallas kernels, put_back(): pl.pallas_call(last_kernel, out_shape=jax.ShapeDtypeStruct((FIELDS, ROWS,...  7.05 us
  transfers between devices with their start and end apart: 4, of which 3 were waited for; matrix products, arithmetic and copies ran while one was open for 0% of the time, Pallas kernels for 4%

profile of v3, /device:TPU:0, one launch (start us, length us, event | category | flops | bytes accessed | tf_op | source)
XLA Modules:
  0.0 178.7 jit_solution(10086083712295553371)
XLA Ops:
  0.0 0.0 copy-start
  0.0 1.1 dynamic-slice_bitcast_fusion
  1.1 0.1 collective-permute-start
  1.2 1.8 collective-permute-done.halo_ref
  2.9 0.0 copy-start.3
  2.9 0.8 copy-done.3
  3.7 33.6 %forecast.1 = bf16[64,3,72,128]{3,2,1,0:T(8,128)(2,1)} custom-call(s32[1]{0:T(128)} %bitcast.role_ref, bf16[69,64,384]{2,1,0:T(8,128)(2,1)} %bitcast.9, bf16[69,8,384]{2,1,0:T(8,128)(2,1)} %copy-done.3, f32[1,69]{1,0:T(1,128)} %bitcast.12, bf16[69,512]{1,0:T(8,128)(2,1)} %bitcast.10, f32[1,512]{1,0:T(1,128)} %bitcast.11, bf16[69,512]{1,0:T(8,128)(2,1)} %w_out_ref.1), custom_call_target="tpu_custom_call" | custom-call | flops 25769803776 | bytes 7340032 | tf_op jit(solution)/shard_map/forecast/pallas_call | solution.py:344
  37.3 0.0 copy-start.1
  37.3 0.0 copy-start.2
  37.3 11.7 %all-to-all-start = ((bf16[64,3,72,128]{3,2,1,0:T(8,128)(2,1)}), bf16[64,3,72,128]{3,2,1,0:T(8,128)(2,1)}, u32[]{:S(2)}, u32[]{:S(2)}) async-start(bf16[64,3,72,128]{3,2,1,0:T(8,128)(2,1)} %forecast.1), calls=%async_computation | async-start | bytes 7077888 | tf_op jit(solution)/shard_map/all_to_all | solution.py:417
  49.1 0.0 copy-done
  49.1 45.3 %all-to-all-done.g_ref = bf16[64,3,72,128]{3,2,1,0:T(8,128)(2,1)} async-done(((bf16[64,3,72,128]{3,2,1,0:T(8,128)(2,1)}), bf16[64,3,72,128]{3,2,1,0:T(8,128)(2,1)}, u32[]{:S(2)}, u32[]{:S(2)}) %all-to-all-start) | async-done | bytes 3538976 | tf_op jit(solution)/shard_map/all_to_all | solution.py:417
  94.4 0.0 copy-done.1
  94.4 0.0 copy-done.2
  94.4 19.4 %mix.1 = bf16[64,3,72,128]{3,2,1,0:T(8,128)(2,1)} custom-call(s32[6,128]{1,0:T(8,128)S(1)} %constant_dynamic-slice_fusion.idx_ref, f32[6,128]{1,0:T(8,128)S(1)} %copy-done.1, f32[6,128]{1,0:T(8,128)S(1)} %copy-done.2, bf16[64,3,72,128]{3,2,1,0:T(8,128)(2,1)} %all-to-all-done.g_ref), custom_call_target="tpu_custom_call" | custom-call | flops 8589934592 | bytes 7340032 | tf_op jit(solution)/shard_map/mix/pallas_call | solution.py:364
  113.9 10.8 %all-to-all-start.1 = ((bf16[64,3,72,128]{3,2,1,0:T(8,128)(2,1)}), bf16[64,3,72,128]{3,2,1,0:T(8,128)(2,1)}, u32[]{:S(2)}, u32[]{:S(2)}) async-start(bf16[64,3,72,128]{3,2,1,0:T(8,128)(2,1)} %mix.1), calls=%async_computation.1 | async-start | bytes 7077888 | tf_op jit(solution)/shard_map/all_to_all | solution.py:417
  125.3 42.0 %all-to-all-done.1.back_ref = bf16[64,3,72,128]{3,2,1,0:T(8,128)(2,1)} async-done(((bf16[64,3,72,128]{3,2,1,0:T(8,128)(2,1)}), bf16[64,3,72,128]{3,2,1,0:T(8,128)(2,1)}, u32[]{:S(2)}, u32[]{:S(2)}) %all-to-all-start.1) | async-done | bytes 3538976 | tf_op jit(solution)/shard_map/all_to_all | solution.py:417
  167.3 1.6 convert_reduce_fusion
  168.9 0.0 collective-permute-start.1
  168.9 7.0 %put_back.1.field_ref = bf16[69,64,384]{2,1,0:T(8,128)(2,1)} custom-call(bf16[64,3,72,128]{3,2,1,0:T(8,128)(2,1)} %all-to-all-done.1.back_ref), custom_call_target="tpu_custom_call" | custom-call | flops 1048576 | bytes 7340032 | tf_op jit(solution)/shard_map/put_back/pallas_call | solution.py:382
  176.0 0.0 collective-permute-done.1.other_ref
  176.0 2.7 %nudge.1 = bf16[69,64,384]{2,1,0:T(8,128)(2,1)} custom-call(f32[1]{0:T(128)} %bitcast.6.total_ref, f32[1]{0:T(128)} %collective-permute-done.1.other_ref, f32[1]{0:T(128)S(6)} %copy.12.climate_ref, bf16[69,64,384]{2,1,0:T(8,128)(2,1)} %put_back.1.field_ref), custom_call_target="tpu_custom_call", output_to_operand_aliasing={{}: (3, {})} | custom-call | flops 65536 | bytes 131072 | tf_op jit(solution)/shard_map/nudge/pallas_call | solution.py:404
  (1 shorter events, 0.0 us)
Async XLA Ops:
  0.0 49.1 %copy-start = (s32[384,128]{1,0:T(8,128)S(1)}, s32[384,128]{1,0:T(8,128)}, u32[]{:S(2)}) copy-start(s32[384,128]{1,0:T(8,128)} %param.14) | copy-start | bytes 589828
  1.1 1.8 %collective-permute-start = (bf16[69,8,384]{2,1,0:T(8,128)(2,1)S(1)}, bf16[69,8,384]{2,1,0:T(8,128)(2,1)S(1)}, u32[]{:S(2)}, u32[]{:S(2)}) collective-permute-start(bf16[69,8,384]{2,1,0:T(8,128)(2,1)S(1)} %dynamic-slice_bitcast_fusion), channel_id=1, source_target_pairs={{0,64},{64,0},{1,65},{65,1},{2,66},{66,2},{3,67},{67,3},{4,68},{68... | collective-permute-start | bytes 1271816 | tf_op jit(solution)/shard_map/ppermute | solution.py:427
  2.9 0.8 copy-start.3
  37.3 57.1 %copy-start.1 = (f32[6,128]{1,0:T(8,128)S(1)}, f32[6,128]{1,0:T(8,128)}, u32[]{:S(2)}) copy-start(f32[6,128]{1,0:T(8,128)} %value_ref.1) | copy-start | bytes 9220
  37.3 57.1 %copy-start.2 = (f32[6,128]{1,0:T(8,128)S(1)}, f32[6,128]{1,0:T(8,128)}, u32[]{:S(2)}) copy-start(f32[6,128]{1,0:T(8,128)} %weight_ref.1) | copy-start | bytes 9220
  37.3 57.1 %all-to-all-start = ((bf16[64,3,72,128]{3,2,1,0:T(8,128)(2,1)}), bf16[64,3,72,128]{3,2,1,0:T(8,128)(2,1)}, u32[]{:S(2)}, u32[]{:S(2)}) async-start(bf16[64,3,72,128]{3,2,1,0:T(8,128)(2,1)} %forecast.1), calls=%async_computation | async-start | bytes 7077888 | tf_op jit(solution)/shard_map/all_to_all | solution.py:417
  113.9 53.5 %all-to-all-start.1 = ((bf16[64,3,72,128]{3,2,1,0:T(8,128)(2,1)}), bf16[64,3,72,128]{3,2,1,0:T(8,128)(2,1)}, u32[]{:S(2)}, u32[]{:S(2)}) async-start(bf16[64,3,72,128]{3,2,1,0:T(8,128)(2,1)} %mix.1), calls=%async_computation.1 | async-start | bytes 7077888 | tf_op jit(solution)/shard_map/all_to_all | solution.py:417
  168.9 7.1 %collective-permute-start.1 = (f32[1]{0:T(128)}, f32[1]{0:T(128)}, u32[]{:S(2)}, u32[]{:S(2)}) collective-permute-start(f32[1]{0:T(128)} %bitcast.6.total_ref), channel_id=1, source_target_pairs={{0,64},{64,0},{1,65},{65,1},{2,66},{66,2},{3,67},{67,3},{4,68},{68... | collective-permute-start | bytes 20 | tf_op jit(solution)/shard_map/ppermute | solution.py:436

commit v4 on v3

--- a/solution.py
+++ b/solution.py
@@ -34,6 +34,10 @@
     return pltpu.CompilerParams(vmem_limit_bytes=mib * 1024 * 1024)
 
 
+def in_hbm(x):
+    return pltpu.with_memory_space_constraint(x, pltpu.HBM)
+
+
 def cost(flops, size, tanhs=0):
     return pl.CostEstimate(flops=flops, bytes_accessed=size, transcendentals=tanhs)
 
@@ -41,7 +45,7 @@
 def gelu_twice(linear):
     linear = linear.astype(jnp.bfloat16)
     inner = linear * (jnp.bfloat16(GELU_A) + jnp.bfloat16(GELU_B) * (linear * linear))
-    return linear + linear * jnp.tanh(inner)
+    return linear * (jnp.bfloat16(1.0) + jnp.tanh(inner))
 
 
 def mlp(smooth, w_in, w_out):
@@ -73,8 +77,8 @@
 
 
 def forecast_kernel(
-    role_ref, x_ref, halo_ref, diff_ref, w_in_ref, b_in_ref, w_out_ref, out_ref, own, before, after, messages,
-    in_sems, out_sems,
+    role_ref, climate_ref, x_ref, halo_ref, diff_ref, w_in_ref, b_in_ref, w_out_ref,
+    out_ref, climate_out, own, before, after, in_sems,
 ):
     f32, bf16 = jnp.float32, jnp.bfloat16
     role = role_ref[0]
@@ -83,12 +87,9 @@
         rows = pl.ds(step * 16, 16)
         return pltpu.make_async_copy(x_ref.at[:, rows, :], own.at[:, rows, :], in_sems.at[step])
 
-    def send(r):
-        owners = pl.ds(r * 8, 8)
-        return pltpu.make_async_copy(messages.at[owners], out_ref.at[owners], out_sems.at[r])
-
     for step in range(ROWS // 16):
         fetch(step).start()
+    climate_out[...] = jnp.full((1, LANES), climate_ref[0], f32)
 
     def turned(block):
         ones = jnp.ones((PADDED - FIELDS,) + block.shape[1:], bf16)
@@ -149,13 +150,10 @@
             pieces = [row[:, tile * LANES : (tile + 1) * LANES].astype(bf16) for row in rows]
             for group, message in enumerate(swap_groups(pieces)):
                 owner, slot = owner_of(r, tile, group)
-                messages[owner, slot] = message
-        send(r).start()
+                out_ref[owner, slot] = message
         return carry
 
     lax.fori_loop(0, ROWS // 8, second, 0)
-    for r in range(ROWS // 8):
-        send(r).wait()
 
 
 def split(a):
@@ -191,7 +189,9 @@
     return lax.dot_general(left, right, (((1,), (1,)), ((), ())), preferred_element_type=jnp.float32)
 
 
-def mix_kernel(idx_ref, value_ref, weight_ref, g_ref, out_ref, turn, back, messages, sems):
+def weights_kernel(
+    idx_ref, value_ref, weight_ref, g_ref, turn, mix_ref, total_ref
+):
     f32, bf16 = jnp.float32, jnp.bfloat16
     lane = lax.broadcasted_iota(jnp.int32, (MEMBERS, LANES), 1)
     low = lane < MEMBERS
@@ -204,9 +204,6 @@
         first = jnp.sum(jnp.where(low[: a.shape[0]], a, 0.0), axis=1, keepdims=True)
         second = jnp.sum(jnp.where(low[: a.shape[0]], 0.0, a), axis=1, keepdims=True)
         return jnp.where(low[: a.shape[0]], first, second)
-
-    def send(k):
-        return pltpu.make_async_copy(messages.at[:, k], out_ref.at[:, k], sems.at[k])
 
     precisions, pulled = [], []
     for k in range(TILES):
@@ -263,119 +260,149 @@
     _, roots = lax.fori_loop(0, NS_ITERS, newton, (iterates, [eye] * TILES))
     shifts = [pair_dot([r], p)[0] for r, p in zip(roots, pulled)]
     shifts = [pair_dot([r], p)[0] for r, p in zip(roots, shifts)]
+    total = jnp.zeros((1, LANES), f32)
+    odd_cell = (lane & EDGE) != 0
+    for k, (root, shift, scale) in enumerate(zip(roots, shifts, scales)):
+        combined = jnp.sqrt((MEMBERS - 1.0) / scale) * root + shift / scale
+        rest = (1.0 - jnp.sum(combined, axis=0, keepdims=True)) * (1.0 / MEMBERS)
+        mix = combined + rest
+        across = mix.T
+        mix_ref[k] = jnp.concatenate([across[:MEMBERS], across[MEMBERS:]], axis=1).astype(bf16)
+        shares = jnp.where(
+            odd_cell,
+            jnp.sum(jnp.where(low, 0.0, mix), axis=1, keepdims=True),
+            jnp.sum(jnp.where(low, mix, 0.0), axis=1, keepdims=True),
+        )
+        total = total + jnp.sum(shares * turn[k, 0].astype(f32), axis=0, keepdims=True)
+    total_ref[...] = jnp.sum(total, axis=1, keepdims=True)
+
+
+def apply_kernel(climate_ref, total_ref, other_ref, mix_ref, turn, out_ref, back):
+    f32, bf16 = jnp.float32, jnp.bfloat16
     even = jnp.where((lax.broadcasted_iota(jnp.int32, (MEMBERS, BLOCK), 1) & EDGE) == 0, 1.0, 0.0)
     even = even.astype(bf16)
     uneven = bf16(1.0) - even
-    mixes = []
-    for root, shift, scale in zip(roots, shifts, scales):
-        combined = jnp.sqrt((MEMBERS - 1.0) / scale) * root + shift / scale
-        rest = (1.0 - jnp.sum(combined, axis=0, keepdims=True)) * (1.0 / MEMBERS)
-        across = (combined + rest).T
-        mixes.append(jnp.concatenate([across[:MEMBERS], across[MEMBERS:]], axis=1).astype(bf16))
-
-    def mixed(k, f):
-        x = jnp.concatenate([turn[k, f], turn[k, f + 1]], axis=1)
-        x = jnp.concatenate([x * even, x * uneven], axis=0)
-        return jnp.dot(mixes[k], x, preferred_element_type=f32)
-
-    total = jnp.zeros((1, 1), f32)
+    total = total_ref[...] + other_ref[...] - climate_ref[...] * (VALUES // MEMBERS)
+    total = jnp.broadcast_to(total, (MEMBERS, LANES))
+    high = total.astype(bf16)
+    middle = (total - high.astype(f32)).astype(bf16)
+    low = (total - high.astype(f32) - middle.astype(f32)).astype(bf16)
     for k in range(TILES):
+        mix = mix_ref[k]
 
         def apply(step, carry):
             for pair in range(12):
                 f = step * 24 + 2 * pair
-                new = mixed(k, f).astype(bf16)
+                x = jnp.concatenate([turn[k, f], turn[k, f + 1]], axis=1)
+                x = jnp.concatenate([x * even, x * uneven], axis=0)
+                new = jnp.dot(mix, x, preferred_element_type=f32).astype(bf16)
                 back[k, f] = new[:, :LANES]
                 back[k, f + 1] = new[:, LANES:]
             return carry
 
         lax.fori_loop(0, PADDED // 24, apply, 0)
-        first = mixed(k, 0)[:, :LANES]
-        total = total + jnp.sum(jnp.sum(first, axis=0, keepdims=True), axis=1, keepdims=True)
-
-    high = total.astype(bf16)
-    middle = (total - high.astype(f32)).astype(bf16)
-    low_part = (total - high.astype(f32) - middle.astype(f32)).astype(bf16)
-    for row, part in enumerate((high, middle, low_part)):
-        back[TILES - 1, FIELDS + row] = jnp.broadcast_to(part, (MEMBERS, LANES))
-    for k in range(TILES):
+        if k == TILES - 1:
+            for row, part in enumerate((high, middle, low)):
+                back[k, FIELDS + row] = part
 
         def give(step, carry):
             m = pl.multiple_of(step * 16, 16)
-            messages[pl.ds(m, 16), k] = jnp.swapaxes(back[k, :, pl.ds(m, 16), :], 0, 1)
+            out_ref[pl.ds(m, 16), k] = jnp.swapaxes(back[k, :, pl.ds(m, 16), :], 0, 1)
             return carry
 
         lax.fori_loop(0, MEMBERS // 16, give, 0, unroll=2)
-        send(k).start()
-    for k in range(TILES):
-        send(k).wait()
 
 
 def last_kernel(back_ref, out_ref, grid, sems):
-    def send(step):
-        rows = pl.ds(pl.multiple_of(step * 16, 16), 16)
-        return pltpu.make_async_copy(grid.at[:, rows, :], out_ref.at[:, rows, :], sems.at[step])
-
-    def block(step, carry):
-        for tile in range(TILES):
-            rows = []
-            for half in range(2):
-                pieces = []
-                for group in range(8):
-                    owner, slot = owner_of(step * 2 + half, tile, group)
-                    pieces.append(back_ref[owner, slot])
-                rows += swap_groups(pieces)
-            values = jnp.swapaxes(jnp.stack(rows), 0, 1)[:FIELDS]
-            place = pl.ds(pl.multiple_of(step * 16, 16), 16)
-            grid[:, place, tile * LANES : (tile + 1) * LANES] = values
-        send(step).start()
-        return carry
-
-    lax.fori_loop(0, ROWS // 16, block, 0)
-    for step in range(ROWS // 16):
-        send(step).wait()
+    f32, bf16 = jnp.float32, jnp.bfloat16
+
+    def send(first, count):
+        fields = pl.ds(first, count)
+        return pltpu.make_async_copy(grid.at[fields], out_ref.at[fields], sems.at[first // 16])
+
+    totals = jnp.zeros((8, LANES), f32)
+    for owner in range(MEMBERS):
+        totals = totals + back_ref[owner, TILES - 1, PADDED - 8 : PADDED, :].astype(f32)
+    offset = jnp.sum(totals[8 - PADDED + FIELDS :], axis=0, keepdims=True) / -VALUES
+
+    chunks = [(first, min(16, FIELDS - first)) for first in range(0, FIELDS, 16)]
+    for first, count in chunks:
+        taken = slice(first, min(first + 16, PADDED))
+
+        def block(step, carry):
+            for tile in range(TILES):
+                rows = []
+                for half in range(2):
+                    pieces = []
+                    for group in range(8):
+                        owner, slot = owner_of(step * 2 + half, tile, group)
+                        pieces.append(back_ref[owner, slot, taken, :])
+                    rows += swap_groups(pieces)
+                values = jnp.swapaxes(jnp.stack(rows), 0, 1)[:count]
+                place = pl.ds(pl.multiple_of(step * 16, 16), 16)
+                lanes = slice(tile * LANES, (tile + 1) * LANES)
+                if first == 0:
+                    grid[0:1, place, lanes] = (values[:1].astype(f32) + offset).astype(bf16)
+                    grid[1:count, place, lanes] = values[1:]
+                else:
+                    grid[first : first + count, place, lanes] = values
+            return carry
+
+        lax.fori_loop(0, ROWS // 16, block, 0)
+        send(first, count).start()
+    for first, count in chunks:
+        send(first, count).wait()
 
 
 MESSAGES = jax.ShapeDtypeStruct((MEMBERS, TILES, PADDED, LANES), jnp.bfloat16)
 
 
-def forecast(role, x, halo, diff, w_in, b_in, w_out):
+def forecast(role, climate, x, halo, diff, w_in, b_in, w_out):
     cells = 2 * ROWS * LON
     return pl.pallas_call(
         forecast_kernel,
-        out_shape=MESSAGES,
-        in_specs=[IN_SMEM, IN_HBM] + [IN_VMEM] * 5,
-        out_specs=IN_HBM,
+        out_shape=(MESSAGES, jax.ShapeDtypeStruct((1, LANES), jnp.float32)),
+        in_specs=[IN_SMEM, IN_SMEM, IN_HBM] + [IN_VMEM] * 5,
+        out_specs=(IN_VMEM, IN_VMEM),
         scratch_shapes=[
             pltpu.VMEM((FIELDS, ROWS, LON), jnp.bfloat16),
             pltpu.VMEM((ROWS + 16, PADDED, LON), jnp.bfloat16),
             pltpu.VMEM((ROWS + 2, PADDED, LON), jnp.bfloat16),
-            pltpu.VMEM(MESSAGES.shape, jnp.bfloat16),
             pltpu.SemaphoreType.DMA((ROWS // 16,)),
-            pltpu.SemaphoreType.DMA((ROWS // 8,)),
         ],
-        compiler_params=params(56),
+        compiler_params=params(32),
         cost_estimate=cost(cells * LATENT * 256 * 4, 7 << 20, cells * LATENT),
         name="forecast",
-    )(role, x, halo, diff, w_in, b_in, w_out)
-
-
-def mix(idx, value, weight, g):
+    )(role, climate, in_hbm(x), halo, in_hbm(diff), in_hbm(w_in), in_hbm(b_in), in_hbm(w_out))
+
+
+def weights(idx, value, weight, g):
     return pl.pallas_call(
-        mix_kernel,
+        weights_kernel,
+        out_shape=(
+            jax.ShapeDtypeStruct((TILES, PADDED, MEMBERS, LANES), jnp.bfloat16),
+            jax.ShapeDtypeStruct((TILES, MEMBERS, LANES), jnp.bfloat16),
+            jax.ShapeDtypeStruct((1, 1), jnp.float32),
+        ),
+        in_specs=[IN_VMEM] * 4,
+        out_specs=(IN_VMEM,) * 3,
+        compiler_params=params(32),
+        cost_estimate=cost(8 << 30, 7 << 20),
+        name="weights",
+    )(idx, value, weight, g)
+
+
+def apply(climate, total, other, mixes, turn):
+    return pl.pallas_call(
+        apply_kernel,
         out_shape=MESSAGES,
-        in_specs=[IN_VMEM] * 4,
-        out_specs=IN_HBM,
-        scratch_shapes=[
-            pltpu.VMEM((TILES, PADDED, MEMBERS, LANES), jnp.bfloat16),
-            pltpu.VMEM((TILES, PADDED, MEMBERS, LANES), jnp.bfloat16),
-            pltpu.VMEM(MESSAGES.shape, jnp.bfloat16),
-            pltpu.SemaphoreType.DMA((TILES,)),
-        ],
-        compiler_params=params(53),
+        in_specs=[IN_VMEM] * 5,
+        out_specs=IN_VMEM,
+        scratch_shapes=[pltpu.VMEM((TILES, PADDED, MEMBERS, LANES), jnp.bfloat16)],
+        compiler_params=params(32),
         cost_estimate=cost(8 << 30, 7 << 20),
-        name="mix",
-    )(idx, value, weight, g)
+        name="apply",
+    )(climate, total, other, mixes, turn)
 
 
 def put_back(back):
@@ -386,31 +413,12 @@
         out_specs=IN_HBM,
         scratch_shapes=[
             pltpu.VMEM((FIELDS, ROWS, LON), jnp.bfloat16),
-            pltpu.SemaphoreType.DMA((ROWS // 16,)),
+            pltpu.SemaphoreType.DMA((PADDED // 16 + 1,)),
         ],
         compiler_params=params(50),
         cost_estimate=cost(1 << 20, 7 << 20),
         name="put_back",
     )(back)
-
-
-def nudge_kernel(total_ref, other_ref, climate_ref, field_ref, out_ref):
-    offset = climate_ref[0] - (total_ref[0] + other_ref[0]) / VALUES
-    out_ref[...] = (field_ref[...].astype(jnp.float32) + offset).astype(jnp.bfloat16)
-
-
-def nudge(total, other, climate, placed):
-    field = pl.BlockSpec((1, ROWS, LON), lambda i: (0, 0, 0))
-    return pl.pallas_call(
-        nudge_kernel,
-        out_shape=jax.ShapeDtypeStruct(placed.shape, placed.dtype),
-        grid=(1,),
-        in_specs=[IN_SMEM, IN_SMEM, IN_SMEM, field],
-        out_specs=field,
-        input_output_aliases={3: 0},
-        cost_estimate=cost(1 << 16, 1 << 17),
-        name="nudge",
-    )(total, other, climate, placed)
 
 
 def exchange(messages):
@@ -423,18 +431,18 @@
     role = lax.axis_index("role")
     dev = lax.axis_index("dev")
     x = initial_realizations.reshape(FIELDS, ROWS, LON)
+    index = lax.dynamic_slice_in_dim(obs_index, dev * PATCHES, PATCHES, 0)
     edge = lax.dynamic_slice_in_dim(x, jnp.where(role == 0, ROWS - 8, 0), 8, 1)
     halo = lax.ppermute(edge, "role", [(0, 1), (1, 0)])
-    sent = forecast(
-        role.reshape(1), x, halo, diffusivity.reshape(1, FIELDS), w_in.T, b_in.reshape(1, LATENT), w_out
+    halo, index = lax.optimization_barrier((halo, index))
+    sent, climate = forecast(
+        role.reshape(1), climate, x, halo, diffusivity.reshape(1, FIELDS), w_in.T, b_in.reshape(1, LATENT), w_out
     )
     got = exchange(sent)
-    index = lax.dynamic_slice_in_dim(obs_index, dev * PATCHES, PATCHES, 0)
-    mixed = mix(index, obs_value, obs_weight, got)
-    back = exchange(mixed)
-    total = jnp.sum(back[:, TILES - 1, FIELDS:, 0].astype(jnp.float32)).reshape(1)
+    turn, mixes, total = weights(index, obs_value, obs_weight, got)
     other = lax.ppermute(total, "role", [(0, 1), (1, 0)])
-    return nudge(total, other, climate, put_back(back))[None]
+    back = exchange(apply(climate, total, other, mixes, turn))
+    return put_back(back)[None]
 
 
 def solution(mesh):

time: 181 us -> 168 us (0.928); the launches traced: 179 us -> 168 us
  blocking collectives: 0 us -> 108 us
  waiting for transfers between devices: 89.1 us -> 2.31 us
  starting transfers between devices: 22.6 us -> 0.09 us
  Pallas kernels: 62.7 us -> 56.1 us
    all_to_all x0 -> x2, blocking collectives: none -> 108 us  [exchange(): lax.all_to_all(messages, 'dev', split_axis=0, concat_axis=0, tiled=True)]
    all_to_all x2 -> x0, waiting for transfers between devices: 87.4 us -> none  [exchange(): lax.all_to_all(messages, 'dev', split_axis=0, concat_axis=0, tiled=True)]
    all_to_all x2 -> x0, starting transfers between devices: 22.5 us -> none  [exchange(): lax.all_to_all(messages, 'dev', split_axis=0, concat_axis=0, tiled=True)]
    pallas_call x3, Pallas kernels: 55.7 us -> 50.7 us  [the longest x1 33 us: forecast(): pl.pallas_call(forecast_kernel, out_shape=(MESSAGES, jax.ShapeDtypeStruct...]
  transfers between devices with their start and end apart: 4 -> 2, of which waited for: 3 -> 2; matrix products, arithmetic and copies ran while one was open for 0% -> 0% of each run, Pallas kernels for 4% -> 0%
where the time goes in v4:
time: 168 us
  blocking collectives  108 us (64%)
  Pallas kernels  56.1 us (33%)
  waiting for transfers between devices  2.31 us (1%)
    all_to_all x2, blocking collectives, exchange(): lax.all_to_all(messages, 'dev', split_axis=0, concat_axis=0, tiled=True)  108 us
    pallas_call x1, Pallas kernels, forecast(): pl.pallas_call(forecast_kernel, out_shape=(MESSAGES, jax.ShapeDtypeStruct...  33 us
    pallas_call x1, Pallas kernels, weights(): pl.pallas_call(weights_kernel, out_shape=(jax.ShapeDtypeStruct((TILES, PA...  12.5 us
    pallas_call x1, Pallas kernels, put_back(): pl.pallas_call(last_kernel, out_shape=jax.ShapeDtypeStruct((FIELDS, ROWS,...  5.4 us
    pallas_call x1, Pallas kernels, apply(): pl.pallas_call(apply_kernel, out_shape=MESSAGES, in_specs=[IN_VMEM] * 5,...  5.29 us
  transfers between devices with their start and end apart: 2, of which 2 were waited for; matrix products, arithmetic and copies ran while one was open for 0% of the time, Pallas kernels for 0%

profile of v4, /device:TPU:0, one launch (start us, length us, event | category | flops | bytes accessed | tf_op | source)
XLA Modules:
  0.0 167.9 jit_solution(8776145283148711181)
XLA Ops:
  0.0 0.0 copy-start
  0.0 1.1 dynamic-slice_bitcast_fusion
  1.1 0.1 collective-permute-start
  1.8 0.0 copy-done
  1.9 1.1 collective-permute-done.halo_ref
  2.9 33.0 %forecast.1 = (bf16[64,3,72,128]{3,2,1,0:T(8,128)(2,1)S(1)}, f32[1,128]{1,0:T(1,128)S(1)}) custom-call(s32[1]{0:T(128)} %bitcast.role_ref, f32[1]{0:T(128)S(6)} %copy.10.climate_ref, bf16[69,64,384]{2,1,0:T(8,128)(2,1)} %bitcast.8, bf16[69,8,384]{2,1,0:T(8,128)(2,1)S(1)} %collective-permute-done.halo_ref, f32[1,69]{1,0:T(1,128)} %bitcast.11, ...), custom_call_target="tpu_custom_call" | custom-call | flops 25769803776 | bytes 7340032 | tf_op jit(solution)/shard_map/forecast/pallas_call | solution.py:362
  35.9 0.0 copy-start.1
  35.9 0.0 copy-start.2
  35.9 56.9 %all_to_all.10.g_ref = bf16[64,3,72,128]{3,2,1,0:T(8,128)(2,1)S(1)} all-to-all(bf16[64,3,72,128]{3,2,1,0:T(8,128)(2,1)S(1)} %get-tuple-element.15), channel_id=1, replica_groups=mesh['role'=2,'dev'=64] {'dev'}, dimensions={0} | all-to-all | bytes 7077888 | tf_op jit(solution)/shard_map/all_to_all | solution.py:425
  92.8 0.0 copy-done.1
  92.8 0.0 copy-done.2
  92.8 12.5 %weights.1 = (bf16[3,72,64,128]{3,2,1,0:T(8,128)(2,1)S(1)}, bf16[3,64,128]{2,1,0:T(8,128)(2,1)S(1)}, f32[1,1]{1,0:T(1,128)}) custom-call(s32[6,128]{1,0:T(8,128)S(1)} %constant_dynamic-slice_fusion.idx_ref, f32[6,128]{1,0:T(8,128)S(1)} %copy-done.1, f32[6,128]{1,0:T(8,128)S(1)} %copy-done.2, bf16[64,3,72,128]{3,2,1,0:T(8,128)(2,1)S(1)} %all_to_all.10.g_ref), custom_call_target="tpu_custom_call" | custom-call | flops 8589934592 | bytes 7340032 | tf_op jit(solution)/shard_map/weights/pallas_call | solution.py:380
  105.3 0.0 collective-permute-start.1
  105.3 1.2 collective-permute-done.1.other_ref
  106.6 5.3 %apply.1 = bf16[64,3,72,128]{3,2,1,0:T(8,128)(2,1)S(1)} custom-call(f32[1,128]{1,0:T(1,128)S(1)} %get-tuple-element.13.climate_ref, f32[1,1]{1,0:T(1,128)} %get-tuple-element.16.total_ref, f32[1,1]{1,0:T(1,128)} %collective-permute-done.1.other_ref, bf16[3,64,128]{2,1,0:T(8,128)(2,1)S(1)} %get-tuple-element.17.mix_ref, ...), custom_call_target="tpu_custom_call" | custom-call | flops 8589934592 | bytes 7340032 | tf_op jit(solution)/shard_map/apply/pallas_call | solution.py:396
  111.9 50.6 %all_to_all.11.back_ref = bf16[64,3,72,128]{3,2,1,0:T(8,128)(2,1)S(1)} all-to-all(bf16[64,3,72,128]{3,2,1,0:T(8,128)(2,1)S(1)} %apply.1), channel_id=1, replica_groups=mesh['role'=2,'dev'=64] {'dev'}, dimensions={0} | all-to-all | bytes 7077888 | tf_op jit(solution)/shard_map/all_to_all | solution.py:425
  162.5 5.4 %put_back.1 = bf16[69,64,384]{2,1,0:T(8,128)(2,1)} custom-call(bf16[64,3,72,128]{3,2,1,0:T(8,128)(2,1)S(1)} %all_to_all.11.back_ref), custom_call_target="tpu_custom_call" | custom-call | flops 1048576 | bytes 7340032 | tf_op jit(solution)/shard_map/put_back/pallas_call | solution.py:409
  (1 shorter events, 0.0 us)
Async XLA Ops:
  0.0 1.8 %copy-start = (s32[384,128]{1,0:T(8,128)S(1)}, s32[384,128]{1,0:T(8,128)}, u32[]{:S(2)}) copy-start(s32[384,128]{1,0:T(8,128)} %param.14) | copy-start | bytes 589828
  1.1 1.8 %collective-permute-start = (bf16[69,8,384]{2,1,0:T(8,128)(2,1)S(1)}, bf16[69,8,384]{2,1,0:T(8,128)(2,1)S(1)}, u32[]{:S(2)}, u32[]{:S(2)}) collective-permute-start(bf16[69,8,384]{2,1,0:T(8,128)(2,1)S(1)} %dynamic-slice_bitcast_fusion), channel_id=1, source_target_pairs={{0,64},{64,0},{1,65},{65,1},{2,66},{66,2},{3,67},{67,3},{4,68},{68... | collective-permute-start | bytes 1271816 | tf_op jit(solution)/shard_map/ppermute | solution.py:436
  35.9 56.9 %copy-start.1 = (f32[6,128]{1,0:T(8,128)S(1)}, f32[6,128]{1,0:T(8,128)}, u32[]{:S(2)}) copy-start(f32[6,128]{1,0:T(8,128)} %value_ref.1) | copy-start | bytes 9220
  35.9 56.9 %copy-start.2 = (f32[6,128]{1,0:T(8,128)S(1)}, f32[6,128]{1,0:T(8,128)}, u32[]{:S(2)}) copy-start(f32[6,128]{1,0:T(8,128)} %weight_ref.1) | copy-start | bytes 9220
  105.3 1.2 collective-permute-start.1

commit v5 on v4

--- a/solution.py
+++ b/solution.py
@@ -18,6 +18,10 @@
 MEMBERS = 64
 OBS = 128
 PATCHES = 6
+MAIN = 64
+REST = FIELDS - MAIN
+TAIL = TILES * MAIN
+MESSAGE = 208
 GROUP = 16
 BLOCK = 256
 DEPTH = 3
@@ -48,17 +52,14 @@
     return linear * (jnp.bfloat16(1.0) + jnp.tanh(inner))
 
 
-def mlp(smooth, w_in, w_out):
-    count = smooth.shape[1] // BLOCK
-    linear, changes = {}, []
+def mlp(count, smooth_of, done, w_in, w_out):
+    linear = {}
     for n in range(count + DEPTH):
         if n < count:
-            cols = slice(n * BLOCK, (n + 1) * BLOCK)
-            linear[n] = jnp.dot(w_in, smooth[:, cols], preferred_element_type=jnp.float32)
+            linear[n] = jnp.dot(w_in, smooth_of(n), preferred_element_type=jnp.float32)
         if n >= DEPTH:
             hidden = gelu_twice(linear.pop(n - DEPTH))
-            changes.append(jnp.dot(w_out, hidden, preferred_element_type=jnp.float32))
-    return jnp.concatenate(changes, axis=1)
+            done(n - DEPTH, jnp.dot(w_out, hidden, preferred_element_type=jnp.float32))
 
 
 def swap_groups(rows):
@@ -78,7 +79,7 @@
 
 def forecast_kernel(
     role_ref, climate_ref, x_ref, halo_ref, diff_ref, w_in_ref, b_in_ref, w_out_ref,
-    out_ref, climate_out, own, before, after, in_sems,
+    out_ref, climate_out, own, before, after, rests, in_sems,
 ):
     f32, bf16 = jnp.float32, jnp.bfloat16
     role = role_ref[0]
@@ -100,9 +101,12 @@
     before[72:80] = zeros
     before[pl.ds(jnp.where(role == 0, 72, 0), 8)] = turned(halo_ref[...])
 
-    for step in range(ROWS // 16):
+    def take(step):
         fetch(step).wait()
-        before[8 + step * 16 : 24 + step * 16] = turned(own[:, step * 16 : (step + 1) * 16, :])
+        place = pl.multiple_of(step * 16, 16)
+        before[pl.ds(8 + place, 16)] = turned(own[:, pl.ds(place, 16), :])
+
+    take(0)
 
     diff = jnp.concatenate([diff_ref[...], jnp.zeros((1, LANES - FIELDS), f32)], axis=1)
     diff = jnp.broadcast_to(diff, (LANES, LANES)).T[:PADDED]
@@ -117,24 +121,52 @@
         [w_out_ref[...] * bf16(0.5), jnp.zeros((PADDED - FIELDS, LATENT), bf16)], axis=0
     )
 
-    def advance(ref, place, count):
-        centre, smooth = [], []
-        packed = [ref[place + k - 1] for k in range(count + 2)]
-        rows = [row.astype(f32) for row in packed]
-        for k in range(count):
-            c = rows[k + 1]
-            around = rows[k] + rows[k + 2] + pltpu.roll(packed[k + 1], 1, 1).astype(f32) + pltpu.roll(packed[k + 1], LON - 1, 1).astype(f32)
-            smooth.append((c + diff * (around - 4.0 * c)).astype(bf16))
-            centre.append(c)
-        change = mlp(jnp.concatenate(smooth, axis=1), w_in, w_out)
-        return [centre[k] + change[:, k * LON : (k + 1) * LON] for k in range(count)]
+    def advance(ref, place, count, give):
+        rows, smooth = {}, {}
+
+        def row(k):
+            if k not in rows:
+                rows[k] = ref[place + k]
+            return rows[k].astype(f32)
+
+        def smooth_of(n):
+            pieces = []
+            for piece in (2 * n, 2 * n + 1):
+                k, tile = divmod(piece, TILES)
+                if k not in smooth:
+                    c = row(k)
+                    around = row(k - 1) + row(k + 1) + pltpu.roll(rows[k], 1, 1).astype(f32)
+                    around = around + pltpu.roll(rows[k], LON - 1, 1).astype(f32)
+                    smooth[k] = (c + diff * (around - 4.0 * c)).astype(bf16)
+                pieces.append(smooth[k][:, tile * LANES : (tile + 1) * LANES])
+            return jnp.concatenate(pieces, axis=1)
+
+        def done(n, change):
+            for half, piece in enumerate((2 * n, 2 * n + 1)):
+                k, tile = divmod(piece, TILES)
+                lanes = slice(tile * LANES, (tile + 1) * LANES)
+                new = rows[k][:, lanes].astype(f32) + change[:, half * LANES : (half + 1) * LANES]
+                give(k, tile, new.astype(bf16))
+
+        mlp(count * TILES // 2, smooth_of, done, w_in, w_out)
+
+    def first_rows(start, count):
+        def give(k, tile, new):
+            after[start + k, :, tile * LANES : (tile + 1) * LANES] = new
+
+        advance(before, start + 7, count, give)
 
     def first(step, carry):
-        for k, row in enumerate(advance(before, step * 6 + 7, 6)):
-            after[step * 6 + k] = row.astype(bf16)
+        first_rows(step * 16, 16)
+
+        @pl.when(step < ROWS // 16 - 1)
+        def _():
+            take(step + 1)
+
         return carry
 
-    lax.fori_loop(0, (ROWS + 2) // 6, first, 0)
+    lax.fori_loop(0, ROWS // 16, first, 0)
+    first_rows(ROWS, 2)
 
     @pl.when(role == 0)
     def _():
@@ -144,16 +176,28 @@
     def _():
         after[ROWS + 1] = jnp.zeros((PADDED, LON), bf16)
 
-    def second(r, carry):
-        rows = advance(after, r * 8 + 1, 8)
-        for tile in range(TILES):
-            pieces = [row[:, tile * LANES : (tile + 1) * LANES].astype(bf16) for row in rows]
-            for group, message in enumerate(swap_groups(pieces)):
-                owner, slot = owner_of(r, tile, group)
-                out_ref[owner, slot] = message
+    def second(step, carry):
+        pieces = {}
+
+        def give(k, tile, new):
+            pieces[k, tile] = new
+            if k % 8 == 7:
+                rows = [pieces.pop((k - 7 + a, tile)) for a in range(8)]
+                for group, message in enumerate(swap_groups(rows)):
+                    owner, slot = owner_of(step * 2 + k // 8, tile, group)
+                    out_ref[owner, slot * MAIN : (slot + 1) * MAIN, :] = message[:MAIN]
+                    rests[owner, slot] = message[MAIN:]
+
+        advance(after, step * 16 + 1, 16, give)
+        for half in range(2):
+            for u in range(8):
+                owner = step * 16 + half * 8 + u
+                parts = [rests[owner, slot].astype(f32)[:REST] for slot in range(TILES)]
+                tail = jnp.concatenate(parts + [jnp.zeros((1, LANES), f32)], axis=0)
+                out_ref[owner, TAIL:MESSAGE, :] = tail.astype(bf16)
         return carry
 
-    lax.fori_loop(0, ROWS // 8, second, 0)
+    lax.fori_loop(0, ROWS // 16, second, 0)
 
 
 def split(a):
@@ -161,25 +205,19 @@
     return high, (a - high.astype(jnp.float32)).astype(jnp.bfloat16)
 
 
-def stacked(a):
+def streamed(a):
+    high, rest = split(a)
+    return jnp.concatenate([high, rest, high], axis=1)
+
+
+def held(a):
     low = lax.broadcasted_iota(jnp.int32, (MEMBERS, LANES), 1) < MEMBERS
-    high, rest = split(a)
-    high_turned, rest_turned = pltpu.roll(high, MEMBERS, 1), pltpu.roll(rest, MEMBERS, 1)
-    first = jnp.concatenate([jnp.where(low, high, rest_turned), high[:, :MEMBERS]], axis=1)
-    second = jnp.concatenate([jnp.where(low, high_turned, rest), high_turned[:, :MEMBERS]], axis=1)
-    return jnp.concatenate([first, second], axis=0)
-
-
-def pair_dot(lefts, right):
-    low = lax.broadcasted_iota(jnp.int32, (MEMBERS, LANES), 1) < MEMBERS
-    high, rest = split(right)
-    right = jnp.concatenate([high, high, rest], axis=0)
-    left = jnp.concatenate([stacked(a) for a in lefts], axis=0)
-    both = jnp.dot(left, right, preferred_element_type=jnp.float32)
-    return [
-        jnp.where(low, both[n * LANES : n * LANES + MEMBERS], both[n * LANES + MEMBERS : (n + 1) * LANES])
-        for n in range(len(lefts))
-    ]
+    high, rest = split(jnp.concatenate([jnp.where(low, a, 0.0), jnp.where(low, 0.0, a)], axis=0))
+    return jnp.concatenate([high, high, rest], axis=0)
+
+
+def pair_dot(left, right):
+    return jnp.dot(left, right, preferred_element_type=jnp.float32)
 
 
 def wide_dot(a, b):
@@ -205,15 +243,13 @@
         second = jnp.sum(jnp.where(low[: a.shape[0]], 0.0, a), axis=1, keepdims=True)
         return jnp.where(low[: a.shape[0]], first, second)
 
+    def load(step, carry):
+        m = pl.multiple_of(step * 16, 16)
+        turn[:, pl.ds(m, 16), :] = jnp.swapaxes(g_ref[pl.ds(m, 16)], 0, 1)
+        return carry
+
+    lax.fori_loop(0, MEMBERS // 16, load, 0, unroll=2)
     precisions, pulled = [], []
-    for k in range(TILES):
-
-        def load(step, carry):
-            m = pl.multiple_of(step * 16, 16)
-            turn[k, :, pl.ds(m, 16), :] = jnp.swapaxes(g_ref[pl.ds(m, 16), k], 0, 1)
-            return carry
-
-        lax.fori_loop(0, MEMBERS // 16, load, 0, unroll=2)
     for k in range(TILES):
         idx = jnp.concatenate(
             [idx_ref[2 * k + e : 2 * k + e + 1, :] for e in range(2)], axis=1
@@ -224,17 +260,22 @@
         hot = jnp.where(lax.broadcasted_iota(jnp.int32, (LANES, 2 * OBS), 0) == place, 1.0, 0.0)
         hot = hot.astype(bf16)
 
-        def pick(step, total):
-            for part in range(3):
-                start = step * 24 + part * 8
-                block = turn[k, pl.ds(start, 8)].reshape(8 * MEMBERS, LANES)
-                values = jnp.dot(block, hot, preferred_element_type=f32)
-                for f in range(8):
-                    here = field == start + f
-                    total = jnp.where(here, values[f * MEMBERS : (f + 1) * MEMBERS], total)
+        def pick(total, start, first, count):
+            block = turn[pl.ds(start, count)].reshape(count * MEMBERS, LANES)
+            values = jnp.dot(block, hot, preferred_element_type=f32)
+            for f in range(count):
+                here = field == first + f
+                total = jnp.where(here, values[f * MEMBERS : (f + 1) * MEMBERS], total)
             return total
 
-        observed = lax.fori_loop(0, PADDED // 24, pick, jnp.zeros((MEMBERS, 2 * OBS), f32))
+        def picks(step, total):
+            for part in range(4):
+                first = step * 32 + part * 8
+                total = pick(total, k * MAIN + first, first, 8)
+            return total
+
+        observed = pick(jnp.zeros((MEMBERS, 2 * OBS), f32), TAIL + k * REST, MAIN, REST)
+        observed = lax.fori_loop(0, MAIN // 32, picks, observed)
         sides, pulls = [], []
         for e in range(2):
             mine = observed[:, e * OBS : (e + 1) * OBS]
@@ -252,14 +293,16 @@
 
     def newton(step, carry):
         iterates, roots = carry
-        products = [pair_dot([r], i)[0] for r, i in zip(roots, iterates)]
+        rights = [held(i) for i in iterates]
+        products = [pair_dot(streamed(r), i) for r, i in zip(roots, rights)]
+        rights = [jnp.concatenate([i, held(r)], axis=1) for i, r in zip(rights, roots)]
         factors = [0.5 * (3.0 * eye - p) for p in products]
-        new = [pair_dot([i, r], f) for i, r, f in zip(iterates, roots, factors)]
-        return [n[0] for n in new], [n[1] for n in new]
-
-    _, roots = lax.fori_loop(0, NS_ITERS, newton, (iterates, [eye] * TILES))
-    shifts = [pair_dot([r], p)[0] for r, p in zip(roots, pulled)]
-    shifts = [pair_dot([r], p)[0] for r, p in zip(roots, shifts)]
+        new = [pair_dot(streamed(f), r) for f, r in zip(factors, rights)]
+        return [n[:, :LANES] for n in new], [n[:, LANES:] for n in new]
+
+    _, roots = lax.fori_loop(0, NS_ITERS, newton, (iterates, [eye] * TILES), unroll=2)
+    shifts = [pair_dot(streamed(r), held(p)) for r, p in zip(roots, pulled)]
+    shifts = [pair_dot(streamed(r), held(p)) for r, p in zip(roots, shifts)]
     total = jnp.zeros((1, LANES), f32)
     odd_cell = (lane & EDGE) != 0
     for k, (root, shift, scale) in enumerate(zip(roots, shifts, scales)):
@@ -273,7 +316,7 @@
             jnp.sum(jnp.where(low, 0.0, mix), axis=1, keepdims=True),
             jnp.sum(jnp.where(low, mix, 0.0), axis=1, keepdims=True),
         )
-        total = total + jnp.sum(shares * turn[k, 0].astype(f32), axis=0, keepdims=True)
+        total = total + jnp.sum(shares * turn[k * MAIN].astype(f32), axis=0, keepdims=True)
     total_ref[...] = jnp.sum(total, axis=1, keepdims=True)
 
 
@@ -283,34 +326,47 @@
     even = even.astype(bf16)
     uneven = bf16(1.0) - even
     total = total_ref[...] + other_ref[...] - climate_ref[...] * (VALUES // MEMBERS)
-    total = jnp.broadcast_to(total, (MEMBERS, LANES))
-    high = total.astype(bf16)
-    middle = (total - high.astype(f32)).astype(bf16)
-    low = (total - high.astype(f32) - middle.astype(f32)).astype(bf16)
+    high = total.astype(bf16).astype(f32)
+    middle = (total - high).astype(bf16).astype(f32)
+    lane = lax.broadcasted_iota(jnp.int32, (1, LANES), 1)
+    parts = jnp.where(lane == 0, high, jnp.where(lane == 1, middle, total - high - middle))
+    parts = jnp.where(lane < 3, parts, 0.0)
+    back[MESSAGE - 1] = jnp.broadcast_to(parts, (MEMBERS, LANES)).astype(bf16)
+
+    def mixed(k, places):
+        x = jnp.concatenate([turn[place] for place in places], axis=1)
+        width = len(places) * LANES
+        x = jnp.concatenate([x * even[:, :width], x * uneven[:, :width]], axis=0)
+        new = jnp.dot(mix_ref[k], x, preferred_element_type=f32).astype(bf16)
+        for n, place in enumerate(places):
+            back[place] = new[:, n * LANES : (n + 1) * LANES]
+
+    def main(k, step):
+        for pair in range(8):
+            place = k * MAIN + step * 16 + 2 * pair
+            mixed(k, [place, place + 1])
+
+    def give(first, count, step):
+        members = pl.ds(pl.multiple_of(step * 16, 16), 16)
+        block = jnp.swapaxes(back[first : first + count, members, :], 0, 1)
+        out_ref[members, first : first + count, :] = block
+
     for k in range(TILES):
-        mix = mix_ref[k]
-
-        def apply(step, carry):
-            for pair in range(12):
-                f = step * 24 + 2 * pair
-                x = jnp.concatenate([turn[k, f], turn[k, f + 1]], axis=1)
-                x = jnp.concatenate([x * even, x * uneven], axis=0)
-                new = jnp.dot(mix, x, preferred_element_type=f32).astype(bf16)
-                back[k, f] = new[:, :LANES]
-                back[k, f + 1] = new[:, LANES:]
+        for place in range(TAIL + k * REST, TAIL + (k + 1) * REST, 2):
+            mixed(k, [p for p in (place, place + 1) if p < TAIL + (k + 1) * REST])
+
+    for k in range(TILES + 1):
+
+        def both(step, carry):
+            if k < TILES:
+                main(k, step)
+            if k > 0:
+                give((k - 1) * MAIN, MAIN, step)
+            else:
+                give(TAIL, MESSAGE - TAIL, step)
             return carry
 
-        lax.fori_loop(0, PADDED // 24, apply, 0)
-        if k == TILES - 1:
-            for row, part in enumerate((high, middle, low)):
-                back[k, FIELDS + row] = part
-
-        def give(step, carry):
-            m = pl.multiple_of(step * 16, 16)
-            out_ref[pl.ds(m, 16), k] = jnp.swapaxes(back[k, :, pl.ds(m, 16), :], 0, 1)
-            return carry
-
-        lax.fori_loop(0, MEMBERS // 16, give, 0, unroll=2)
+        lax.fori_loop(0, 4, both, 0)
 
 
 def last_kernel(back_ref, out_ref, grid, sems):
@@ -320,14 +376,19 @@
         fields = pl.ds(first, count)
         return pltpu.make_async_copy(grid.at[fields], out_ref.at[fields], sems.at[first // 16])
 
-    totals = jnp.zeros((8, LANES), f32)
+    totals = jnp.zeros((MESSAGE - TAIL, LANES), f32)
     for owner in range(MEMBERS):
-        totals = totals + back_ref[owner, TILES - 1, PADDED - 8 : PADDED, :].astype(f32)
-    offset = jnp.sum(totals[8 - PADDED + FIELDS :], axis=0, keepdims=True) / -VALUES
+        totals = totals + back_ref[owner, TAIL:MESSAGE, :].astype(f32)
+    offset = jnp.sum(totals[MESSAGE - TAIL - 1 :], axis=1, keepdims=True) / -VALUES
+
+    def piece(owner, slot, first, count):
+        if first < MAIN:
+            return back_ref[owner, slot * MAIN + first : slot * MAIN + first + count, :]
+        rest = back_ref[owner, TAIL:MESSAGE, :].astype(f32)
+        return rest[slot * REST : (slot + 1) * REST].astype(bf16)
 
     chunks = [(first, min(16, FIELDS - first)) for first in range(0, FIELDS, 16)]
     for first, count in chunks:
-        taken = slice(first, min(first + 16, PADDED))
 
         def block(step, carry):
             for tile in range(TILES):
@@ -336,9 +397,9 @@
                     pieces = []
                     for group in range(8):
                         owner, slot = owner_of(step * 2 + half, tile, group)
-                        pieces.append(back_ref[owner, slot, taken, :])
+                        pieces.append(piece(owner, slot, first, count))
                     rows += swap_groups(pieces)
-                values = jnp.swapaxes(jnp.stack(rows), 0, 1)[:count]
+                values = jnp.swapaxes(jnp.stack(rows), 0, 1)
                 place = pl.ds(pl.multiple_of(step * 16, 16), 16)
                 lanes = slice(tile * LANES, (tile + 1) * LANES)
                 if first == 0:
@@ -354,7 +415,8 @@
         send(first, count).wait()
 
 
-MESSAGES = jax.ShapeDtypeStruct((MEMBERS, TILES, PADDED, LANES), jnp.bfloat16)
+MESSAGES = jax.ShapeDtypeStruct((MEMBERS, MESSAGE, LANES), jnp.bfloat16)
+TURNED = jax.ShapeDtypeStruct((MESSAGE, MEMBERS, LANES), jnp.bfloat16)
 
 
 def forecast(role, climate, x, halo, diff, w_in, b_in, w_out):
@@ -368,6 +430,7 @@
             pltpu.VMEM((FIELDS, ROWS, LON), jnp.bfloat16),
             pltpu.VMEM((ROWS + 16, PADDED, LON), jnp.bfloat16),
             pltpu.VMEM((ROWS + 2, PADDED, LON), jnp.bfloat16),
+            pltpu.VMEM((MEMBERS, TILES, PADDED - MAIN, LANES), jnp.bfloat16),
             pltpu.SemaphoreType.DMA((ROWS // 16,)),
         ],
         compiler_params=params(32),
@@ -380,7 +443,7 @@
     return pl.pallas_call(
         weights_kernel,
         out_shape=(
-            jax.ShapeDtypeStruct((TILES, PADDED, MEMBERS, LANES), jnp.bfloat16),
+            TURNED,
             jax.ShapeDtypeStruct((TILES, MEMBERS, LANES), jnp.bfloat16),
             jax.ShapeDtypeStruct((1, 1), jnp.float32),
         ),
@@ -398,7 +461,7 @@
         out_shape=MESSAGES,
         in_specs=[IN_VMEM] * 5,
         out_specs=IN_VMEM,
-        scratch_shapes=[pltpu.VMEM((TILES, PADDED, MEMBERS, LANES), jnp.bfloat16)],
+        scratch_shapes=[pltpu.VMEM(TURNED.shape, jnp.bfloat16)],
         compiler_params=params(32),
         cost_estimate=cost(8 << 30, 7 << 20),
         name="apply",

time: 168 us -> 160 us (0.952)
  Pallas kernels: 56.1 us -> 50.8 us
  blocking collectives: 108 us -> 105 us
    pallas_call x1, Pallas kernels: 33 us -> 29.6 us  [forecast(): pl.pallas_call(forecast_kernel, out_shape=(MESSAGES, jax.ShapeDtypeStruct...]
    all_to_all x2, blocking collectives: 108 us -> 105 us  [exchange(): lax.all_to_all(messages, 'dev', split_axis=0, concat_axis=0, tiled=True)]
    pallas_call x1, Pallas kernels: 12.5 us -> 10.1 us  [weights(): pl.pallas_call(weights_kernel, out_shape=(TURNED, jax.ShapeDtypeStruct((T...]
where the time goes in v5:
time: 160 us
  blocking collectives  105 us (66%)
  Pallas kernels  50.8 us (32%)
  waiting for transfers between devices  2.31 us (1%)
    all_to_all x2, blocking collectives, exchange(): lax.all_to_all(messages, 'dev', split_axis=0, concat_axis=0, tiled=True)  105 us
    pallas_call x1, Pallas kernels, forecast(): pl.pallas_call(forecast_kernel, out_shape=(MESSAGES, jax.ShapeDtypeStruct...  29.6 us
    pallas_call x1, Pallas kernels, weights(): pl.pallas_call(weights_kernel, out_shape=(TURNED, jax.ShapeDtypeStruct((T...  10.1 us
    pallas_call x1, Pallas kernels, apply(): pl.pallas_call(apply_kernel, out_shape=MESSAGES, in_specs=[IN_VMEM] * 5,...  5.6 us
    pallas_call x1, Pallas kernels, put_back(): pl.pallas_call(last_kernel, out_shape=jax.ShapeDtypeStruct((FIELDS, ROWS,...  5.58 us
  transfers between devices with their start and end apart: 2, of which 2 were waited for; matrix products, arithmetic and copies ran while one was open for 0% of the time, Pallas kernels for 0%

profile of v5, /device:TPU:0, one launch (start us, length us, event | category | flops | bytes accessed | tf_op | source)
XLA Modules:
  0.0 160.0 jit_solution(4940427885109007736)
XLA Ops:
  0.0 0.0 copy-start
  0.0 1.1 dynamic-slice_bitcast_fusion
  1.1 0.1 collective-permute-start
  1.8 0.0 copy-done
  1.9 1.1 collective-permute-done.halo_ref
  2.9 29.6 %forecast.1 = (bf16[64,208,128]{2,1,0:T(8,128)(2,1)S(1)}, f32[1,128]{1,0:T(1,128)S(1)}) custom-call(s32[1]{0:T(128)} %bitcast.role_ref, f32[1]{0:T(128)S(6)} %copy.10.climate_ref, bf16[69,64,384]{2,1,0:T(8,128)(2,1)} %bitcast.8, bf16[69,8,384]{2,1,0:T(8,128)(2,1)S(1)} %collective-permute-done.halo_ref, f32[1,69]{1,0:T(1,128)} %bitcast.11, ...), custom_call_target="tpu_custom_call" | custom-call | flops 25769803776 | bytes 7340032 | tf_op jit(solution)/shard_map/forecast/pallas_call | solution.py:424
  32.5 0.0 copy-start.1
  32.5 0.0 copy-start.2
  32.5 55.5 %all_to_all.10.g_ref = bf16[64,208,128]{2,1,0:T(8,128)(2,1)S(1)} all-to-all(bf16[64,208,128]{2,1,0:T(8,128)(2,1)S(1)} %get-tuple-element.15), channel_id=1, replica_groups=mesh['role'=2,'dev'=64] {'dev'}, dimensions={0} | all-to-all | bytes 6815744 | tf_op jit(solution)/shard_map/all_to_all | solution.py:488
  88.1 0.0 copy-done.1
  88.1 0.0 copy-done.2
  88.1 10.1 %weights.1 = (bf16[208,64,128]{2,1,0:T(8,128)(2,1)S(1)}, bf16[3,64,128]{2,1,0:T(8,128)(2,1)S(1)}, f32[1,1]{1,0:T(1,128)}) custom-call(s32[6,128]{1,0:T(8,128)S(1)} %constant_dynamic-slice_fusion.idx_ref, f32[6,128]{1,0:T(8,128)S(1)} %copy-done.1, f32[6,128]{1,0:T(8,128)S(1)} %copy-done.2, bf16[64,208,128]{2,1,0:T(8,128)(2,1)S(1)} %all_to_all.10.g_ref), custom_call_target="tpu_custom_call" | custom-call | flops 8589934592 | bytes 7340032 | tf_op jit(solution)/shard_map/weights/pallas_call | solution.py:443
  98.1 0.0 collective-permute-start.1
  98.1 1.2 collective-permute-done.1.other_ref
  99.4 5.6 %apply.1 = bf16[64,208,128]{2,1,0:T(8,128)(2,1)S(1)} custom-call(f32[1,128]{1,0:T(1,128)S(1)} %get-tuple-element.13.climate_ref, f32[1,1]{1,0:T(1,128)} %get-tuple-element.16.total_ref, f32[1,1]{1,0:T(1,128)} %collective-permute-done.1.other_ref, bf16[3,64,128]{2,1,0:T(8,128)(2,1)S(1)} %get-tuple-element.17.mix_ref, ...), custom_call_target="tpu_custom_call" | custom-call | flops 8589934592 | bytes 7340032 | tf_op jit(solution)/shard_map/apply/pallas_call | solution.py:459
  105.0 49.2 %all_to_all.11.back_ref = bf16[64,208,128]{2,1,0:T(8,128)(2,1)S(1)} all-to-all(bf16[64,208,128]{2,1,0:T(8,128)(2,1)S(1)} %apply.1), channel_id=1, replica_groups=mesh['role'=2,'dev'=64] {'dev'}, dimensions={0} | all-to-all | bytes 6815744 | tf_op jit(solution)/shard_map/all_to_all | solution.py:488
  154.2 5.6 %put_back.1 = bf16[69,64,384]{2,1,0:T(8,128)(2,1)} custom-call(bf16[64,208,128]{2,1,0:T(8,128)(2,1)S(1)} %all_to_all.11.back_ref), custom_call_target="tpu_custom_call" | custom-call | flops 1048576 | bytes 7340032 | tf_op jit(solution)/shard_map/put_back/pallas_call | solution.py:472
  (1 shorter events, 0.0 us)
Async XLA Ops:
  0.0 1.8 %copy-start = (s32[384,128]{1,0:T(8,128)S(1)}, s32[384,128]{1,0:T(8,128)}, u32[]{:S(2)}) copy-start(s32[384,128]{1,0:T(8,128)} %param.14) | copy-start | bytes 589828
  1.1 1.8 %collective-permute-start = (bf16[69,8,384]{2,1,0:T(8,128)(2,1)S(1)}, bf16[69,8,384]{2,1,0:T(8,128)(2,1)S(1)}, u32[]{:S(2)}, u32[]{:S(2)}) collective-permute-start(bf16[69,8,384]{2,1,0:T(8,128)(2,1)S(1)} %dynamic-slice_bitcast_fusion), channel_id=1, source_target_pairs={{0,64},{64,0},{1,65},{65,1},{2,66},{66,2},{3,67},{67,3},{4,68},{68... | collective-permute-start | bytes 1271816 | tf_op jit(solution)/shard_map/ppermute | solution.py:499
  32.5 55.6 %copy-start.1 = (f32[6,128]{1,0:T(8,128)S(1)}, f32[6,128]{1,0:T(8,128)}, u32[]{:S(2)}) copy-start(f32[6,128]{1,0:T(8,128)} %value_ref.1) | copy-start | bytes 9220
  32.5 55.6 %copy-start.2 = (f32[6,128]{1,0:T(8,128)S(1)}, f32[6,128]{1,0:T(8,128)}, u32[]{:S(2)}) copy-start(f32[6,128]{1,0:T(8,128)} %weight_ref.1) | copy-start | bytes 9220
  98.1 1.2 collective-permute-start.1

commit v6 on v5

--- a/solution.py
+++ b/solution.py
@@ -62,14 +62,22 @@
             done(n - DEPTH, jnp.dot(w_out, hidden, preferred_element_type=jnp.float32))
 
 
-def swap_groups(rows):
+def choose(rows):
     lane = lax.broadcasted_iota(jnp.int32, rows[0].shape, 1)
-    rows = [pltpu.roll(row, a * GROUP, 1) if a else row for a, row in enumerate(rows)]
     rows = [rows[-p % 8] for p in range(8)]
     for bit in (1, 2, 4):
         move = (lane & (bit * GROUP)) != 0
         rows = [jnp.where(move, rows[(p - bit) % 8], rows[p]) for p in range(8)]
-    return [pltpu.roll(row, LANES - p * GROUP, 1) if p else row for p, row in enumerate(rows)]
+    return rows
+
+
+def to_messages(rows):
+    return choose([pltpu.roll(row, a * GROUP, 1) if a else row for a, row in enumerate(rows)])
+
+
+def to_rows(messages):
+    rows = choose(messages)
+    return [pltpu.roll(row, LANES - a * GROUP, 1) if a else row for a, row in enumerate(rows)]
 
 
 def owner_of(r, tile, group):
@@ -183,7 +191,7 @@
             pieces[k, tile] = new
             if k % 8 == 7:
                 rows = [pieces.pop((k - 7 + a, tile)) for a in range(8)]
-                for group, message in enumerate(swap_groups(rows)):
+                for group, message in enumerate(to_messages(rows)):
                     owner, slot = owner_of(step * 2 + k // 8, tile, group)
                     out_ref[owner, slot * MAIN : (slot + 1) * MAIN, :] = message[:MAIN]
                     rests[owner, slot] = message[MAIN:]
@@ -248,7 +256,7 @@
         turn[:, pl.ds(m, 16), :] = jnp.swapaxes(g_ref[pl.ds(m, 16)], 0, 1)
         return carry
 
-    lax.fori_loop(0, MEMBERS // 16, load, 0, unroll=2)
+    lax.fori_loop(0, MEMBERS // 16, load, 0, unroll=4)
     precisions, pulled = [], []
     for k in range(TILES):
         idx = jnp.concatenate(
@@ -275,7 +283,7 @@
             return total
 
         observed = pick(jnp.zeros((MEMBERS, 2 * OBS), f32), TAIL + k * REST, MAIN, REST)
-        observed = lax.fori_loop(0, MAIN // 32, picks, observed)
+        observed = lax.fori_loop(0, MAIN // 32, picks, observed, unroll=2)
         sides, pulls = [], []
         for e in range(2):
             mine = observed[:, e * OBS : (e + 1) * OBS]
@@ -300,7 +308,9 @@
         new = [pair_dot(streamed(f), r) for f, r in zip(factors, rights)]
         return [n[:, :LANES] for n in new], [n[:, LANES:] for n in new]
 
-    _, roots = lax.fori_loop(0, NS_ITERS, newton, (iterates, [eye] * TILES), unroll=2)
+    factors = [0.5 * (3.0 * eye - i) for i in iterates]
+    iterates = [pair_dot(streamed(f), held(i)) for f, i in zip(factors, iterates)]
+    _, roots = lax.fori_loop(1, NS_ITERS, newton, (iterates, factors), unroll=NS_ITERS - 1)
     shifts = [pair_dot(streamed(r), held(p)) for r, p in zip(roots, pulled)]
     shifts = [pair_dot(streamed(r), held(p)) for r, p in zip(roots, shifts)]
     total = jnp.zeros((1, LANES), f32)
@@ -320,19 +330,11 @@
     total_ref[...] = jnp.sum(total, axis=1, keepdims=True)
 
 
-def apply_kernel(climate_ref, total_ref, other_ref, mix_ref, turn, out_ref, back):
+def apply_kernel(mix_ref, turn, out_ref, back):
     f32, bf16 = jnp.float32, jnp.bfloat16
     even = jnp.where((lax.broadcasted_iota(jnp.int32, (MEMBERS, BLOCK), 1) & EDGE) == 0, 1.0, 0.0)
     even = even.astype(bf16)
     uneven = bf16(1.0) - even
-    total = total_ref[...] + other_ref[...] - climate_ref[...] * (VALUES // MEMBERS)
-    high = total.astype(bf16).astype(f32)
-    middle = (total - high).astype(bf16).astype(f32)
-    lane = lax.broadcasted_iota(jnp.int32, (1, LANES), 1)
-    parts = jnp.where(lane == 0, high, jnp.where(lane == 1, middle, total - high - middle))
-    parts = jnp.where(lane < 3, parts, 0.0)
-    back[MESSAGE - 1] = jnp.broadcast_to(parts, (MEMBERS, LANES)).astype(bf16)
-
     def mixed(k, places):
         x = jnp.concatenate([turn[place] for place in places], axis=1)
         width = len(places) * LANES
@@ -366,7 +368,21 @@
                 give(TAIL, MESSAGE - TAIL, step)
             return carry
 
-        lax.fori_loop(0, 4, both, 0)
+        lax.fori_loop(0, 4, both, 0, unroll=4)
+
+
+def seal_kernel(climate_ref, total_ref, other_ref, messages_ref, out_ref):
+    f32, bf16 = jnp.float32, jnp.bfloat16
+    total = total_ref[...] + other_ref[...] - climate_ref[...] * (VALUES // MEMBERS)
+    high = total.astype(bf16).astype(f32)
+    middle = (total - high).astype(bf16).astype(f32)
+    lane = lax.broadcasted_iota(jnp.int32, (16, LANES), 1)
+    row = lax.broadcasted_iota(jnp.int32, (16, LANES), 0)
+    parts = jnp.where(lane == 0, high, jnp.where(lane == 1, middle, total - high - middle))
+    parts = jnp.where(lane < 3, parts, 0.0)
+    for owner in range(MEMBERS):
+        tail = messages_ref[owner, TAIL:MESSAGE, :].astype(f32)
+        out_ref[owner, TAIL:MESSAGE, :] = jnp.where(row == 15, parts, tail).astype(bf16)
 
 
 def last_kernel(back_ref, out_ref, grid, sems):
@@ -398,7 +414,7 @@
                     for group in range(8):
                         owner, slot = owner_of(step * 2 + half, tile, group)
                         pieces.append(piece(owner, slot, first, count))
-                    rows += swap_groups(pieces)
+                    rows += to_rows(pieces)
                 values = jnp.swapaxes(jnp.stack(rows), 0, 1)
                 place = pl.ds(pl.multiple_of(step * 16, 16), 16)
                 lanes = slice(tile * LANES, (tile + 1) * LANES)
@@ -409,7 +425,7 @@
                     grid[first : first + count, place, lanes] = values
             return carry
 
-        lax.fori_loop(0, ROWS // 16, block, 0)
+        lax.fori_loop(0, ROWS // 16, block, 0, unroll=4)
         send(first, count).start()
     for first, count in chunks:
         send(first, count).wait()
@@ -455,17 +471,30 @@
     )(idx, value, weight, g)
 
 
-def apply(climate, total, other, mixes, turn):
+def apply(mixes, turn):
     return pl.pallas_call(
         apply_kernel,
         out_shape=MESSAGES,
-        in_specs=[IN_VMEM] * 5,
+        in_specs=[IN_VMEM] * 2,
         out_specs=IN_VMEM,
         scratch_shapes=[pltpu.VMEM(TURNED.shape, jnp.bfloat16)],
         compiler_params=params(32),
         cost_estimate=cost(8 << 30, 7 << 20),
         name="apply",
-    )(climate, total, other, mixes, turn)
+    )(mixes, turn)
+
+
+def seal(climate, total, other, messages):
+    return pl.pallas_call(
+        seal_kernel,
+        out_shape=MESSAGES,
+        in_specs=[IN_VMEM] * 4,
+        out_specs=IN_VMEM,
+        input_output_aliases={3: 0},
+        compiler_params=params(32),
+        cost_estimate=cost(1 << 16, 1 << 18),
+        name="seal",
+    )(climate, total, other, messages)
 
 
 def put_back(back):
@@ -495,6 +524,8 @@
     dev = lax.axis_index("dev")
     x = initial_realizations.reshape(FIELDS, ROWS, LON)
     index = lax.dynamic_slice_in_dim(obs_index, dev * PATCHES, PATCHES, 0)
+    group = dev % 8 * 3 + jnp.arange(PATCHES)[:, None] // 2
+    index = (index & ~(CELLS - EDGE)) | ((index + group * EDGE) & (CELLS - EDGE))
     edge = lax.dynamic_slice_in_dim(x, jnp.where(role == 0, ROWS - 8, 0), 8, 1)
     halo = lax.ppermute(edge, "role", [(0, 1), (1, 0)])
     halo, index = lax.optimization_barrier((halo, index))
@@ -504,7 +535,7 @@
     got = exchange(sent)
     turn, mixes, total = weights(index, obs_value, obs_weight, got)
     other = lax.ppermute(total, "role", [(0, 1), (1, 0)])
-    back = exchange(apply(climate, total, other, mixes, turn))
+    back = exchange(seal(climate, total, other, apply(mixes, turn)))
     return put_back(back)[None]
 
 

time: 160 us -> 152 us (0.950)
  Pallas kernels: 50.8 us -> 43.8 us
  waiting for transfers between devices: 2.31 us -> 0.3 us
    pallas_call x1, Pallas kernels: 10.1 us -> 7.69 us  [weights(): pl.pallas_call(weights_kernel, out_shape=(TURNED, jax.ShapeDtypeStruct((T...]
    pallas_call x1, Pallas kernels: 5.58 us -> 3.41 us  [put_back(): pl.pallas_call(last_kernel, out_shape=jax.ShapeDtypeStruct((FIELDS, ROWS,...]
    pallas_call x1 -> x2, Pallas kernels: 5.6 us -> 3.56 us  [the longest x1 2.24 us: apply(): pl.pallas_call(apply_kernel, out_shape=MESSAGES, in_specs=[IN_VMEM] * 2,...]
  transfers between devices with their start and end apart: 2 -> 2, of which waited for: 2 -> 1; matrix products, arithmetic and copies ran while one was open for 0% -> 1% of each run, Pallas kernels for 0% -> 1%
where the time goes in v6:
time: 152 us
  blocking collectives  105 us (69%)
  Pallas kernels  43.8 us (29%)
    all_to_all x2, blocking collectives, exchange(): lax.all_to_all(messages, 'dev', split_axis=0, concat_axis=0, tiled=True)  105 us
    pallas_call x1, Pallas kernels, forecast(): pl.pallas_call(forecast_kernel, out_shape=(MESSAGES, jax.ShapeDtypeStruct...  29.2 us
    pallas_call x1, Pallas kernels, weights(): pl.pallas_call(weights_kernel, out_shape=(TURNED, jax.ShapeDtypeStruct((T...  7.69 us
    pallas_call x1, Pallas kernels, put_back(): pl.pallas_call(last_kernel, out_shape=jax.ShapeDtypeStruct((FIELDS, ROWS,...  3.41 us
  transfers between devices with their start and end apart: 2, of which 1 were waited for; matrix products, arithmetic and copies ran while one was open for 1% of the time, Pallas kernels for 1%

profile of v6, /device:TPU:0, one launch (start us, length us, event | category | flops | bytes accessed | tf_op | source)
XLA Modules:
  0.0 151.6 jit_solution(6542166776887958254)
XLA Ops:
  0.0 1.0 dynamic-slice_bitcast_fusion
  1.1 0.1 collective-permute-start
  1.8 0.8 and_or_fusion.idx_ref
  2.6 0.3 collective-permute-done.halo_ref
  2.9 29.2 %forecast.1 = (bf16[64,208,128]{2,1,0:T(8,128)(2,1)S(1)}, f32[1,128]{1,0:T(1,128)S(1)}) custom-call(s32[1]{0:T(128)} %bitcast.role_ref, f32[1]{0:T(128)S(6)} %copy.12.climate_ref, bf16[69,64,384]{2,1,0:T(8,128)(2,1)} %bitcast.8, bf16[69,8,384]{2,1,0:T(8,128)(2,1)S(1)} %collective-permute-done.halo_ref, f32[1,69]{1,0:T(1,128)} %bitcast.11, ...), custom_call_target="tpu_custom_call" | custom-call | flops 25769803776 | bytes 7340032 | tf_op jit(solution)/shard_map/forecast/pallas_call | solution.py:440
  32.1 0.0 copy-start
  32.1 0.0 copy-start.1
  32.1 55.6 %all_to_all.10.g_ref = bf16[64,208,128]{2,1,0:T(8,128)(2,1)S(1)} all-to-all(bf16[64,208,128]{2,1,0:T(8,128)(2,1)S(1)} %get-tuple-element.15), channel_id=1, replica_groups=mesh['role'=2,'dev'=64] {'dev'}, dimensions={0} | all-to-all | bytes 6815744 | tf_op jit(solution)/shard_map/all_to_all | solution.py:517
  87.7 0.0 copy-done
  87.7 0.0 copy-done.1
  87.7 7.7 %weights.1 = (bf16[208,64,128]{2,1,0:T(8,128)(2,1)S(1)}, bf16[3,64,128]{2,1,0:T(8,128)(2,1)S(1)}, f32[1,1]{1,0:T(1,128)}) custom-call(s32[6,128]{1,0:T(8,128)S(1)} %and_or_fusion.idx_ref, f32[6,128]{1,0:T(8,128)S(1)} %copy-done, f32[6,128]{1,0:T(8,128)S(1)} %copy-done.1, bf16[64,208,128]{2,1,0:T(8,128)(2,1)S(1)} %all_to_all.10.g_ref), custom_call_target="tpu_custom_call" | custom-call | flops 8589934592 | bytes 7340032 | tf_op jit(solution)/shard_map/weights/pallas_call | solution.py:459
  95.4 0.0 collective-permute-start.1
  95.4 2.2 %apply.1.messages_ref = bf16[64,208,128]{2,1,0:T(8,128)(2,1)S(1)} custom-call(bf16[3,64,128]{2,1,0:T(8,128)(2,1)S(1)} %get-tuple-element.17.mix_ref, bf16[208,64,128]{2,1,0:T(8,128)(2,1)S(1)} %get-tuple-element.18.turn), custom_call_target="tpu_custom_call" | custom-call | flops 8589934592 | bytes 7340032 | tf_op jit(solution)/shard_map/apply/pallas_call | solution.py:475
  97.6 0.0 collective-permute-done.1.other_ref
  97.6 1.3 seal.1
  99.0 49.1 %all_to_all.11.back_ref = bf16[64,208,128]{2,1,0:T(8,128)(2,1)S(1)} all-to-all(bf16[64,208,128]{2,1,0:T(8,128)(2,1)S(1)} %seal.1), channel_id=1, replica_groups=mesh['role'=2,'dev'=64] {'dev'}, dimensions={0} | all-to-all | bytes 6815744 | tf_op jit(solution)/shard_map/all_to_all | solution.py:517
  148.1 3.4 %put_back.1 = bf16[69,64,384]{2,1,0:T(8,128)(2,1)} custom-call(bf16[64,208,128]{2,1,0:T(8,128)(2,1)S(1)} %all_to_all.11.back_ref), custom_call_target="tpu_custom_call" | custom-call | flops 1048576 | bytes 7340032 | tf_op jit(solution)/shard_map/put_back/pallas_call | solution.py:501
  (1 shorter events, 0.0 us)
Async XLA Ops:
  1.1 1.8 %collective-permute-start = (bf16[69,8,384]{2,1,0:T(8,128)(2,1)S(1)}, bf16[69,8,384]{2,1,0:T(8,128)(2,1)S(1)}, u32[]{:S(2)}, u32[]{:S(2)}) collective-permute-start(bf16[69,8,384]{2,1,0:T(8,128)(2,1)S(1)} %dynamic-slice_bitcast_fusion), channel_id=1, source_target_pairs={{0,64},{64,0},{1,65},{65,1},{2,66},{66,2},{3,67},{67,3},{4,68},{68... | collective-permute-start | bytes 1271816 | tf_op jit(solution)/shard_map/ppermute | solution.py:530
  32.1 55.6 %copy-start = (f32[6,128]{1,0:T(8,128)S(1)}, f32[6,128]{1,0:T(8,128)}, u32[]{:S(2)}) copy-start(f32[6,128]{1,0:T(8,128)} %value_ref.1) | copy-start | bytes 9220
  32.1 55.6 %copy-start.1 = (f32[6,128]{1,0:T(8,128)S(1)}, f32[6,128]{1,0:T(8,128)}, u32[]{:S(2)}) copy-start(f32[6,128]{1,0:T(8,128)} %weight_ref.1) | copy-start | bytes 9220
  95.4 2.2 %collective-permute-start.1 = (f32[1,1]{1,0:T(1,128)}, f32[1,1]{1,0:T(1,128)}, u32[]{:S(2)}, u32[]{:S(2)}) collective-permute-start(f32[1,1]{1,0:T(1,128)} %get-tuple-element.16.total_ref), channel_id=1, source_target_pairs={{0,64},{64,0},{1,65},{65,1},{2,66},{66,2},{3,67},{67,3},{4,68},{68... | collective-permute-start | bytes 20 | tf_op jit(solution)/shard_map/ppermute | solution.py:537

commit v7 on v6

--- a/solution.py
+++ b/solution.py
@@ -87,7 +87,7 @@
 
 def forecast_kernel(
     role_ref, climate_ref, x_ref, halo_ref, diff_ref, w_in_ref, b_in_ref, w_out_ref,
-    out_ref, climate_out, own, before, after, rests, in_sems,
+    out_ref, climate_out, own, before, after, rests, in_sems, first_sems,
 ):
     f32, bf16 = jnp.float32, jnp.bfloat16
     role = role_ref[0]
@@ -96,8 +96,15 @@
         rows = pl.ds(step * 16, 16)
         return pltpu.make_async_copy(x_ref.at[:, rows, :], own.at[:, rows, :], in_sems.at[step])
 
-    for step in range(ROWS // 16):
-        fetch(step).start()
+    def fetch_first(part):
+        fields = pl.ds(part * (FIELDS // 3), FIELDS // 3)
+        rows = pl.ds(0, 16)
+        return pltpu.make_async_copy(
+            x_ref.at[fields, rows, :], own.at[fields, rows, :], first_sems.at[part]
+        )
+
+    for part in range(3):
+        fetch_first(part).start()
     climate_out[...] = jnp.full((1, LANES), climate_ref[0], f32)
 
     def turned(block):
@@ -110,11 +117,8 @@
     before[pl.ds(jnp.where(role == 0, 72, 0), 8)] = turned(halo_ref[...])
 
     def take(step):
-        fetch(step).wait()
         place = pl.multiple_of(step * 16, 16)
         before[pl.ds(8 + place, 16)] = turned(own[:, pl.ds(place, 16), :])
-
-    take(0)
 
     diff = jnp.concatenate([diff_ref[...], jnp.zeros((1, LANES - FIELDS), f32)], axis=1)
     diff = jnp.broadcast_to(diff, (LANES, LANES)).T[:PADDED]
@@ -129,6 +133,12 @@
         [w_out_ref[...] * bf16(0.5), jnp.zeros((PADDED - FIELDS, LATENT), bf16)], axis=0
     )
 
+    for part in range(3):
+        fetch_first(part).wait()
+    for step in range(1, ROWS // 16):
+        fetch(step).start()
+    take(0)
+
     def advance(ref, place, count, give):
         rows, smooth = {}, {}
 
@@ -169,6 +179,7 @@
 
         @pl.when(step < ROWS // 16 - 1)
         def _():
+            fetch(step + 1).wait()
             take(step + 1)
 
         return carry
@@ -320,7 +331,8 @@
         rest = (1.0 - jnp.sum(combined, axis=0, keepdims=True)) * (1.0 / MEMBERS)
         mix = combined + rest
         across = mix.T
-        mix_ref[k] = jnp.concatenate([across[:MEMBERS], across[MEMBERS:]], axis=1).astype(bf16)
+        across = jnp.concatenate([across[:MEMBERS], across[MEMBERS:]], axis=1)
+        mix_ref[k] = jnp.concatenate(split(across), axis=1)
         shares = jnp.where(
             odd_cell,
             jnp.sum(jnp.where(low, 0.0, mix), axis=1, keepdims=True),
@@ -339,6 +351,7 @@
         x = jnp.concatenate([turn[place] for place in places], axis=1)
         width = len(places) * LANES
         x = jnp.concatenate([x * even[:, :width], x * uneven[:, :width]], axis=0)
+        x = jnp.concatenate([x, x], axis=0)
         new = jnp.dot(mix_ref[k], x, preferred_element_type=f32).astype(bf16)
         for n, place in enumerate(places):
             back[place] = new[:, n * LANES : (n + 1) * LANES]
@@ -448,6 +461,7 @@
             pltpu.VMEM((ROWS + 2, PADDED, LON), jnp.bfloat16),
             pltpu.VMEM((MEMBERS, TILES, PADDED - MAIN, LANES), jnp.bfloat16),
             pltpu.SemaphoreType.DMA((ROWS // 16,)),
+            pltpu.SemaphoreType.DMA((3,)),
         ],
         compiler_params=params(32),
         cost_estimate=cost(cells * LATENT * 256 * 4, 7 << 20, cells * LATENT),
@@ -460,7 +474,7 @@
         weights_kernel,
         out_shape=(
             TURNED,
-            jax.ShapeDtypeStruct((TILES, MEMBERS, LANES), jnp.bfloat16),
+            jax.ShapeDtypeStruct((TILES, MEMBERS, 2 * LANES), jnp.bfloat16),
             jax.ShapeDtypeStruct((1, 1), jnp.float32),
         ),
         in_specs=[IN_VMEM] * 4,

time: 152 us -> 152 us (level)
  transfers between devices with their start and end apart: 2 -> 2, of which waited for: 1 -> 1; matrix products, arithmetic and copies ran while one was open for 1% -> 1% of each run, Pallas kernels for 1% -> 2%
where the time goes in v7:
time: 152 us
  blocking collectives  105 us (69%)
  Pallas kernels  43.8 us (29%)
    all_to_all x2, blocking collectives, exchange(): lax.all_to_all(messages, 'dev', split_axis=0, concat_axis=0, tiled=True)  105 us
    pallas_call x1, Pallas kernels, forecast(): pl.pallas_call(forecast_kernel, out_shape=(MESSAGES, jax.ShapeDtypeStruct...  29 us
    pallas_call x1, Pallas kernels, weights(): pl.pallas_call(weights_kernel, out_shape=(TURNED, jax.ShapeDtypeStruct((T...  7.78 us
    pallas_call x1, Pallas kernels, put_back(): pl.pallas_call(last_kernel, out_shape=jax.ShapeDtypeStruct((FIELDS, ROWS,...  3.41 us
  transfers between devices with their start and end apart: 2, of which 1 were waited for; matrix products, arithmetic and copies ran while one was open for 1% of the time, Pallas kernels for 2%

profile of v7, /device:TPU:0, one launch (start us, length us, event | category | flops | bytes accessed | tf_op | source)
XLA Modules:
  0.0 151.6 jit_solution(13049457776885907636)
XLA Ops:
  0.0 1.0 dynamic-slice_bitcast_fusion
  1.1 0.1 collective-permute-start
  1.8 0.8 and_or_fusion.idx_ref
  2.6 0.3 collective-permute-done.halo_ref
  2.9 29.0 %forecast.1 = (bf16[64,208,128]{2,1,0:T(8,128)(2,1)S(1)}, f32[1,128]{1,0:T(1,128)S(1)}) custom-call(s32[1]{0:T(128)} %bitcast.role_ref, f32[1]{0:T(128)S(6)} %copy.12.climate_ref, bf16[69,64,384]{2,1,0:T(8,128)(2,1)} %bitcast.8, bf16[69,8,384]{2,1,0:T(8,128)(2,1)S(1)} %collective-permute-done.halo_ref, f32[1,69]{1,0:T(1,128)} %bitcast.11, ...), custom_call_target="tpu_custom_call" | custom-call | flops 25769803776 | bytes 7340032 | tf_op jit(solution)/shard_map/forecast/pallas_call | solution.py:453
  31.9 0.0 copy-start
  31.9 0.0 copy-start.1
  31.9 55.6 %all_to_all.10.g_ref = bf16[64,208,128]{2,1,0:T(8,128)(2,1)S(1)} all-to-all(bf16[64,208,128]{2,1,0:T(8,128)(2,1)S(1)} %get-tuple-element.15), channel_id=1, replica_groups=mesh['role'=2,'dev'=64] {'dev'}, dimensions={0} | all-to-all | bytes 6815744 | tf_op jit(solution)/shard_map/all_to_all | solution.py:531
  87.5 0.0 copy-done
  87.5 0.0 copy-done.1
  87.5 7.8 %weights.1 = (bf16[208,64,128]{2,1,0:T(8,128)(2,1)S(1)}, bf16[3,64,256]{2,1,0:T(8,128)(2,1)S(1)}, f32[1,1]{1,0:T(1,128)}) custom-call(s32[6,128]{1,0:T(8,128)S(1)} %and_or_fusion.idx_ref, f32[6,128]{1,0:T(8,128)S(1)} %copy-done, f32[6,128]{1,0:T(8,128)S(1)} %copy-done.1, bf16[64,208,128]{2,1,0:T(8,128)(2,1)S(1)} %all_to_all.10.g_ref), custom_call_target="tpu_custom_call" | custom-call | flops 8589934592 | bytes 7340032 | tf_op jit(solution)/shard_map/weights/pallas_call | solution.py:473
  95.3 0.0 collective-permute-start.1
  95.3 2.3 %apply.1.messages_ref = bf16[64,208,128]{2,1,0:T(8,128)(2,1)S(1)} custom-call(bf16[3,64,256]{2,1,0:T(8,128)(2,1)S(1)} %get-tuple-element.17.mix_ref, bf16[208,64,128]{2,1,0:T(8,128)(2,1)S(1)} %get-tuple-element.18.turn), custom_call_target="tpu_custom_call" | custom-call | flops 8589934592 | bytes 7340032 | tf_op jit(solution)/shard_map/apply/pallas_call | solution.py:489
  97.6 0.0 collective-permute-done.1.other_ref
  97.6 1.3 seal.1
  99.0 49.1 %all_to_all.11.back_ref = bf16[64,208,128]{2,1,0:T(8,128)(2,1)S(1)} all-to-all(bf16[64,208,128]{2,1,0:T(8,128)(2,1)S(1)} %seal.1), channel_id=1, replica_groups=mesh['role'=2,'dev'=64] {'dev'}, dimensions={0} | all-to-all | bytes 6815744 | tf_op jit(solution)/shard_map/all_to_all | solution.py:531
  148.1 3.4 %put_back.1 = bf16[69,64,384]{2,1,0:T(8,128)(2,1)} custom-call(bf16[64,208,128]{2,1,0:T(8,128)(2,1)S(1)} %all_to_all.11.back_ref), custom_call_target="tpu_custom_call" | custom-call | flops 1048576 | bytes 7340032 | tf_op jit(solution)/shard_map/put_back/pallas_call | solution.py:515
  (1 shorter events, 0.0 us)
Async XLA Ops:
  1.1 1.8 %collective-permute-start = (bf16[69,8,384]{2,1,0:T(8,128)(2,1)S(1)}, bf16[69,8,384]{2,1,0:T(8,128)(2,1)S(1)}, u32[]{:S(2)}, u32[]{:S(2)}) collective-permute-start(bf16[69,8,384]{2,1,0:T(8,128)(2,1)S(1)} %dynamic-slice_bitcast_fusion), channel_id=1, source_target_pairs={{0,64},{64,0},{1,65},{65,1},{2,66},{66,2},{3,67},{67,3},{4,68},{68... | collective-permute-start | bytes 1271816 | tf_op jit(solution)/shard_map/ppermute | solution.py:544
  31.9 55.6 %copy-start = (f32[6,128]{1,0:T(8,128)S(1)}, f32[6,128]{1,0:T(8,128)}, u32[]{:S(2)}) copy-start(f32[6,128]{1,0:T(8,128)} %value_ref.1) | copy-start | bytes 9220
  31.9 55.6 %copy-start.1 = (f32[6,128]{1,0:T(8,128)S(1)}, f32[6,128]{1,0:T(8,128)}, u32[]{:S(2)}) copy-start(f32[6,128]{1,0:T(8,128)} %weight_ref.1) | copy-start | bytes 9220
  95.3 2.3 %collective-permute-start.1 = (f32[1,1]{1,0:T(1,128)}, f32[1,1]{1,0:T(1,128)}, u32[]{:S(2)}, u32[]{:S(2)}) collective-permute-start(f32[1,1]{1,0:T(1,128)} %get-tuple-element.16.total_ref), channel_id=1, source_target_pairs={{0,64},{64,0},{1,65},{65,1},{2,66},{66,2},{3,67},{67,3},{4,68},{68... | collective-permute-start | bytes 20 | tf_op jit(solution)/shard_map/ppermute | solution.py:551

commit v8 on v7

--- a/solution.py
+++ b/solution.py
@@ -275,26 +275,30 @@
         )
         cell = idx & (CELLS - 1)
         place = (cell >> 3) * GROUP + odd + (cell & 7)
-        field = jnp.broadcast_to(idx >> 6, (MEMBERS, 2 * OBS))
+        field = idx >> 6
         hot = jnp.where(lax.broadcasted_iota(jnp.int32, (LANES, 2 * OBS), 0) == place, 1.0, 0.0)
-        hot = hot.astype(bf16)
-
-        def pick(total, start, first, count):
-            block = turn[pl.ds(start, count)].reshape(count * MEMBERS, LANES)
-            values = jnp.dot(block, hot, preferred_element_type=f32)
+        late = (field & 32) != 0
+        both = jnp.concatenate([jnp.where(late, 0.0, hot), jnp.where(late, hot, 0.0)], axis=0)
+        hot, both = hot.astype(bf16), both.astype(bf16)
+        rest = jnp.broadcast_to(field - MAIN, (MEMBERS, 2 * OBS))
+        main = jnp.broadcast_to(jnp.where(field < MAIN, field & 31, -1), (MEMBERS, 2 * OBS))
+
+        def flat(start, count):
+            return turn[start : start + count].reshape(count * MEMBERS, LANES)
+
+        def pick(total, values, wanted, first, count):
             for f in range(count):
-                here = field == first + f
+                here = wanted == first + f
                 total = jnp.where(here, values[f * MEMBERS : (f + 1) * MEMBERS], total)
             return total
 
-        def picks(step, total):
-            for part in range(4):
-                first = step * 32 + part * 8
-                total = pick(total, k * MAIN + first, first, 8)
-            return total
-
-        observed = pick(jnp.zeros((MEMBERS, 2 * OBS), f32), TAIL + k * REST, MAIN, REST)
-        observed = lax.fori_loop(0, MAIN // 32, picks, observed, unroll=2)
+        values = jnp.dot(flat(TAIL + k * REST, REST), hot, preferred_element_type=f32)
+        observed = pick(jnp.zeros((MEMBERS, 2 * OBS), f32), values, rest, 0, REST)
+        for first in range(0, 32, 8):
+            start = k * MAIN + first
+            block = jnp.concatenate([flat(start, 8), flat(start + 32, 8)], axis=1)
+            values = jnp.dot(block, both, preferred_element_type=f32)
+            observed = pick(observed, values, main, first, 8)
         sides, pulls = [], []
         for e in range(2):
             mine = observed[:, e * OBS : (e + 1) * OBS]
@@ -392,10 +396,10 @@
     lane = lax.broadcasted_iota(jnp.int32, (16, LANES), 1)
     row = lax.broadcasted_iota(jnp.int32, (16, LANES), 0)
     parts = jnp.where(lane == 0, high, jnp.where(lane == 1, middle, total - high - middle))
-    parts = jnp.where(lane < 3, parts, 0.0)
+    parts = jnp.where(lane < 3, parts, 0.0).astype(bf16)
     for owner in range(MEMBERS):
-        tail = messages_ref[owner, TAIL:MESSAGE, :].astype(f32)
-        out_ref[owner, TAIL:MESSAGE, :] = jnp.where(row == 15, parts, tail).astype(bf16)
+        tail = messages_ref[owner, TAIL:MESSAGE, :]
+        out_ref[owner, TAIL:MESSAGE, :] = jnp.where(row == 15, parts, tail)
 
 
 def last_kernel(back_ref, out_ref, grid, sems):

time: 152 us -> 152 us (level)
  no operation moved by 1% of the time
where the time goes in v8:
time: 152 us; the launch traced here: 151 us
  blocking collectives  105 us (69%)
  Pallas kernels  43.3 us (28%)
    all_to_all x2, blocking collectives, exchange(): lax.all_to_all(messages, 'dev', split_axis=0, concat_axis=0, tiled=True)  105 us
    pallas_call x1, Pallas kernels, forecast(): pl.pallas_call(forecast_kernel, out_shape=(MESSAGES, jax.ShapeDtypeStruct...  29 us
    pallas_call x1, Pallas kernels, weights(): pl.pallas_call(weights_kernel, out_shape=(TURNED, jax.ShapeDtypeStruct((T...  7.26 us
    pallas_call x1, Pallas kernels, put_back(): pl.pallas_call(last_kernel, out_shape=jax.ShapeDtypeStruct((FIELDS, ROWS,...  3.41 us
  transfers between devices with their start and end apart: 2, of which 1 were waited for; matrix products, arithmetic and copies ran while one was open for 1% of the time, Pallas kernels for 2%

profile of v8, /device:TPU:0, one launch (start us, length us, event | category | flops | bytes accessed | tf_op | source)
XLA Modules:
  0.0 151.1 jit_solution(1315053923656838571)
XLA Ops:
  0.0 1.0 dynamic-slice_bitcast_fusion
  1.1 0.1 collective-permute-start
  1.8 0.8 and_or_fusion.idx_ref
  2.6 0.3 collective-permute-done.halo_ref
  2.9 29.0 %forecast.1 = (bf16[64,208,128]{2,1,0:T(8,128)(2,1)S(1)}, f32[1,128]{1,0:T(1,128)S(1)}) custom-call(s32[1]{0:T(128)} %bitcast.role_ref, f32[1]{0:T(128)S(6)} %copy.12.climate_ref, bf16[69,64,384]{2,1,0:T(8,128)(2,1)} %bitcast.8, bf16[69,8,384]{2,1,0:T(8,128)(2,1)S(1)} %collective-permute-done.halo_ref, f32[1,69]{1,0:T(1,128)} %bitcast.11, ...), custom_call_target="tpu_custom_call" | custom-call | flops 25769803776 | bytes 7340032 | tf_op jit(solution)/shard_map/forecast/pallas_call | solution.py:457
  31.9 0.0 copy-start
  31.9 0.0 copy-start.1
  31.9 55.6 %all_to_all.10.g_ref = bf16[64,208,128]{2,1,0:T(8,128)(2,1)S(1)} all-to-all(bf16[64,208,128]{2,1,0:T(8,128)(2,1)S(1)} %get-tuple-element.15), channel_id=1, replica_groups=mesh['role'=2,'dev'=64] {'dev'}, dimensions={0} | all-to-all | bytes 6815744 | tf_op jit(solution)/shard_map/all_to_all | solution.py:535
  87.5 0.0 copy-done
  87.5 0.0 copy-done.1
  87.5 7.3 %weights.1 = (bf16[208,64,128]{2,1,0:T(8,128)(2,1)S(1)}, bf16[3,64,256]{2,1,0:T(8,128)(2,1)S(1)}, f32[1,1]{1,0:T(1,128)}) custom-call(s32[6,128]{1,0:T(8,128)S(1)} %and_or_fusion.idx_ref, f32[6,128]{1,0:T(8,128)S(1)} %copy-done, f32[6,128]{1,0:T(8,128)S(1)} %copy-done.1, bf16[64,208,128]{2,1,0:T(8,128)(2,1)S(1)} %all_to_all.10.g_ref), custom_call_target="tpu_custom_call" | custom-call | flops 8589934592 | bytes 7340032 | tf_op jit(solution)/shard_map/weights/pallas_call | solution.py:477
  94.8 0.0 collective-permute-start.1
  94.8 2.3 %apply.1.messages_ref = bf16[64,208,128]{2,1,0:T(8,128)(2,1)S(1)} custom-call(bf16[3,64,256]{2,1,0:T(8,128)(2,1)S(1)} %get-tuple-element.17.mix_ref, bf16[208,64,128]{2,1,0:T(8,128)(2,1)S(1)} %get-tuple-element.18.turn), custom_call_target="tpu_custom_call" | custom-call | flops 8589934592 | bytes 7340032 | tf_op jit(solution)/shard_map/apply/pallas_call | solution.py:493
  97.1 0.0 collective-permute-done.1.other_ref
  97.1 1.4 seal.1
  98.5 49.1 %all_to_all.11.back_ref = bf16[64,208,128]{2,1,0:T(8,128)(2,1)S(1)} all-to-all(bf16[64,208,128]{2,1,0:T(8,128)(2,1)S(1)} %seal.1), channel_id=1, replica_groups=mesh['role'=2,'dev'=64] {'dev'}, dimensions={0} | all-to-all | bytes 6815744 | tf_op jit(solution)/shard_map/all_to_all | solution.py:535
  147.6 3.4 %put_back.1 = bf16[69,64,384]{2,1,0:T(8,128)(2,1)} custom-call(bf16[64,208,128]{2,1,0:T(8,128)(2,1)S(1)} %all_to_all.11.back_ref), custom_call_target="tpu_custom_call" | custom-call | flops 1048576 | bytes 7340032 | tf_op jit(solution)/shard_map/put_back/pallas_call | solution.py:519
  (1 shorter events, 0.0 us)
Async XLA Ops:
  1.1 1.8 %collective-permute-start = (bf16[69,8,384]{2,1,0:T(8,128)(2,1)S(1)}, bf16[69,8,384]{2,1,0:T(8,128)(2,1)S(1)}, u32[]{:S(2)}, u32[]{:S(2)}) collective-permute-start(bf16[69,8,384]{2,1,0:T(8,128)(2,1)S(1)} %dynamic-slice_bitcast_fusion), channel_id=1, source_target_pairs={{0,64},{64,0},{1,65},{65,1},{2,66},{66,2},{3,67},{67,3},{4,68},{68... | collective-permute-start | bytes 1271816 | tf_op jit(solution)/shard_map/ppermute | solution.py:548
  31.9 55.6 %copy-start = (f32[6,128]{1,0:T(8,128)S(1)}, f32[6,128]{1,0:T(8,128)}, u32[]{:S(2)}) copy-start(f32[6,128]{1,0:T(8,128)} %value_ref.1) | copy-start | bytes 9220
  31.9 55.6 %copy-start.1 = (f32[6,128]{1,0:T(8,128)S(1)}, f32[6,128]{1,0:T(8,128)}, u32[]{:S(2)}) copy-start(f32[6,128]{1,0:T(8,128)} %weight_ref.1) | copy-start | bytes 9220
  94.8 2.3 %collective-permute-start.1 = (f32[1,1]{1,0:T(1,128)}, f32[1,1]{1,0:T(1,128)}, u32[]{:S(2)}, u32[]{:S(2)}) collective-permute-start(f32[1,1]{1,0:T(1,128)} %get-tuple-element.16.total_ref), channel_id=1, source_target_pairs={{0,64},{64,0},{1,65},{65,1},{2,66},{66,2},{3,67},{67,3},{4,68},{68... | collective-permute-start | bytes 20 | tf_op jit(solution)/shard_map/ppermute | solution.py:555

commit v9 on v8

--- a/solution.py
+++ b/solution.py
@@ -325,7 +325,12 @@
 
     factors = [0.5 * (3.0 * eye - i) for i in iterates]
     iterates = [pair_dot(streamed(f), held(i)) for f, i in zip(factors, iterates)]
-    _, roots = lax.fori_loop(1, NS_ITERS, newton, (iterates, factors), unroll=NS_ITERS - 1)
+    iterates, roots = lax.fori_loop(
+        1, NS_ITERS - 1, newton, (iterates, factors), unroll=NS_ITERS - 2
+    )
+    products = [pair_dot(streamed(r), held(i)) for r, i in zip(roots, iterates)]
+    factors = [0.5 * (3.0 * eye - p) for p in products]
+    roots = [pair_dot(streamed(f), held(r)) for f, r in zip(factors, roots)]
     shifts = [pair_dot(streamed(r), held(p)) for r, p in zip(roots, pulled)]
     shifts = [pair_dot(streamed(r), held(p)) for r, p in zip(roots, shifts)]
     total = jnp.zeros((1, LANES), f32)

time: 152 us -> 151 us (level)
  no operation moved by 1% of the time
where the time goes in v9:
time: 151 us
  blocking collectives  105 us (70%)
  Pallas kernels  43.3 us (29%)
    all_to_all x2, blocking collectives, exchange(): lax.all_to_all(messages, 'dev', split_axis=0, concat_axis=0, tiled=True)  105 us
    pallas_call x1, Pallas kernels, forecast(): pl.pallas_call(forecast_kernel, out_shape=(MESSAGES, jax.ShapeDtypeStruct...  29 us
    pallas_call x1, Pallas kernels, weights(): pl.pallas_call(weights_kernel, out_shape=(TURNED, jax.ShapeDtypeStruct((T...  7.23 us
    pallas_call x1, Pallas kernels, put_back(): pl.pallas_call(last_kernel, out_shape=jax.ShapeDtypeStruct((FIELDS, ROWS,...  3.41 us
  transfers between devices with their start and end apart: 2, of which 1 were waited for; matrix products, arithmetic and copies ran while one was open for 1% of the time, Pallas kernels for 2%

profile of v9, /device:TPU:0, one launch (start us, length us, event | category | flops | bytes accessed | tf_op | source)
XLA Modules:
  0.0 151.1 jit_solution(875863776297800028)
XLA Ops:
  0.0 1.0 dynamic-slice_bitcast_fusion
  1.1 0.1 collective-permute-start
  1.8 0.8 and_or_fusion.idx_ref
  2.6 0.3 collective-permute-done.halo_ref
  2.9 29.0 %forecast.1 = (bf16[64,208,128]{2,1,0:T(8,128)(2,1)S(1)}, f32[1,128]{1,0:T(1,128)S(1)}) custom-call(s32[1]{0:T(128)} %bitcast.role_ref, f32[1]{0:T(128)S(6)} %copy.12.climate_ref, bf16[69,64,384]{2,1,0:T(8,128)(2,1)} %bitcast.8, bf16[69,8,384]{2,1,0:T(8,128)(2,1)S(1)} %collective-permute-done.halo_ref, f32[1,69]{1,0:T(1,128)} %bitcast.11, ...), custom_call_target="tpu_custom_call" | custom-call | flops 25769803776 | bytes 7340032 | tf_op jit(solution)/shard_map/forecast/pallas_call | solution.py:462
  31.9 0.0 copy-start
  31.9 0.0 copy-start.1
  31.9 55.6 %all_to_all.10.g_ref = bf16[64,208,128]{2,1,0:T(8,128)(2,1)S(1)} all-to-all(bf16[64,208,128]{2,1,0:T(8,128)(2,1)S(1)} %get-tuple-element.15), channel_id=1, replica_groups=mesh['role'=2,'dev'=64] {'dev'}, dimensions={0} | all-to-all | bytes 6815744 | tf_op jit(solution)/shard_map/all_to_all | solution.py:540
  87.5 0.0 copy-done
  87.5 0.0 copy-done.1
  87.5 7.2 %weights.1 = (bf16[208,64,128]{2,1,0:T(8,128)(2,1)S(1)}, bf16[3,64,256]{2,1,0:T(8,128)(2,1)S(1)}, f32[1,1]{1,0:T(1,128)}) custom-call(s32[6,128]{1,0:T(8,128)S(1)} %and_or_fusion.idx_ref, f32[6,128]{1,0:T(8,128)S(1)} %copy-done, f32[6,128]{1,0:T(8,128)S(1)} %copy-done.1, bf16[64,208,128]{2,1,0:T(8,128)(2,1)S(1)} %all_to_all.10.g_ref), custom_call_target="tpu_custom_call" | custom-call | flops 8589934592 | bytes 7340032 | tf_op jit(solution)/shard_map/weights/pallas_call | solution.py:482
  94.8 0.0 collective-permute-start.1
  94.8 2.3 %apply.1.messages_ref = bf16[64,208,128]{2,1,0:T(8,128)(2,1)S(1)} custom-call(bf16[3,64,256]{2,1,0:T(8,128)(2,1)S(1)} %get-tuple-element.17.mix_ref, bf16[208,64,128]{2,1,0:T(8,128)(2,1)S(1)} %get-tuple-element.18.turn), custom_call_target="tpu_custom_call" | custom-call | flops 8589934592 | bytes 7340032 | tf_op jit(solution)/shard_map/apply/pallas_call | solution.py:498
  97.1 0.0 collective-permute-done.1.other_ref
  97.1 1.4 seal.1
  98.5 49.1 %all_to_all.11.back_ref = bf16[64,208,128]{2,1,0:T(8,128)(2,1)S(1)} all-to-all(bf16[64,208,128]{2,1,0:T(8,128)(2,1)S(1)} %seal.1), channel_id=1, replica_groups=mesh['role'=2,'dev'=64] {'dev'}, dimensions={0} | all-to-all | bytes 6815744 | tf_op jit(solution)/shard_map/all_to_all | solution.py:540
  147.5 3.4 %put_back.1 = bf16[69,64,384]{2,1,0:T(8,128)(2,1)} custom-call(bf16[64,208,128]{2,1,0:T(8,128)(2,1)S(1)} %all_to_all.11.back_ref), custom_call_target="tpu_custom_call" | custom-call | flops 1048576 | bytes 7340032 | tf_op jit(solution)/shard_map/put_back/pallas_call | solution.py:524
  (1 shorter events, 0.0 us)
Async XLA Ops:
  1.1 1.8 %collective-permute-start = (bf16[69,8,384]{2,1,0:T(8,128)(2,1)S(1)}, bf16[69,8,384]{2,1,0:T(8,128)(2,1)S(1)}, u32[]{:S(2)}, u32[]{:S(2)}) collective-permute-start(bf16[69,8,384]{2,1,0:T(8,128)(2,1)S(1)} %dynamic-slice_bitcast_fusion), channel_id=1, source_target_pairs={{0,64},{64,0},{1,65},{65,1},{2,66},{66,2},{3,67},{67,3},{4,68},{68... | collective-permute-start | bytes 1271816 | tf_op jit(solution)/shard_map/ppermute | solution.py:553
  31.9 55.6 %copy-start = (f32[6,128]{1,0:T(8,128)S(1)}, f32[6,128]{1,0:T(8,128)}, u32[]{:S(2)}) copy-start(f32[6,128]{1,0:T(8,128)} %value_ref.1) | copy-start | bytes 9220
  31.9 55.6 %copy-start.1 = (f32[6,128]{1,0:T(8,128)S(1)}, f32[6,128]{1,0:T(8,128)}, u32[]{:S(2)}) copy-start(f32[6,128]{1,0:T(8,128)} %weight_ref.1) | copy-start | bytes 9220
  94.8 2.3 %collective-permute-start.1 = (f32[1,1]{1,0:T(1,128)}, f32[1,1]{1,0:T(1,128)}, u32[]{:S(2)}, u32[]{:S(2)}) collective-permute-start(f32[1,1]{1,0:T(1,128)} %get-tuple-element.16.total_ref), channel_id=1, source_target_pairs={{0,64},{64,0},{1,65},{65,1},{2,66},{66,2},{3,67},{67,3},{4,68},{68... | collective-permute-start | bytes 20 | tf_op jit(solution)/shard_map/ppermute | solution.py:560
